TPU v7x, 512 devices: a whole 4x4x16 slice. The times are simulated.
512 devices in a mesh: ctx: 32 (over x, z_lo), tp: 4 (over z_hi, core), dp: 4 (over y).
Axes of the slice: x: 4, y: 4, z: 16 (z_hi: 2, z_lo: 8; z = z_hi * 8 + z_lo), core: 2. Of those that a mesh axis runs over, the one named last changes fastest.
Arguments:
- queries: bfloat16 [32768, 4096], P(('dp', 'ctx'), 'tp'), parts along dimension 0, may hold values from -10 to 10
- keys: bfloat16 [32768, 512], P(('dp', 'ctx'), 'tp'), parts along dimension 0, may hold values from -4 to 4
- values: bfloat16 [32768, 512], P(('dp', 'ctx'), 'tp'), parts along dimension 0, may hold values from -5 to 5
- doc_ids: int32 [32768], P(('dp', 'ctx')), parts along dimension 0, may hold values from 0 to 127, never falling along the last dimension, each value on 1 to 4096 neighbouring positions
Outputs:
- attended: bfloat16 [32768, 4096], P(('dp', 'ctx'), 'tp'), parts along dimension 0
There are 4 independent parts, one for each index of `dp`. A program takes and returns all parts, laid end to end along the dimension named above; each array names one. Nothing has to cross between parts.
Inputs may be any that keep to these rules, and one draw needn't show every extreme that they name: `doc_ids`: document numbers never fall along the sequence, every number appears, and no document is longer than 4096 positions; one has exactly 4096.
All inputs are finite; a program needn't handle non-finite values.
Results may differ from a plain program's by a relative error of at most 0.003.
Values may be sent and summed in bfloat16 or wider, within the bound.
No kernel may reach another device: no remote copies, remote signals or barrier semaphores. Data moves between devices by JAX's collectives and lax.ppermute only.
A program may use at most 64 MiB of HBM per device.

v0:
```python
import math

import jax
import jax.numpy as jnp
from jax import lax
from jax.sharding import PartitionSpec as P

HEAD_SIZE = 128


NEGATIVE = -1e30


def attend_tile(state, grouped_queries, query_ids, query_pos, block, block_ids, block_pos):
    visible = (
        (query_ids[:, None] == block_ids[None, :])
        & (block_pos[None, :] <= query_pos[:, None])
        & True
    )
    scale = grouped_queries.shape[-1] ** (-0.5)

    def compute(current):
        running_max, running_sum, weighted = current
        rows = block.shape[1]
        groups = grouped_queries.shape[1]
        key_block = block[0].reshape(rows, groups, grouped_queries.shape[-1])
        value_block = block[1].reshape(rows, groups, grouped_queries.shape[-1])
        scores = (
            jnp.einsum(
                "qhgd,khd->qhgk", grouped_queries, key_block, preferred_element_type=jnp.float32
            )
            * scale
        )
        shown = visible[:, None, None, :]
        block_max = jnp.max(jnp.where(shown, scores, NEGATIVE), axis=-1)
        new_max = jnp.maximum(running_max, block_max)
        weights = jnp.where(shown, jnp.exp(scores - new_max[..., None]), 0.0)
        factor = jnp.exp(running_max - new_max)
        new_sum = running_sum * factor + jnp.sum(weights, axis=-1)
        update = jnp.einsum(
            "qhgk,khd->qhgd",
            weights.astype(jnp.bfloat16),
            value_block,
            preferred_element_type=jnp.float32,
        )
        return (new_max, new_sum, weighted * factor[..., None] + update)

    return lax.cond(jnp.any(visible), compute, lambda current: current, state)


def per_device(queries, keys, values, doc_ids):
    rows_here = queries.shape[0]
    kv_width = keys.shape[1]
    groups = kv_width // HEAD_SIZE
    queries_per_group = queries.shape[1] // kv_width
    grouped_queries = queries.reshape(rows_here, groups, queries_per_group, HEAD_SIZE)
    own_index = lax.axis_index("ctx")
    all_ids = lax.all_gather(doc_ids, "ctx", axis=0, tiled=True)
    query_pos = own_index * rows_here + jnp.arange(rows_here, dtype=jnp.int32)
    start_state = (
        jnp.full((rows_here, groups, queries_per_group), NEGATIVE, jnp.float32),
        jnp.zeros((rows_here, groups, queries_per_group), jnp.float32),
        jnp.zeros((rows_here, groups, queries_per_group, HEAD_SIZE), jnp.float32),
    )
    key_value = jnp.stack([keys, values])

    def visit(state, block, first):
        rows = block.shape[1]
        block_ids = lax.dynamic_slice_in_dim(all_ids, jnp.maximum(first, 0), rows, 0)
        block_pos = first + jnp.arange(rows, dtype=jnp.int32)
        return attend_tile(state, grouped_queries, doc_ids, query_pos, block, block_ids, block_pos)

    piece = lax.all_gather(key_value, "ctx", axis=1, tiled=True)
    total_rows = piece.shape[1]
    block_rows = math.gcd(total_rows, 512)
    count = total_rows // block_rows
    blocks = piece.reshape(2, count, block_rows, kv_width).transpose(1, 0, 2, 3)

    def scan_step(current, inputs):
        block, number = inputs
        return (visit(current, block, number * block_rows), None)

    final, unused = lax.scan(scan_step, start_state, (blocks, jnp.arange(count, dtype=jnp.int32)))
    state = final
    running_max, running_sum, weighted = state
    attended = weighted / running_sum[..., None]
    return attended.reshape(rows_here, queries_per_group * kv_width).astype(jnp.bfloat16)


def solution(mesh):
    return jax.shard_map(
        per_device,
        mesh=mesh,
        in_specs=(
            P(("dp", "ctx"), "tp"),
            P(("dp", "ctx"), "tp"),
            P(("dp", "ctx"), "tp"),
            P(("dp", "ctx")),
        ),
        out_specs=P(("dp", "ctx"), "tp"),
        check_vma=False,
    )
```

profile of v0, /device:TPU:254, one launch (start us, length us, event | category | flops | bytes accessed | tf_op | source)
XLA Modules:
  0.0 379.1 jit_solution(5018690073305397074)
XLA Ops:
  9.6 111.4 %all-gather = s32[32,1,256]{2,1,0:T(1,128)S(1)} all-gather(s32[1,1,256]{2,1,0:T(1,128)} %bitcast.82), channel_id=1, replica_groups=mesh['ctx'=32,'tp'=4,'dp'=4] {'ctx'}, dimensions={0}, use_global_device_ids=true | all-gather | bytes 33792 | tf_op jit(solution)/shard_map/all_gather | solution.py:58
  121.1 126.4 %all-gather.3.cloned.1.call-done = bf16[2,8192,128]{2,1,0:T(8,128)(2,1)} async-done(((bf16[2,256,128]{2,1,0:T(8,128)(2,1)}), bf16[2,8192,128]{2,1,0:T(8,128)(2,1)}) %all-gather.3.cloned.1.call-update) | async-done | bytes 4194320 | tf_op jit(solution)/shard_map/all_gather | solution.py:73
  247.5 4.6 %copy.17 = bf16[16,2,512,128]{3,2,1,0:T(8,128)(2,1)} copy(bf16[16,2,512,128]{3,2,0,1:T(8,128)(2,1)} %bitcast.75) | data formatting | bytes 8388608
  252.2 118.9 %while.15 = (s32[]{:T(128)}, f32[256,1,8]{0,2,1:T(8,128)S(1)}, f32[256,1,8]{0,2,1:T(8,128)S(1)}, f32[256,1,8,128]{0,3,2,1:T(8,128)S(1)}, s32[256]{0:T(256)S(1)},...) while((s32[]{:T(128)}, f32[256,1,8]{0,2,1:T(8,128)S(1)}, ...), condition=%wide.region_6.7_spmd.clone, body=%wide.region_0.6_spmd.clone.sunk | while | flops 549460736 | bytes 32913744 | solution.py:83
  275.1 8.1 %conditional.3 = ((f32[256,1,8]{0,2,1:T(8,128)S(1)}, f32[256,1,8]{0,2,1:T(8,128)S(1)}, f32[256,1,8,128]{0,3,2,1:T(8,128)S(1)})) conditional(s32[]{:T(128)} %convert_element_type.26, (f32[256,1,8]{0,2,1:T(8,128)S(1)}, f32[256,1,8]{0,2,1:T(8,128)S(1)}, f32[256,1,8,128]{0,3,2,1:T(8,128)S(1)}) %tuple.41, (pred[256,512]{0,1:T(8,128)(4,1)S(1)}, ...), branch_computations={%region_2.2_spmd, %region_3.5_spmd} | conditional | flops 548935680 | bytes 32769100 | solution.py:48
  275.1 3.7 fusion.2
  286.1 8.1 %conditional.3 = ((f32[256,1,8]{0,2,1:T(8,128)S(1)}, f32[256,1,8]{0,2,1:T(8,128)S(1)}, f32[256,1,8,128]{0,3,2,1:T(8,128)S(1)})) conditional(s32[]{:T(128)} %convert_element_type.26, (f32[256,1,8]{0,2,1:T(8,128)S(1)}, f32[256,1,8]{0,2,1:T(8,128)S(1)}, f32[256,1,8,128]{0,3,2,1:T(8,128)S(1)}) %tuple.41, (pred[256,512]{0,1:T(8,128)(4,1)S(1)}, ...), branch_computations={%region_2.2_spmd, %region_3.5_spmd} | conditional | flops 548935680 | bytes 32769100 | solution.py:48
  286.1 3.6 fusion.2
  289.7 3.6 fusion.14
  297.0 8.1 %conditional.3 = ((f32[256,1,8]{0,2,1:T(8,128)S(1)}, f32[256,1,8]{0,2,1:T(8,128)S(1)}, f32[256,1,8,128]{0,3,2,1:T(8,128)S(1)})) conditional(s32[]{:T(128)} %convert_element_type.26, (f32[256,1,8]{0,2,1:T(8,128)S(1)}, f32[256,1,8]{0,2,1:T(8,128)S(1)}, f32[256,1,8,128]{0,3,2,1:T(8,128)S(1)}) %tuple.41, (pred[256,512]{0,1:T(8,128)(4,1)S(1)}, ...), branch_computations={%region_2.2_spmd, %region_3.5_spmd} | conditional | flops 548935680 | bytes 32769100 | solution.py:48
  297.1 3.6 fusion.2
  300.7 3.6 fusion.14
  308.0 8.1 %conditional.3 = ((f32[256,1,8]{0,2,1:T(8,128)S(1)}, f32[256,1,8]{0,2,1:T(8,128)S(1)}, f32[256,1,8,128]{0,3,2,1:T(8,128)S(1)})) conditional(s32[]{:T(128)} %convert_element_type.26, (f32[256,1,8]{0,2,1:T(8,128)S(1)}, f32[256,1,8]{0,2,1:T(8,128)S(1)}, f32[256,1,8,128]{0,3,2,1:T(8,128)S(1)}) %tuple.41, (pred[256,512]{0,1:T(8,128)(4,1)S(1)}, ...), branch_computations={%region_2.2_spmd, %region_3.5_spmd} | conditional | flops 548935680 | bytes 32769100 | solution.py:48
  308.0 3.6 fusion.2
  319.0 8.1 %conditional.3 = ((f32[256,1,8]{0,2,1:T(8,128)S(1)}, f32[256,1,8]{0,2,1:T(8,128)S(1)}, f32[256,1,8,128]{0,3,2,1:T(8,128)S(1)})) conditional(s32[]{:T(128)} %convert_element_type.26, (f32[256,1,8]{0,2,1:T(8,128)S(1)}, f32[256,1,8]{0,2,1:T(8,128)S(1)}, f32[256,1,8,128]{0,3,2,1:T(8,128)S(1)}) %tuple.41, (pred[256,512]{0,1:T(8,128)(4,1)S(1)}, ...), branch_computations={%region_2.2_spmd, %region_3.5_spmd} | conditional | flops 548935680 | bytes 32769100 | solution.py:48
  319.0 3.6 fusion.2
  330.0 8.1 %conditional.3 = ((f32[256,1,8]{0,2,1:T(8,128)S(1)}, f32[256,1,8]{0,2,1:T(8,128)S(1)}, f32[256,1,8,128]{0,3,2,1:T(8,128)S(1)})) conditional(s32[]{:T(128)} %convert_element_type.26, (f32[256,1,8]{0,2,1:T(8,128)S(1)}, f32[256,1,8]{0,2,1:T(8,128)S(1)}, f32[256,1,8,128]{0,3,2,1:T(8,128)S(1)}) %tuple.41, (pred[256,512]{0,1:T(8,128)(4,1)S(1)}, ...), branch_computations={%region_2.2_spmd, %region_3.5_spmd} | conditional | flops 548935680 | bytes 32769100 | solution.py:48
  330.0 3.6 fusion.2
  341.0 8.1 %conditional.3 = ((f32[256,1,8]{0,2,1:T(8,128)S(1)}, f32[256,1,8]{0,2,1:T(8,128)S(1)}, f32[256,1,8,128]{0,3,2,1:T(8,128)S(1)})) conditional(s32[]{:T(128)} %convert_element_type.26, (f32[256,1,8]{0,2,1:T(8,128)S(1)}, f32[256,1,8]{0,2,1:T(8,128)S(1)}, f32[256,1,8,128]{0,3,2,1:T(8,128)S(1)}) %tuple.41, (pred[256,512]{0,1:T(8,128)(4,1)S(1)}, ...), branch_computations={%region_2.2_spmd, %region_3.5_spmd} | conditional | flops 548935680 | bytes 32769100 | solution.py:48
  341.0 3.6 fusion.2
  352.0 8.1 %conditional.3 = ((f32[256,1,8]{0,2,1:T(8,128)S(1)}, f32[256,1,8]{0,2,1:T(8,128)S(1)}, f32[256,1,8,128]{0,3,2,1:T(8,128)S(1)})) conditional(s32[]{:T(128)} %convert_element_type.26, (f32[256,1,8]{0,2,1:T(8,128)S(1)}, f32[256,1,8]{0,2,1:T(8,128)S(1)}, f32[256,1,8,128]{0,3,2,1:T(8,128)S(1)}) %tuple.41, (pred[256,512]{0,1:T(8,128)(4,1)S(1)}, ...), branch_computations={%region_2.2_spmd, %region_3.5_spmd} | conditional | flops 548935680 | bytes 32769100 | solution.py:48
  352.0 3.6 fusion.2
  363.0 8.1 %conditional.3 = ((f32[256,1,8]{0,2,1:T(8,128)S(1)}, f32[256,1,8]{0,2,1:T(8,128)S(1)}, f32[256,1,8,128]{0,3,2,1:T(8,128)S(1)})) conditional(s32[]{:T(128)} %convert_element_type.26, (f32[256,1,8]{0,2,1:T(8,128)S(1)}, f32[256,1,8]{0,2,1:T(8,128)S(1)}, f32[256,1,8,128]{0,3,2,1:T(8,128)S(1)}) %tuple.41, (pred[256,512]{0,1:T(8,128)(4,1)S(1)}, ...), branch_computations={%region_2.2_spmd, %region_3.5_spmd} | conditional | flops 548935680 | bytes 32769100 | solution.py:48
  363.0 3.6 fusion.2
  (161 shorter events, 61.5 us)
Async XLA Ops:
  6.5 241.0 %all-gather.3.cloned.1.call-start = ((), (), s32[]{:S(2)}) async-start(), calls=%async_computation | async-start | bytes 4325376 | tf_op jit(solution)/shard_map/all_gather | solution.py:73
  247.5 4.7 %copy-start.1 = (s32[256]{0:T(256)S(1)}, s32[256]{0:T(256)}, u32[]{:S(2)}) copy-start(s32[256]{0:T(256)} %param.11) | copy-start | bytes 3076
  278.7 3.6 copy-start
  289.7 3.6 copy-start
  300.7 3.6 copy-start
  311.7 3.6 copy-start
  322.7 3.6 copy-start
  333.7 3.6 copy-start
  344.7 3.6 copy-start
  355.7 3.6 copy-start
  366.7 3.6 copy-start
Sparse Core Ops, SparseCore 0:
  9.4 238.0 all-gather.2
where the time goes:
time: 380 us; the launch traced here: 379 us
  waiting for transfers between devices  126 us (33%)
  blocking collectives  111 us (29%)
  matrix products  64.9 us (17%)
  other arithmetic  23.1 us (6%)
  loops' own time  21.8 us (6%)
  local copies, waits for them, and re-layouts  17.9 us (5%)
  between operations  13.5 us (4%)
    all_gather x1, waiting for transfers between devices, per_device(): piece = lax.all_gather(key_value, 'ctx', axis=1, tiled=True)  126 us
    all_gather x1, blocking collectives, per_device(): all_ids = lax.all_gather(doc_ids, 'ctx', axis=0, tiled=True)  111 us
    dot_general x9, matrix products, compute(): jnp.einsum('qhgd,khd->qhgk', grouped_queries, key_block, preferred_elemen...  32.8 us
    dot_general x9, matrix products, compute(): jnp.einsum('qhgk,khd->qhgd', weights.astype(jnp.bfloat16), value_block, p...  32 us
    another operation x1, loops' own time, per_device(): lax.scan(scan_step, start_state, (blocks, jnp.arange(count, dtype=jnp.int...  21.3 us
    reduce_or x16, other arithmetic, attend_tile(): return lax.cond(jnp.any(visible), compute, lambda current: current, state)  13.4 us
    dynamic_slice x16, local copies, waits for them, and re-layouts, per_device(): lax.scan(scan_step, start_state, (blocks, jnp.arange(count, dtype=jnp.int...  9.39 us
    reduce_sum x9, other arithmetic, compute(): new_sum = running_sum * factor + jnp.sum(weights, axis=-1)  7.81 us
  transfers between devices with their start and end apart: 1, of which 1 were waited for; matrix products, arithmetic and copies ran while one was open for 0% of the time, Pallas kernels for 0%

commit v1 on v0

v1 whole, which is shorter than its diff:
```python
import functools
import math

import jax
import jax.numpy as jnp
from jax import lax
from jax.experimental import pallas as pl
from jax.experimental.pallas import tpu as pltpu
from jax.sharding import PartitionSpec as P

HEAD = 128
BLOCK = 256
HEADS = 8
IDS = 16
SLOT = 2 * BLOCK + IDS
NEGATIVE = -1e30
FACTOR = HEAD**-0.5 * math.log2(math.e)
NX, NZ = 4, 8


def contract_last(a, b):
    return lax.dot_general(a, b, (((1,), (1,)), ((), ())), preferred_element_type=jnp.float32)


def own_kernel(q_ref, own_ref, m_ref, l_ref, acc_ref):
    ids = own_ref[2 * BLOCK :, :].astype(jnp.float32)
    row = jnp.concatenate([ids[0:1, :], ids[1:2, :]], axis=1)
    key_ids = jnp.broadcast_to(row, (BLOCK, BLOCK))
    query_ids = key_ids.T
    q_pos = lax.broadcasted_iota(jnp.int32, (BLOCK, BLOCK), 0)
    k_pos = lax.broadcasted_iota(jnp.int32, (BLOCK, BLOCK), 1)
    visible = (key_ids == query_ids) & (k_pos <= q_pos)
    in_first = (query_ids == key_ids[0:1, 0:1])[:, :HEAD]
    keys = own_ref[:BLOCK, :]
    values = own_ref[BLOCK : 2 * BLOCK, :]
    for h in range(HEADS):
        rows = pl.ds(h * BLOCK, BLOCK)
        scores = contract_last(q_ref[:, h * HEAD : (h + 1) * HEAD], keys) * FACTOR
        scores = jnp.where(visible, scores, NEGATIVE)
        top = jnp.max(scores, axis=1, keepdims=True)
        weights = jnp.exp2(scores - top)
        l_ref[rows, :] = weights[:, :HEAD] + weights[:, HEAD:]
        acc_ref[rows, :] = jnp.dot(
            weights.astype(jnp.bfloat16), values, preferred_element_type=jnp.float32
        )
        m_ref[rows, :] = jnp.where(in_first, jnp.broadcast_to(top, (BLOCK, HEAD)), -NEGATIVE)


def more_kernel(counts, last, *refs):
    n = len(counts)
    ok_ref, q_ref, own_ref, m_in, l_in, acc_in = refs[:6]
    slots = refs[6 : 6 + n]
    if last:
        out_ref, m_ref, l_ref, acc_ref = refs[6 + n :]
    else:
        m_ref, l_ref, acc_ref = refs[6 + n :]
    m_ref[...] = m_in[...]
    l_ref[...] = l_in[...]
    acc_ref[...] = acc_in[...]
    first_id = own_ref[2 * BLOCK :, :].astype(jnp.float32)[0:1, 0:1]
    at = 0
    for ref, count in zip(slots, counts):
        for k in range(count):
            base = k * SLOT
            ids = ref[base + 2 * BLOCK : base + SLOT, :].astype(jnp.float32)
            seen = jnp.sum(jnp.where(ids == first_id, 1.0, 0.0)).astype(jnp.int32)
            seen = seen * ok_ref[at]
            at += 1

            @pl.when(seen > 0)
            def _():
                k_pos = lax.broadcasted_iota(jnp.int32, (1, BLOCK), 1)
                bias = jnp.where(k_pos >= BLOCK - seen, 0.0, NEGATIVE)
                keys = ref[base : base + BLOCK, :]
                values = ref[base + BLOCK : base + 2 * BLOCK, :]

                def head(h, carry):
                    rows = pl.ds(pl.multiple_of(h * BLOCK, BLOCK), BLOCK)
                    q = q_ref[:, pl.ds(pl.multiple_of(h * HEAD, HEAD), HEAD)]
                    scores = contract_last(q, keys) * FACTOR + bias
                    old = m_ref[rows, :]
                    new = jnp.maximum(old, jnp.max(scores, axis=1, keepdims=True))
                    fade = jnp.exp2(old - new)
                    weights = jnp.exp2(scores - new[:, 0:1])
                    l_ref[rows, :] = l_ref[rows, :] * fade + weights[:, :HEAD] + weights[:, HEAD:]
                    acc_ref[rows, :] = acc_ref[rows, :] * fade + jnp.dot(
                        weights.astype(jnp.bfloat16), values, preferred_element_type=jnp.float32
                    )
                    m_ref[rows, :] = new
                    return carry

                lax.fori_loop(0, HEADS, head, 0, unroll=4)

    if last:
        for h in range(HEADS):
            rows = pl.ds(h * BLOCK, BLOCK)
            total = jnp.sum(l_ref[rows, :], axis=1, keepdims=True)
            out_ref[:, h * HEAD : (h + 1) * HEAD] = (acc_ref[rows, :] / total).astype(jnp.bfloat16)


VMEM = pl.BlockSpec(memory_space=pltpu.VMEM)
SMEM = pl.BlockSpec(memory_space=pltpu.SMEM)
STATE = [jax.ShapeDtypeStruct((HEADS * BLOCK, HEAD), jnp.float32)] * 3
PARAMS = pltpu.CompilerParams(vmem_limit_bytes=40 * 1024 * 1024)


def cost(blocks):
    pairs = blocks * HEADS * BLOCK * BLOCK
    return pl.CostEstimate(
        flops=4 * HEAD * pairs, bytes_accessed=4 * 2**20, transcendentals=pairs
    )


def attend_own(q, own):
    return pl.pallas_call(
        own_kernel, out_shape=STATE, in_specs=[VMEM] * 2, out_specs=[VMEM] * 3,
        compiler_params=PARAMS, cost_estimate=cost(1), name="attend_own",
    )(q, own)


def attend_more(state, q, own, arrays, ok, last=False):
    counts = [a.shape[0] // SLOT for a in arrays]
    ok = jnp.stack([jnp.asarray(o, jnp.int32) for o in ok])
    scratch = [pltpu.VMEM((HEADS * BLOCK, HEAD), jnp.float32)] * 3 if last else []
    out = jax.ShapeDtypeStruct((BLOCK, HEADS * HEAD), jnp.bfloat16)
    return pl.pallas_call(
        functools.partial(more_kernel, counts, last),
        out_shape=out if last else STATE,
        in_specs=[SMEM] + [VMEM] * (5 + len(arrays)),
        out_specs=VMEM if last else [VMEM] * 3,
        scratch_shapes=scratch,
        compiler_params=PARAMS, cost_estimate=cost(sum(counts)),
        name="attend_last" if last else "attend_more",
    )(ok, q, own, *state, *arrays)


def exchange(v, mask):
    return lax.ppermute(v, "ctx", [(i, i ^ mask) for i in range(NX * NZ)])


def along_x(v, steps):
    return lax.ppermute(v, "ctx", [(i, i + NZ * steps) for i in range((NX - steps) * NZ)])


def per_device(queries, keys, values, doc_ids):
    index = lax.axis_index("ctx")
    z = index % NZ
    bit = [(z >> b) & 1 for b in range(3)]
    one = jnp.int32(1)
    ids = (doc_ids + 1).astype(jnp.bfloat16).reshape(2, HEAD)
    ids = jnp.pad(ids, ((0, IDS - 2), (0, 0)))
    own = jnp.concatenate([keys, values, ids], axis=0)

    def hold(*values):
        return lax.optimization_barrier(values)

    p1 = exchange(own, 4)
    b0 = along_x(own, 1)
    c0 = along_x(own, 2)
    state = attend_own(queries, own)
    p1, b0, c0, state = hold(p1, b0, c0, state)
    p2 = exchange(jnp.concatenate([own, p1]), 2)
    near0 = exchange(jnp.concatenate([b0, jnp.where(bit[0] == 0, own, c0)]), 1)
    b1 = along_x(p1, 1)
    c1 = along_x(p1, 2)
    state = attend_more(state, queries, own, [p1, b0, c0], [bit[2], one, one])
    p2, near0, b1, c1, state = hold(p2, near0, b1, c1, state)
    near1 = exchange(jnp.concatenate([b1, jnp.where(bit[2] == 1, p1, c1), p2]), 1)
    b2 = along_x(p2, 1)
    c2 = along_x(p2, 2)
    state = attend_more(
        state, queries, own, [p2, near0, b1, c1], [bit[1], bit[2], one, one, one, one]
    )
    near1, b2, c2, state = hold(near1, b2, c2, state)
    c3 = exchange(c2, 1)
    b3 = along_x(near1[2 * SLOT :], 1)
    state = attend_more(
        state, queries, own, [near1, b2, c2], [one, one, bit[1], bit[2], one, one, one, one]
    )
    c3, b3, state = hold(c3, b3, state)
    return attend_more(state, queries, own, [c3, b3], [one] * 4, last=True)


def solution(mesh):
    return jax.shard_map(
        per_device,
        mesh=mesh,
        in_specs=(
            P(("dp", "ctx"), "tp"),
            P(("dp", "ctx"), "tp"),
            P(("dp", "ctx"), "tp"),
            P(("dp", "ctx")),
        ),
        out_specs=P(("dp", "ctx"), "tp"),
        check_vma=False,
    )
```

time: 380 us -> 102 us (0.27)
  the two profiles are of different devices: /device:TPU:254 before, /device:TPU:148 now
where the time goes in v1:
time: 102 us; the launch traced here: 101 us
  Pallas kernels  46.2 us (45%)
  starting transfers between devices  33.5 us (33%)
  waiting for transfers between devices  9.27 us (9%)
  local copies, waits for them, and re-layouts  6.75 us (7%)
  other arithmetic  5.44 us (5%)
    pallas_call x4, Pallas kernels, attend_more(): pl.pallas_call(functools.partial(more_kernel, counts, last), out_shape=ou...  45 us
    ppermute x5, starting transfers between devices, exchange(): return lax.ppermute(v, 'ctx', [(i, i ^ mask) for i in range(NX * NZ)])  20.8 us
    ppermute x7, starting transfers between devices, along_x(): lax.ppermute(v, 'ctx', [(i, i + NZ * steps) for i in range((NX - steps) *...  12.7 us
    unnamed x26, local copies, waits for them, and re-layouts  6.71 us
    ppermute x5, waiting for transfers between devices, exchange(): return lax.ppermute(v, 'ctx', [(i, i ^ mask) for i in range(NX * NZ)])  6.24 us
    ppermute x7, waiting for transfers between devices, along_x(): lax.ppermute(v, 'ctx', [(i, i + NZ * steps) for i in range((NX - steps) *...  3.02 us
    concatenate x1, other arithmetic, per_device(): jnp.concatenate([b1, jnp.where(bit[2] == 1, p1, c1), p2])  2.16 us
  transfers between devices with their start and end apart: 12, of which 3 were waited for; matrix products, arithmetic and copies ran while one was open for 1% of the time, Pallas kernels for 36%

profile of v1, /device:TPU:148, one launch (start us, length us, event | category | flops | bytes accessed | tf_op | source)
XLA Modules:
  0.0 101.5 jit_solution(17126640370771119692)
XLA Ops:
  1.6 1.3 %collective-permute-start.2 = (bf16[528,128]{1,0:T(8,128)(2,1)S(1)}, bf16[528,128]{1,0:T(8,128)(2,1)S(1)}, u32[]{:S(2)}, u32[]{:S(2)}) collective-permute-start(bf16[528,128]{1,0:T(8,128)(2,1)S(1)} %pad_maximum_fusion.3.own_ref.refs_2_), channel_id=1, source_target_pairs={{0,256},{16,272},{32,288},{48,304},{64,320},{80,336},{96,352},{112... | collective-permute-start | bytes 405512 | tf_op jit(solution)/shard_map/ppermute | solution.py:142
  2.9 3.1 %collective-permute-start.1 = (bf16[528,128]{1,0:T(8,128)(2,1)S(1)}, bf16[528,128]{1,0:T(8,128)(2,1)S(1)}, u32[]{:S(2)}, u32[]{:S(2)}) collective-permute-start(bf16[528,128]{1,0:T(8,128)(2,1)S(1)} %pad_maximum_fusion.3.own_ref.refs_2_), channel_id=1, source_target_pairs={{0,128},{16,144},{32,160},{48,176},{64,192},{80,208},{96,224},{112... | collective-permute-start | bytes 405512 | tf_op jit(solution)/shard_map/ppermute | solution.py:142
  6.0 1.9 %collective-permute-start = (bf16[528,128]{1,0:T(8,128)(2,1)S(1)}, bf16[528,128]{1,0:T(8,128)(2,1)S(1)}, u32[]{:S(2)}, u32[]{:S(2)}) collective-permute-start(bf16[528,128]{1,0:T(8,128)(2,1)S(1)} %pad_maximum_fusion.3.own_ref.refs_2_), channel_id=1, source_target_pairs={{0,64},{16,80},{32,96},{48,112},{64,0},{80,16},{96,32},{112,48},{1... | collective-permute-start | bytes 405512 | tf_op jit(solution)/shard_map/ppermute | solution.py:138
  8.0 1.0 %copy-done = bf16[256,1024]{1,0:T(8,128)(2,1)S(1)} copy-done((bf16[256,1024]{1,0:T(8,128)(2,1)S(1)}, bf16[256,1024]{1,0:T(8,128)(2,1)}, u32[]{:S(2)}) %copy-start) | copy-done | bytes 524312
  9.0 1.2 %attend_own.1 = (f32[2048,128]{1,0:T(8,128)S(1)}, f32[2048,128]{1,0:T(8,128)S(1)}, f32[2048,128]{1,0:T(8,128)S(1)}) custom-call(bf16[256,1024]{1,0:T(8,128)(2,1)S(1)} %copy-done, bf16[528,128]{1,0:T(8,128)(2,1)S(1)} %pad_maximum_fusion.3.own_ref.refs_2_), custom_call_target="tpu_custom_call" | custom-call | flops 268435456 | bytes 4194304 | tf_op jit(solution)/shard_map/attend_own/pallas_call | solution.py:115
  11.0 2.2 %collective-permute-done.1.refs_7_ = bf16[528,128]{1,0:T(8,128)(2,1)S(1)} collective-permute-done((bf16[528,128]{1,0:T(8,128)(2,1)S(1)}, bf16[528,128]{1,0:T(8,128)(2,1)S(1)}, u32[]{:S(2)}, u32[]{:S(2)}) %collective-permute-start.1) | collective-permute-done | bytes 135200 | tf_op jit(solution)/shard_map/ppermute | solution.py:142
  13.2 6.2 %collective-permute-done.refs_6_ = bf16[528,128]{1,0:T(8,128)(2,1)S(1)} collective-permute-done((bf16[528,128]{1,0:T(8,128)(2,1)S(1)}, bf16[528,128]{1,0:T(8,128)(2,1)S(1)}, u32[]{:S(2)}, u32[]{:S(2)}) %collective-permute-start) | collective-permute-done | bytes 135200 | tf_op jit(solution)/shard_map/ppermute | solution.py:138
  20.2 7.6 %collective-permute-start.3 = (bf16[1056,128]{1,0:T(8,128)(2,1)}, bf16[1056,128]{1,0:T(8,128)(2,1)S(1)}, u32[]{:S(2)}, u32[]{:S(2)}) collective-permute-start(bf16[1056,128]{1,0:T(8,128)(2,1)} %pad_maximum_fusion.1), channel_id=1, source_target_pairs={{0,32},{16,48},{32,0},{48,16},{64,96},{80,112},{96,64},{112,80},{1... | collective-permute-start | bytes 811016 | tf_op jit(solution)/shard_map/ppermute | solution.py:138
  28.6 6.2 %collective-permute-start.4 = (bf16[1056,128]{1,0:T(8,128)(2,1)}, bf16[1056,128]{1,0:T(8,128)(2,1)}, u32[]{:S(2)}, u32[]{:S(2)}) collective-permute-start(bf16[1056,128]{1,0:T(8,128)(2,1)} %pad_maximum_fusion.2), channel_id=1, source_target_pairs={{0,16},{16,0},{32,48},{48,32},{64,80},{80,64},{96,112},{112,96},{1... | collective-permute-start | bytes 811016 | tf_op jit(solution)/shard_map/ppermute | solution.py:138
  34.7 1.3 %collective-permute-start.6 = (bf16[528,128]{1,0:T(8,128)(2,1)S(1)}, bf16[528,128]{1,0:T(8,128)(2,1)}, u32[]{:S(2)}, u32[]{:S(2)}) collective-permute-start(bf16[528,128]{1,0:T(8,128)(2,1)S(1)} %collective-permute-done.refs_6_), channel_id=1, source_target_pairs={{0,256},{16,272},{32,288},{48,304},{64,320},{80,336},{96,352},{112... | collective-permute-start | bytes 405512 | tf_op jit(solution)/shard_map/ppermute | solution.py:142
  36.0 1.9 %collective-permute-start.5 = (bf16[528,128]{1,0:T(8,128)(2,1)S(1)}, bf16[528,128]{1,0:T(8,128)(2,1)}, u32[]{:S(2)}, u32[]{:S(2)}) collective-permute-start(bf16[528,128]{1,0:T(8,128)(2,1)S(1)} %collective-permute-done.refs_6_), channel_id=1, source_target_pairs={{0,128},{16,144},{32,160},{48,176},{64,192},{80,208},{96,224},{112... | collective-permute-start | bytes 405512 | tf_op jit(solution)/shard_map/ppermute | solution.py:142
  38.0 1.2 %copy-done.3 = f32[2048,128]{1,0:T(8,128)S(1)} copy-done((f32[2048,128]{1,0:T(8,128)S(1)}, f32[2048,128]{1,0:T(8,128)}, u32[]{:S(2)}) %copy-start.3) | copy-done | bytes 1048600
  39.2 8.2 %attend_more.3 = (f32[2048,128]{1,0:T(8,128)S(1)}, f32[2048,128]{1,0:T(8,128)S(1)}, f32[2048,128]{1,0:T(8,128)S(1)}) custom-call(s32[3]{0:T(128)S(1)} %stack.19.refs_0_, bf16[256,1024]{1,0:T(8,128)(2,1)S(1)} %copy-done.1, bf16[528,128]{1,0:T(8,128)(2,1)S(1)} %pad_maximum_fusion.3.own_ref.refs_2_, f32[2048,128]{1,0:T(8,128)S(1)} %get-tuple-element.47.refs_3_, ...), custom_call_target="tpu_custom_call" | custom-call | flops 805306368 | bytes 4194304 | tf_op jit(solution)/shard_map/attend_more/pallas_call | solution.py:126
  49.5 2.2 %pad_maximum_fusion = bf16[2112,128]{1,0:T(8,128)(2,1)} fusion(bf16[1056,128]{1,0:T(8,128)(2,1)S(1)} %collective-permute-done.3.refs_6_, bf16[528,128]{1,0:T(8,128)(2,1)S(1)} %broadcast_select_fusion, bf16[528,128]{1,0:T(8,128)(2,1)} %collective-permute-done.5.refs_8_), kind=kLoop, calls=%fused_computation | loop fusion | flops 1622016 | bytes 1081344 | tf_op jit(solution)/shard_map/concatenate | solution.py:168
  51.6 1.9 %collective-permute-start.7 = (bf16[2112,128]{1,0:T(8,128)(2,1)}, bf16[2112,128]{1,0:T(8,128)(2,1)S(1)}, u32[]{:S(2)}, u32[]{:S(2)}) collective-permute-start(bf16[2112,128]{1,0:T(8,128)(2,1)} %pad_maximum_fusion), channel_id=1, source_target_pairs={{0,16},{16,0},{32,48},{48,32},{64,80},{80,64},{96,112},{112,96},{1... | collective-permute-start | bytes 1622024 | tf_op jit(solution)/shard_map/ppermute | solution.py:138
  53.6 1.3 %collective-permute-start.9 = (bf16[1056,128]{1,0:T(8,128)(2,1)S(1)}, bf16[1056,128]{1,0:T(8,128)(2,1)S(1)}, u32[]{:S(2)}, u32[]{:S(2)}) collective-permute-start(bf16[1056,128]{1,0:T(8,128)(2,1)S(1)} %collective-permute-done.3.refs_6_), channel_id=1, source_target_pairs={{0,256},{16,272},{32,288},{48,304},{64,320},{80,336},{96,352},{112... | collective-permute-start | bytes 811016 | tf_op jit(solution)/shard_map/ppermute | solution.py:142
  54.9 1.9 %collective-permute-start.8 = (bf16[1056,128]{1,0:T(8,128)(2,1)S(1)}, bf16[1056,128]{1,0:T(8,128)(2,1)S(1)}, u32[]{:S(2)}, u32[]{:S(2)}) collective-permute-start(bf16[1056,128]{1,0:T(8,128)(2,1)S(1)} %collective-permute-done.3.refs_6_), channel_id=1, source_target_pairs={{0,128},{16,144},{32,160},{48,176},{64,192},{80,208},{96,224},{112... | collective-permute-start | bytes 811016 | tf_op jit(solution)/shard_map/ppermute | solution.py:142
  56.9 1.2 %copy-done.5 = f32[2048,128]{1,0:T(8,128)S(1)} copy-done((f32[2048,128]{1,0:T(8,128)S(1)}, f32[2048,128]{1,0:T(8,128)}, u32[]{:S(2)}) %copy-start.5) | copy-done | bytes 1048600
  58.1 1.2 %copy-done.9 = f32[2048,128]{1,0:T(8,128)S(1)} copy-done((f32[2048,128]{1,0:T(8,128)S(1)}, f32[2048,128]{1,0:T(8,128)}, u32[]{:S(2)}) %copy-start.9) | copy-done | bytes 1048600
  59.3 11.4 %attend_more.4 = (f32[2048,128]{1,0:T(8,128)S(1)}, f32[2048,128]{1,0:T(8,128)S(1)}, f32[2048,128]{1,0:T(8,128)S(1)}) custom-call(s32[6]{0:T(128)S(1)} %pad_add_fusion.refs_0_, bf16[256,1024]{1,0:T(8,128)(2,1)S(1)} %copy-done.1, bf16[528,128]{1,0:T(8,128)(2,1)S(1)} %pad_maximum_fusion.3.own_ref.refs_2_, f32[2048,128]{1,0:T(8,128)S(1)} %copy-done.5, ...), custom_call_target="tpu_custom_call" | custom-call | flops 1610612736 | bytes 4194304 | tf_op jit(solution)/shard_map/attend_more/pallas_call | solution.py:126
  70.8 1.9 %collective-permute-start.11 = (bf16[1056,128]{1,0:T(8,128)(2,1)S(1)}, bf16[1056,128]{1,0:T(8,128)(2,1)S(1)}, u32[]{:S(2)}, u32[]{:S(2)}) collective-permute-start(bf16[1056,128]{1,0:T(8,128)(2,1)S(1)} %slice.3), channel_id=1, source_target_pairs={{0,128},{16,144},{32,160},{48,176},{64,192},{80,208},{96,224},{112... | collective-permute-start | bytes 811016 | tf_op jit(solution)/shard_map/ppermute | solution.py:142
  72.7 3.2 %collective-permute-start.10 = (bf16[1056,128]{1,0:T(8,128)(2,1)S(1)}, bf16[1056,128]{1,0:T(8,128)(2,1)S(1)}, u32[]{:S(2)}, u32[]{:S(2)}) collective-permute-start(bf16[1056,128]{1,0:T(8,128)(2,1)S(1)} %collective-permute-done.9.refs_8_), channel_id=1, source_target_pairs={{0,16},{16,0},{32,48},{48,32},{64,80},{80,64},{96,112},{112,96},{1... | collective-permute-start | bytes 811016 | tf_op jit(solution)/shard_map/ppermute | solution.py:138
  76.1 16.0 %attend_more.5 = (f32[2048,128]{1,0:T(8,128)S(1)}, f32[2048,128]{1,0:T(8,128)S(1)}, f32[2048,128]{1,0:T(8,128)S(1)}) custom-call(s32[8]{0:T(128)S(1)} %pad_add_fusion.1.refs_0_, bf16[256,1024]{1,0:T(8,128)(2,1)S(1)} %copy-done.1, bf16[528,128]{1,0:T(8,128)(2,1)S(1)} %pad_maximum_fusion.3.own_ref.refs_2_, f32[2048,128]{1,0:T(8,128)S(1)} %get-tuple-element.65.refs_3_, ...), custom_call_target="tpu_custom_call" | custom-call | flops 2147483648 | bytes 4194304 | tf_op jit(solution)/shard_map/attend_more/pallas_call | solution.py:126
  92.1 9.4 %attend_last.1 = bf16[256,1024]{1,0:T(8,128)(2,1)} custom-call(s32[4]{0:T(128)S(1)} %broadcast_2_refs_0_.2.refs_0_, bf16[256,1024]{1,0:T(8,128)(2,1)S(1)} %copy-done.1, bf16[528,128]{1,0:T(8,128)(2,1)S(1)} %pad_maximum_fusion.3.own_ref.refs_2_, f32[2048,128]{1,0:T(8,128)S(1)} %get-tuple-element.72.refs_3_, f32[2048,128]{1,0:T(8,128)S(1)} %get-tuple-element.73.refs_4_, ...), custom_call_target="tpu_custom_call" | custom-call | flops 1073741824 | bytes 4194304 | tf_op jit(solution)/shard_map/attend_last/pallas_call | solution.py:126
  (45 shorter events, 6.1 us)
Async XLA Ops:
  0.0 19.5 %copy-start.10 = (bf16[256,128]{1,0:T(8,128)(2,1)S(1)}, bf16[256,128]{1,0:T(8,128)(2,1)}, u32[]{:S(2)}) copy-start(bf16[256,128]{1,0:T(8,128)(2,1)} %param.6) | copy-start | bytes 196612
  0.0 19.5 %copy-start.11 = (bf16[256,128]{1,0:T(8,128)(2,1)S(1)}, bf16[256,128]{1,0:T(8,128)(2,1)}, u32[]{:S(2)}) copy-start(bf16[256,128]{1,0:T(8,128)(2,1)} %param.5) | copy-start | bytes 196612
  1.6 9.4 %collective-permute-start.2 = (bf16[528,128]{1,0:T(8,128)(2,1)S(1)}, bf16[528,128]{1,0:T(8,128)(2,1)S(1)}, u32[]{:S(2)}, u32[]{:S(2)}) collective-permute-start(bf16[528,128]{1,0:T(8,128)(2,1)S(1)} %pad_maximum_fusion.3.own_ref.refs_2_), channel_id=1, source_target_pairs={{0,256},{16,272},{32,288},{48,304},{64,320},{80,336},{96,352},{112... | collective-permute-start | bytes 405512 | tf_op jit(solution)/shard_map/ppermute | solution.py:142
  2.9 10.3 %collective-permute-start.1 = (bf16[528,128]{1,0:T(8,128)(2,1)S(1)}, bf16[528,128]{1,0:T(8,128)(2,1)S(1)}, u32[]{:S(2)}, u32[]{:S(2)}) collective-permute-start(bf16[528,128]{1,0:T(8,128)(2,1)S(1)} %pad_maximum_fusion.3.own_ref.refs_2_), channel_id=1, source_target_pairs={{0,128},{16,144},{32,160},{48,176},{64,192},{80,208},{96,224},{112... | collective-permute-start | bytes 405512 | tf_op jit(solution)/shard_map/ppermute | solution.py:142
  6.0 13.4 %collective-permute-start = (bf16[528,128]{1,0:T(8,128)(2,1)S(1)}, bf16[528,128]{1,0:T(8,128)(2,1)S(1)}, u32[]{:S(2)}, u32[]{:S(2)}) collective-permute-start(bf16[528,128]{1,0:T(8,128)(2,1)S(1)} %pad_maximum_fusion.3.own_ref.refs_2_), channel_id=1, source_target_pairs={{0,64},{16,80},{32,96},{48,112},{64,0},{80,16},{96,32},{112,48},{1... | collective-permute-start | bytes 405512 | tf_op jit(solution)/shard_map/ppermute | solution.py:138
  8.0 1.0 %copy-start = (bf16[256,1024]{1,0:T(8,128)(2,1)S(1)}, bf16[256,1024]{1,0:T(8,128)(2,1)}, u32[]{:S(2)}) copy-start(bf16[256,1024]{1,0:T(8,128)(2,1)} %refs_1_.7) | copy-start | bytes 1572868
  9.0 18.7 %copy-start.12 = (bf16[256,128]{1,0:T(8,128)(2,1)S(1)}, bf16[256,128]{1,0:T(8,128)(2,1)}, u32[]{:S(2)}) copy-start(bf16[256,128]{1,0:T(8,128)(2,1)} %param.5) | copy-start | bytes 196612
  9.0 29.0 %copy-start.1 = (bf16[256,1024]{1,0:T(8,128)(2,1)S(1)}, bf16[256,1024]{1,0:T(8,128)(2,1)}, u32[]{:S(2)}) copy-start(bf16[256,1024]{1,0:T(8,128)(2,1)} %refs_1_.7) | copy-start | bytes 1572868
  10.2 24.5 %copy-start.2 = (f32[2048,128]{1,0:T(8,128)}, f32[2048,128]{1,0:T(8,128)S(1)}, u32[]{:S(2)}) copy-start(f32[2048,128]{1,0:T(8,128)S(1)} %get-tuple-element.49.refs_5_) | copy-start | bytes 3145732
  20.2 29.2 %collective-permute-start.3 = (bf16[1056,128]{1,0:T(8,128)(2,1)}, bf16[1056,128]{1,0:T(8,128)(2,1)S(1)}, u32[]{:S(2)}, u32[]{:S(2)}) collective-permute-start(bf16[1056,128]{1,0:T(8,128)(2,1)} %pad_maximum_fusion.1), channel_id=1, source_target_pairs={{0,32},{16,48},{32,0},{48,16},{64,96},{80,112},{96,64},{112,80},{1... | collective-permute-start | bytes 811016 | tf_op jit(solution)/shard_map/ppermute | solution.py:138
  28.6 20.9 %collective-permute-start.4 = (bf16[1056,128]{1,0:T(8,128)(2,1)}, bf16[1056,128]{1,0:T(8,128)(2,1)}, u32[]{:S(2)}, u32[]{:S(2)}) collective-permute-start(bf16[1056,128]{1,0:T(8,128)(2,1)} %pad_maximum_fusion.2), channel_id=1, source_target_pairs={{0,16},{16,0},{32,48},{48,32},{64,80},{80,64},{96,112},{112,96},{1... | collective-permute-start | bytes 811016 | tf_op jit(solution)/shard_map/ppermute | solution.py:138
  34.7 14.7 %collective-permute-start.6 = (bf16[528,128]{1,0:T(8,128)(2,1)S(1)}, bf16[528,128]{1,0:T(8,128)(2,1)}, u32[]{:S(2)}, u32[]{:S(2)}) collective-permute-start(bf16[528,128]{1,0:T(8,128)(2,1)S(1)} %collective-permute-done.refs_6_), channel_id=1, source_target_pairs={{0,256},{16,272},{32,288},{48,304},{64,320},{80,336},{96,352},{112... | collective-permute-start | bytes 405512 | tf_op jit(solution)/shard_map/ppermute | solution.py:142
  36.0 13.4 %collective-permute-start.5 = (bf16[528,128]{1,0:T(8,128)(2,1)S(1)}, bf16[528,128]{1,0:T(8,128)(2,1)}, u32[]{:S(2)}, u32[]{:S(2)}) collective-permute-start(bf16[528,128]{1,0:T(8,128)(2,1)S(1)} %collective-permute-done.refs_6_), channel_id=1, source_target_pairs={{0,128},{16,144},{32,160},{48,176},{64,192},{80,208},{96,224},{112... | collective-permute-start | bytes 405512 | tf_op jit(solution)/shard_map/ppermute | solution.py:142
  38.0 1.2 %copy-start.3 = (f32[2048,128]{1,0:T(8,128)S(1)}, f32[2048,128]{1,0:T(8,128)}, u32[]{:S(2)}) copy-start(f32[2048,128]{1,0:T(8,128)} %copy-done.2) | copy-start | bytes 3145732
  48.4 1.0 copy-start.8
  49.4 4.2 %copy-start.4 = (f32[2048,128]{1,0:T(8,128)}, f32[2048,128]{1,0:T(8,128)S(1)}, u32[]{:S(2)}) copy-start(f32[2048,128]{1,0:T(8,128)S(1)} %get-tuple-element.56.refs_3_) | copy-start | bytes 3145732
  49.4 7.5 %copy-start.7 = (f32[2048,128]{1,0:T(8,128)S(1)}, f32[2048,128]{1,0:T(8,128)}, u32[]{:S(2)}) copy-start(f32[2048,128]{1,0:T(8,128)} %copy-done.6) | copy-start | bytes 3145732
  51.6 19.2 %collective-permute-start.7 = (bf16[2112,128]{1,0:T(8,128)(2,1)}, bf16[2112,128]{1,0:T(8,128)(2,1)S(1)}, u32[]{:S(2)}, u32[]{:S(2)}) collective-permute-start(bf16[2112,128]{1,0:T(8,128)(2,1)} %pad_maximum_fusion), channel_id=1, source_target_pairs={{0,16},{16,0},{32,48},{48,32},{64,80},{80,64},{96,112},{112,96},{1... | collective-permute-start | bytes 1622024 | tf_op jit(solution)/shard_map/ppermute | solution.py:138
  53.6 17.2 %collective-permute-start.9 = (bf16[1056,128]{1,0:T(8,128)(2,1)S(1)}, bf16[1056,128]{1,0:T(8,128)(2,1)S(1)}, u32[]{:S(2)}, u32[]{:S(2)}) collective-permute-start(bf16[1056,128]{1,0:T(8,128)(2,1)S(1)} %collective-permute-done.3.refs_6_), channel_id=1, source_target_pairs={{0,256},{16,272},{32,288},{48,304},{64,320},{80,336},{96,352},{112... | collective-permute-start | bytes 811016 | tf_op jit(solution)/shard_map/ppermute | solution.py:142
  54.9 15.9 %collective-permute-start.8 = (bf16[1056,128]{1,0:T(8,128)(2,1)S(1)}, bf16[1056,128]{1,0:T(8,128)(2,1)S(1)}, u32[]{:S(2)}, u32[]{:S(2)}) collective-permute-start(bf16[1056,128]{1,0:T(8,128)(2,1)S(1)} %collective-permute-done.3.refs_6_), channel_id=1, source_target_pairs={{0,128},{16,144},{32,160},{48,176},{64,192},{80,208},{96,224},{112... | collective-permute-start | bytes 811016 | tf_op jit(solution)/shard_map/ppermute | solution.py:142
  56.9 1.2 %copy-start.5 = (f32[2048,128]{1,0:T(8,128)S(1)}, f32[2048,128]{1,0:T(8,128)}, u32[]{:S(2)}) copy-start(f32[2048,128]{1,0:T(8,128)} %copy-done.4) | copy-start | bytes 3145732
  58.1 1.2 %copy-start.9 = (f32[2048,128]{1,0:T(8,128)S(1)}, f32[2048,128]{1,0:T(8,128)}, u32[]{:S(2)}) copy-start(f32[2048,128]{1,0:T(8,128)} %copy-done.8) | copy-start | bytes 3145732
  70.8 21.3 %collective-permute-start.11 = (bf16[1056,128]{1,0:T(8,128)(2,1)S(1)}, bf16[1056,128]{1,0:T(8,128)(2,1)S(1)}, u32[]{:S(2)}, u32[]{:S(2)}) collective-permute-start(bf16[1056,128]{1,0:T(8,128)(2,1)S(1)} %slice.3), channel_id=1, source_target_pairs={{0,128},{16,144},{32,160},{48,176},{64,192},{80,208},{96,224},{112... | collective-permute-start | bytes 811016 | tf_op jit(solution)/shard_map/ppermute | solution.py:142
  72.7 19.4 %collective-permute-start.10 = (bf16[1056,128]{1,0:T(8,128)(2,1)S(1)}, bf16[1056,128]{1,0:T(8,128)(2,1)S(1)}, u32[]{:S(2)}, u32[]{:S(2)}) collective-permute-start(bf16[1056,128]{1,0:T(8,128)(2,1)S(1)} %collective-permute-done.9.refs_8_), channel_id=1, source_target_pairs={{0,16},{16,0},{32,48},{48,32},{64,80},{80,64},{96,112},{112,96},{1... | collective-permute-start | bytes 811016 | tf_op jit(solution)/shard_map/ppermute | solution.py:138
  (1 other events, 1.0 us)

commit v2 on v1

v2 whole, which is shorter than its diff:
```python
import functools
import math

import jax
import jax.numpy as jnp
from jax import lax
from jax.experimental import pallas as pl
from jax.experimental.pallas import tpu as pltpu
from jax.sharding import PartitionSpec as P

HEAD = 128
BLOCK = 256
HEADS = 8
TOGETHER = 4
IDS = 16
SLOT = 2 * BLOCK + IDS
WIDE = 2 * BLOCK
NX, NZ = 4, 8
NEGATIVE = -1e30
FACTOR = HEAD**-0.5 * math.log2(math.e)
LOW, HIGH = 2.0**-80, 2.0**100


def contract_last(a, b):
    return lax.dot_general(a, b, (((1,), (1,)), ((), ())), preferred_element_type=jnp.float32)


def lane_sum(weights):
    parts = [weights[:, i : i + HEAD] for i in range(0, weights.shape[1], HEAD)]
    while len(parts) > 1:
        parts = [a + b for a, b in zip(parts[::2], parts[1::2])]
    return parts[0]


def own_masks(own_ref):
    ids = own_ref[2 * BLOCK :, :].astype(jnp.float32)
    key_ids = jnp.concatenate([ids[0:1, :], ids[1:2, :]], axis=1)
    key_ids = jnp.broadcast_to(key_ids, (BLOCK, BLOCK))
    query_ids = key_ids.T
    q_pos = lax.broadcasted_iota(jnp.int32, (BLOCK, BLOCK), 0)
    k_pos = lax.broadcasted_iota(jnp.int32, (BLOCK, BLOCK), 1)
    visible = (key_ids == query_ids) & (k_pos <= q_pos)
    in_first = (query_ids == key_ids[0:1, 0:1])[:, :HEAD]
    return visible, in_first


def own_kernel(q_ref, own_ref, l_ref, acc_ref, first_ref):
    visible, in_first = own_masks(own_ref)
    first_ref[...] = jnp.where(in_first, 1.0, 0.0)
    keys = own_ref[:BLOCK, :]
    values = own_ref[BLOCK : 2 * BLOCK, :]
    for h in range(HEADS):
        rows = pl.ds(h * BLOCK, BLOCK)
        scores = contract_last(q_ref[:, h * HEAD : (h + 1) * HEAD], keys) * FACTOR
        weights = jnp.exp2(jnp.where(visible, scores, NEGATIVE))
        l_ref[rows, :] = lane_sum(weights)
        acc_ref[rows, :] = jnp.dot(
            weights.astype(jnp.bfloat16), values, preferred_element_type=jnp.float32
        )


def seen_rows(first_id, ids):
    ids = ids.astype(jnp.float32)
    return jnp.sum(jnp.where(ids == first_id, 1.0, 0.0)).astype(jnp.int32)


def add_blocks(slots, counts, ok_ref, q_ref, own_ref, l_sum, acc_sum, k_buf, v_buf, part):
    first_id = own_ref[2 * BLOCK :, :].astype(jnp.float32)[0:1, 0:1]
    full = jnp.int32(0)
    partial = jnp.int32(0)
    at = 0
    for ref, count in zip(slots, counts):
        for k in range(count):
            base = k * SLOT
            seen = seen_rows(first_id, ref[base + 2 * BLOCK : base + SLOT, :]) * ok_ref[at]
            at += 1
            whole = seen == BLOCK

            @pl.when(whole)
            def _():
                to = pl.ds(pl.multiple_of(full * BLOCK, BLOCK), BLOCK)
                k_buf[to, :] = ref[base : base + BLOCK, :]
                v_buf[to, :] = ref[base + BLOCK : base + 2 * BLOCK, :]

            @pl.when((seen > 0) & (seen < BLOCK))
            def _():
                part[...] = ref[base : base + 2 * BLOCK, :]

            full = full + whole.astype(jnp.int32)
            partial = partial + jnp.where(whole, 0, seen)

    def attend(chunk, limit):
        at = pl.ds(pl.multiple_of(chunk * WIDE, WIDE), WIDE)
        keys, values = k_buf[at, :], v_buf[at, :]
        for h in range(0, HEADS, TOGETHER):
            rows = pl.ds(h * BLOCK, TOGETHER * BLOCK)
            some = [q_ref[:, i * HEAD : (i + 1) * HEAD] for i in range(h, h + TOGETHER)]
            scores = contract_last(jnp.concatenate(some, axis=0), keys) * FACTOR
            if limit is not None:
                scores = scores + limit
            weights = jnp.exp2(scores)
            l_sum[rows, :] += lane_sum(weights)
            acc_sum[rows, :] += jnp.dot(
                weights.astype(jnp.bfloat16), values, preferred_element_type=jnp.float32
            )

    found = (full > 0) | (partial > 0)
    pairs = full // 2
    odd = full - 2 * pairs

    @pl.when(found)
    def _():
        l_sum[...] = jnp.zeros_like(l_sum)
        acc_sum[...] = jnp.zeros_like(acc_sum)

    @pl.loop(0, pairs)
    def _(chunk):
        attend(chunk, None)

    @pl.when((odd > 0) | (partial > 0))
    def _():
        left = pl.ds(pl.multiple_of(pairs * WIDE, WIDE), BLOCK)
        right = pl.ds(pl.multiple_of(pairs * WIDE + BLOCK, BLOCK), BLOCK)
        none = jnp.zeros((BLOCK, HEAD), jnp.bfloat16)

        @pl.when(odd == 0)
        def _():
            k_buf[left, :] = none
            v_buf[left, :] = none

        @pl.when(partial > 0)
        def _():
            k_buf[right, :] = part[:BLOCK, :]
            v_buf[right, :] = part[BLOCK:, :]

        @pl.when(partial == 0)
        def _():
            k_buf[right, :] = none
            v_buf[right, :] = none

        k_pos = lax.broadcasted_iota(jnp.int32, (1, WIDE), 1)
        shown = ((k_pos < BLOCK) & (odd > 0)) | (k_pos >= WIDE - partial)
        attend(pairs, jnp.where(shown, 0.0, NEGATIVE))

    return found


def more_kernel(counts, *refs):
    n = len(counts)
    ok_ref, q_ref, own_ref, l_in, acc_in, first_ref = refs[:6]
    slots = refs[6 : 6 + n]
    l_ref, acc_ref, l_sum, acc_sum, k_buf, v_buf, part = refs[6 + n :]
    found = add_blocks(
        slots, counts, ok_ref, q_ref, own_ref, l_sum, acc_sum, k_buf, v_buf, part
    )

    @pl.when(found)
    def _():
        keep = first_ref[...] > 0.0
        for h in range(HEADS):
            rows = pl.ds(h * BLOCK, BLOCK)
            l_ref[rows, :] = l_in[rows, :] + jnp.where(keep, l_sum[rows, :], 0.0)
            acc_ref[rows, :] = acc_in[rows, :] + jnp.where(keep, acc_sum[rows, :], 0.0)

    @pl.when(jnp.logical_not(found))
    def _():
        l_ref[...] = l_in[...]
        acc_ref[...] = acc_in[...]


def last_kernel(counts, all_counts, *refs):
    n, m = len(counts), len(all_counts)
    ok_ref, all_ok_ref, q_ref, own_ref, l_in, acc_in, first_ref = refs[:7]
    slots, everything = refs[7 : 7 + n], refs[7 + n : 7 + n + m]
    out_ref, l_sum, acc_sum, k_buf, v_buf, part, store, top, sem = refs[7 + n + m :]
    found = add_blocks(
        slots, counts, ok_ref, q_ref, own_ref, l_sum, acc_sum, k_buf, v_buf, part
    )

    @pl.when(jnp.logical_not(found))
    def _():
        l_sum[...] = jnp.zeros_like(l_sum)
        acc_sum[...] = jnp.zeros_like(acc_sum)

    keep = first_ref[...] > 0.0
    fine = jnp.ones((BLOCK, 1), jnp.float32)
    for h in range(HEADS):
        rows = pl.ds(h * BLOCK, BLOCK)
        total = l_in[rows, :] + jnp.where(keep, l_sum[rows, :], 0.0)
        total = jnp.sum(total, axis=1, keepdims=True)
        fine = jnp.where((total >= LOW) & (total <= HIGH), fine, 0.0)
        weighted = acc_in[rows, :] + jnp.where(keep, acc_sum[rows, :], 0.0)
        out_ref[:, h * HEAD : (h + 1) * HEAD] = (weighted / total).astype(jnp.bfloat16)

    @pl.when(jnp.min(fine) < 0.5)
    def _():
        at = 0
        for ref, count in zip(everything, all_counts):
            for k in range(count):
                copy = pltpu.make_async_copy(
                    ref.at[k * SLOT : (k + 1) * SLOT, :], store.at[at], sem
                )
                copy.start()
                copy.wait()
                at += 1
        with_maximum(at, all_ok_ref, q_ref, own_ref, store, top, l_sum, acc_sum, out_ref)


def with_maximum(count, ok_ref, q_ref, own_ref, store, top, l_sum, acc_sum, out_ref):
    visible, in_first = own_masks(own_ref)
    first_id = own_ref[2 * BLOCK :, :].astype(jnp.float32)[0:1, 0:1]
    own_bias = jnp.where(visible, 0.0, NEGATIVE)

    def head(h, carry):
        q = q_ref[:, pl.ds(pl.multiple_of(h * HEAD, HEAD), HEAD)]
        scores = contract_last(q, own_ref[:BLOCK, :]) * FACTOR + own_bias
        first_top = jnp.max(scores, axis=1, keepdims=True)
        weights = jnp.exp2(scores - first_top)
        top[...] = jnp.where(in_first, jnp.broadcast_to(first_top, (BLOCK, HEAD)), -NEGATIVE)
        l_sum[:BLOCK, :] = lane_sum(weights)
        acc_sum[:BLOCK, :] = jnp.dot(
            weights.astype(jnp.bfloat16),
            own_ref[BLOCK : 2 * BLOCK, :],
            preferred_element_type=jnp.float32,
        )

        def block(j, carry):
            seen = seen_rows(first_id, store[j, 2 * BLOCK :, :]) * ok_ref[j]

            @pl.when(seen > 0)
            def _():
                k_pos = lax.broadcasted_iota(jnp.int32, (1, BLOCK), 1)
                limit = jnp.where(k_pos >= BLOCK - seen, 0.0, NEGATIVE)
                scores = contract_last(q, store[j, :BLOCK, :]) * FACTOR + limit
                old = top[...]
                new = jnp.maximum(old, jnp.max(scores, axis=1, keepdims=True))
                fade = jnp.exp2(old - new)
                weights = jnp.exp2(scores - new[:, 0:1])
                l_sum[:BLOCK, :] = l_sum[:BLOCK, :] * fade + lane_sum(weights)
                acc_sum[:BLOCK, :] = acc_sum[:BLOCK, :] * fade + jnp.dot(
                    weights.astype(jnp.bfloat16),
                    store[j, BLOCK : 2 * BLOCK, :],
                    preferred_element_type=jnp.float32,
                )
                top[...] = new

            return carry

        lax.fori_loop(0, count, block, 0)
        total = jnp.sum(l_sum[:BLOCK, :], axis=1, keepdims=True)
        out_ref[:, pl.ds(pl.multiple_of(h * HEAD, HEAD), HEAD)] = (
            acc_sum[:BLOCK, :] / total
        ).astype(jnp.bfloat16)
        return carry

    lax.fori_loop(0, HEADS, head, 0)


VMEM = pl.BlockSpec(memory_space=pltpu.VMEM)
SMEM = pl.BlockSpec(memory_space=pltpu.SMEM)
SUMS = jax.ShapeDtypeStruct((HEADS * BLOCK, HEAD), jnp.float32)
FIRST = jax.ShapeDtypeStruct((BLOCK, HEAD), jnp.float32)
PARAMS = pltpu.CompilerParams(vmem_limit_bytes=24 * 1024 * 1024)


def cost(blocks):
    pairs = blocks
    return pl.CostEstimate(
        flops=4 * HEAD * pairs, bytes_accessed=1, transcendentals=pairs
    )


def buffers(blocks):
    rows = (blocks + blocks % 2 + 2) * BLOCK
    return [
        pltpu.VMEM(SUMS.shape, jnp.float32),
        pltpu.VMEM(SUMS.shape, jnp.float32),
        pltpu.VMEM((rows, HEAD), jnp.bfloat16),
        pltpu.VMEM((rows, HEAD), jnp.bfloat16),
        pltpu.VMEM((2 * BLOCK, HEAD), jnp.bfloat16),
    ]


def attend_own(q, own):
    return pl.pallas_call(
        own_kernel, out_shape=[SUMS, SUMS, FIRST], in_specs=[VMEM] * 2, out_specs=[VMEM] * 3,
        compiler_params=PARAMS, cost_estimate=cost(1), name="attend_own",
    )(q, own)


def stack_ok(ok):
    return jnp.stack([jnp.asarray(o, jnp.int32) for o in ok])


def attend_more(state, q, own, arrays, ok):
    counts = [a.shape[0] // SLOT for a in arrays]
    sums = pl.pallas_call(
        functools.partial(more_kernel, counts),
        out_shape=[SUMS, SUMS],
        in_specs=[SMEM] + [VMEM] * (5 + len(arrays)),
        out_specs=[VMEM] * 2,
        scratch_shapes=buffers(sum(counts)),
        compiler_params=PARAMS, cost_estimate=cost(sum(counts)), name="attend_more",
    )(stack_ok(ok), q, own, *state, *arrays)
    return *sums, state[2]


def attend_last(state, q, own, arrays, ok, everything, all_ok):
    counts = [a.shape[0] // SLOT for a in arrays]
    all_counts = [a.shape[0] // SLOT for a in everything]
    return pl.pallas_call(
        functools.partial(last_kernel, counts, all_counts),
        out_shape=jax.ShapeDtypeStruct((BLOCK, HEADS * HEAD), jnp.bfloat16),
        in_specs=[SMEM] * 2 + [VMEM] * (5 + len(arrays))
        + [pl.BlockSpec(memory_space=pl.ANY)] * len(everything),
        out_specs=VMEM,
        scratch_shapes=buffers(sum(counts))
        + [
            pltpu.VMEM((sum(all_counts), SLOT, HEAD), jnp.bfloat16),
            pltpu.VMEM((BLOCK, HEAD), jnp.float32),
            pltpu.SemaphoreType.DMA,
        ],
        compiler_params=PARAMS, cost_estimate=cost(sum(counts)), name="attend_last",
    )(stack_ok(ok), stack_ok(all_ok), q, own, *state, *arrays, *everything)


def exchange(v, mask):
    return lax.ppermute(v, "ctx", [(i, i ^ mask) for i in range(NX * NZ)])


def along_x(v, steps):
    return lax.ppermute(v, "ctx", [(i, i + NZ * steps) for i in range((NX - steps) * NZ)])


def together(*arrays):
    return lax.optimization_barrier(arrays)


def per_device(queries, keys, values, doc_ids):
    z = lax.axis_index("ctx") % NZ
    bit = [(z >> b) & 1 for b in range(3)]
    one = jnp.int32(1)
    ids = (doc_ids + 1).astype(jnp.bfloat16).reshape(2, HEAD)
    ids = jnp.pad(ids, ((0, IDS - 2), (0, 0)))
    own = jnp.concatenate([keys, values, ids], axis=0)
    q = queries

    p1 = exchange(own, 4)
    state = attend_own(q, own)
    state, p1 = together(state, p1)

    pair = jnp.concatenate([own, p1])
    b01 = along_x(pair, 1)
    c01 = along_x(pair, 2)
    p2 = exchange(pair, 2)
    state = attend_more(state, q, own, [p1], [bit[2]])
    state, p2, b01, c01 = together(state, p2, b01, c01)

    send = jnp.where(bit[0] == 0, own, c01[:SLOT])
    near0 = exchange(jnp.concatenate([b01[:SLOT], send]), 1)
    b2 = along_x(p2, 1)
    c2 = along_x(p2, 2)
    p3 = exchange(p2, 1)
    state = attend_more(state, q, own, [p2, b01, c01], [bit[1], bit[2]] + [one] * 4)
    state, near0, b2, c2, p3 = together(state, near0, b2, c2, p3)

    send = jnp.where(bit[2] == 1, p1, c01[SLOT:])
    near1 = exchange(jnp.concatenate([b01[SLOT:], send]), 1)
    b3 = along_x(p3, 1)
    c3 = exchange(c2, 1)
    state = attend_more(
        state, q, own, [near0, b2, c2, p3], [one] * 6 + [bit[1], bit[2]]
    )
    state, near1, b3, c3 = together(state, near1, b3, c3)

    arrays = [p1, p2, b01, c01, near0, b2, c2, p3, near1, b3, c3]
    ok = [bit[2], bit[1], bit[2]] + [one] * 10 + [bit[1], bit[2]] + [one] * 6
    return attend_last(state, q, own, [near1, b3, c3], [one] * 6, arrays, ok)


def solution(mesh):
    return jax.shard_map(
        per_device,
        mesh=mesh,
        in_specs=(
            P(("dp", "ctx"), "tp"),
            P(("dp", "ctx"), "tp"),
            P(("dp", "ctx"), "tp"),
            P(("dp", "ctx")),
        ),
        out_specs=P(("dp", "ctx"), "tp"),
        check_vma=False,
    )
```

time: 102 us -> 185 us (1.81)
  the two profiles are of different devices: /device:TPU:148 before, /device:TPU:4 now
where the time goes in v2:
time: 185 us; the launch traced here: 184 us
  Pallas kernels  119 us (64%)
  starting transfers between devices  31.9 us (17%)
  waiting for transfers between devices  22.2 us (12%)
  local copies, waits for them, and re-layouts  7.78 us (4%)
  other arithmetic  2.57 us (1%)
    pallas_call x1, Pallas kernels, attend_last(): pl.pallas_call(functools.partial(last_kernel, counts, all_counts), out_sh...  107 us
    ppermute x6, starting transfers between devices, exchange(): return lax.ppermute(v, 'ctx', [(i, i ^ mask) for i in range(NX * NZ)])  22.4 us
    ppermute x6, waiting for transfers between devices, exchange(): return lax.ppermute(v, 'ctx', [(i, i ^ mask) for i in range(NX * NZ)])  12.8 us
    pallas_call x3, Pallas kernels, attend_more(): pl.pallas_call(functools.partial(more_kernel, counts), out_shape=[SUMS, S...  10.8 us
    ppermute x5, starting transfers between devices, along_x(): lax.ppermute(v, 'ctx', [(i, i + NZ * steps) for i in range((NX - steps) *...  9.53 us
    ppermute x5, waiting for transfers between devices, along_x(): lax.ppermute(v, 'ctx', [(i, i + NZ * steps) for i in range((NX - steps) *...  9.45 us
    unnamed x20, local copies, waits for them, and re-layouts  7.68 us
  transfers between devices with their start and end apart: 11, of which 5 were waited for; matrix products, arithmetic and copies ran while one was open for 1% of the time, Pallas kernels for 6%

profile of v2, /device:TPU:4, one launch (start us, length us, event | category | flops | bytes accessed | tf_op | source)
XLA Modules:
  0.0 184.1 jit_solution(1604728382488872774)
XLA Ops:
  1.6 9.1 %collective-permute-start = (bf16[528,128]{1,0:T(8,128)(2,1)S(1)}, bf16[528,128]{1,0:T(8,128)(2,1)S(1)}, u32[]{:S(2)}, u32[]{:S(2)}) collective-permute-start(bf16[528,128]{1,0:T(8,128)(2,1)S(1)} %pad_maximum_fusion.3.own_ref.refs_2_.refs_3_), channel_id=1, source_target_pairs={{0,64},{16,80},{32,96},{48,112},{64,0},{80,16},{96,32},{112,48},{1... | collective-permute-start | bytes 405512 | tf_op jit(solution)/shard_map/ppermute | solution.py:328
  10.7 1.0 copy-done
  12.7 1.0 copy-done.2
  13.7 9.2 %collective-permute-done.refs_6_.refs_10_ = bf16[528,128]{1,0:T(8,128)(2,1)S(1)} collective-permute-done((bf16[528,128]{1,0:T(8,128)(2,1)S(1)}, bf16[528,128]{1,0:T(8,128)(2,1)S(1)}, u32[]{:S(2)}, u32[]{:S(2)}) %collective-permute-start) | collective-permute-done | bytes 135200 | tf_op jit(solution)/shard_map/ppermute | solution.py:328
  23.0 1.3 collective-permute-start.3
  24.3 3.1 %collective-permute-start.2 = (bf16[1056,128]{1,0:T(8,128)(2,1)S(1)}, bf16[1056,128]{1,0:T(8,128)(2,1)S(1)}, u32[]{:S(2)}, u32[]{:S(2)}) collective-permute-start(bf16[1056,128]{1,0:T(8,128)(2,1)S(1)} %pad_maximum_fusion), channel_id=1, source_target_pairs={{0,128},{16,144},{32,160},{48,176},{64,192},{80,208},{96,224},{112... | collective-permute-start | bytes 811016 | tf_op jit(solution)/shard_map/ppermute | solution.py:332
  27.4 1.9 %collective-permute-start.1 = (bf16[1056,128]{1,0:T(8,128)(2,1)S(1)}, bf16[1056,128]{1,0:T(8,128)(2,1)S(1)}, u32[]{:S(2)}, u32[]{:S(2)}) collective-permute-start(bf16[1056,128]{1,0:T(8,128)(2,1)S(1)} %pad_maximum_fusion), channel_id=1, source_target_pairs={{0,32},{16,48},{32,0},{48,16},{64,96},{80,112},{96,64},{112,80},{1... | collective-permute-start | bytes 811016 | tf_op jit(solution)/shard_map/ppermute | solution.py:328
  29.3 1.2 copy-done.3
  30.9 4.9 %collective-permute-done.3.refs_8_.refs_13_ = bf16[1056,128]{1,0:T(8,128)(2,1)S(1)} collective-permute-done((bf16[1056,128]{1,0:T(8,128)(2,1)S(1)}, bf16[1056,128]{1,0:T(8,128)(2,1)S(1)}, u32[]{:S(2)}, u32[]{:S(2)}) %collective-permute-start.3) | collective-permute-done | bytes 270368 | tf_op jit(solution)/shard_map/ppermute | solution.py:332
  35.8 4.0 %collective-permute-done.2.refs_7_.refs_12_ = bf16[1056,128]{1,0:T(8,128)(2,1)S(1)} collective-permute-done((bf16[1056,128]{1,0:T(8,128)(2,1)S(1)}, bf16[1056,128]{1,0:T(8,128)(2,1)S(1)}, u32[]{:S(2)}, u32[]{:S(2)}) %collective-permute-start.2) | collective-permute-done | bytes 270368 | tf_op jit(solution)/shard_map/ppermute | solution.py:332
  39.8 3.5 %collective-permute-done.1.refs_6_.refs_11_ = bf16[1056,128]{1,0:T(8,128)(2,1)S(1)} collective-permute-done((bf16[1056,128]{1,0:T(8,128)(2,1)S(1)}, bf16[1056,128]{1,0:T(8,128)(2,1)S(1)}, u32[]{:S(2)}, u32[]{:S(2)}) %collective-permute-start.1) | collective-permute-done | bytes 270368 | tf_op jit(solution)/shard_map/ppermute | solution.py:328
  43.4 1.9 %collective-permute-start.7 = (bf16[1056,128]{1,0:T(8,128)(2,1)S(1)}, bf16[1056,128]{1,0:T(8,128)(2,1)S(1)}, u32[]{:S(2)}, u32[]{:S(2)}) collective-permute-start(bf16[1056,128]{1,0:T(8,128)(2,1)S(1)} %collective-permute-done.1.refs_6_.refs_11_), channel_id=1, source_target_pairs={{0,16},{16,0},{32,48},{48,32},{64,80},{80,64},{96,112},{112,96},{1... | collective-permute-start | bytes 811016 | tf_op jit(solution)/shard_map/ppermute | solution.py:328
  45.3 1.3 collective-permute-start.6
  46.6 1.9 %collective-permute-start.5 = (bf16[1056,128]{1,0:T(8,128)(2,1)S(1)}, bf16[1056,128]{1,0:T(8,128)(2,1)S(1)}, u32[]{:S(2)}, u32[]{:S(2)}) collective-permute-start(bf16[1056,128]{1,0:T(8,128)(2,1)S(1)} %collective-permute-done.1.refs_6_.refs_11_), channel_id=1, source_target_pairs={{0,128},{16,144},{32,160},{48,176},{64,192},{80,208},{96,224},{112... | collective-permute-start | bytes 811016 | tf_op jit(solution)/shard_map/ppermute | solution.py:332
  48.6 3.9 %collective-permute-start.4 = (bf16[1056,128]{1,0:T(8,128)(2,1)S(1)}, bf16[1056,128]{1,0:T(8,128)(2,1)S(1)}, u32[]{:S(2)}, u32[]{:S(2)}) collective-permute-start(bf16[1056,128]{1,0:T(8,128)(2,1)S(1)} %pad_maximum_fusion.1), channel_id=1, source_target_pairs={{0,16},{16,0},{32,48},{48,32},{64,80},{80,64},{96,112},{112,96},{1... | collective-permute-start | bytes 811016 | tf_op jit(solution)/shard_map/ppermute | solution.py:328
  53.4 1.9 %collective-permute-start.8 = (bf16[1056,128]{1,0:T(8,128)(2,1)}, bf16[1056,128]{1,0:T(8,128)(2,1)S(1)}, u32[]{:S(2)}, u32[]{:S(2)}) collective-permute-start(bf16[1056,128]{1,0:T(8,128)(2,1)} %pad_maximum_fusion.2), channel_id=1, source_target_pairs={{0,16},{16,0},{32,48},{48,32},{64,80},{80,64},{96,112},{112,96},{1... | collective-permute-start | bytes 811016 | tf_op jit(solution)/shard_map/ppermute | solution.py:328
  55.3 4.4 %attend_more.4 = (f32[2048,128]{1,0:T(8,128)S(1)}, f32[2048,128]{1,0:T(8,128)S(1)}) custom-call(s32[6]{0:T(128)S(1)} %pad_add_fusion.1.refs_0_, bf16[256,1024]{1,0:T(8,128)(2,1)S(1)} %copy-done.1, bf16[528,128]{1,0:T(8,128)(2,1)S(1)} %pad_maximum_fusion.3.own_ref.refs_2_.refs_3_, f32[2048,128]{1,0:T(8,128)S(1)} %get-tuple-element.46.refs_3_, ...), custom_call_target="tpu_custom_call" | custom-call | flops 3072 | bytes 1 | tf_op jit(solution)/shard_map/attend_more/pallas_call | solution.py:297
  59.7 1.0 copy-done.4
  62.2 3.6 %collective-permute-start.10 = (bf16[1056,128]{1,0:T(8,128)(2,1)S(1)}, bf16[1056,128]{1,0:T(8,128)(2,1)S(1)}, u32[]{:S(2)}, u32[]{:S(2)}) collective-permute-start(bf16[1056,128]{1,0:T(8,128)(2,1)S(1)} %collective-permute-done.6.refs_8_.refs_16_), channel_id=1, source_target_pairs={{0,16},{16,0},{32,48},{48,32},{64,80},{80,64},{96,112},{112,96},{1... | collective-permute-start | bytes 811016 | tf_op jit(solution)/shard_map/ppermute | solution.py:328
  65.8 1.9 %collective-permute-start.9 = (bf16[1056,128]{1,0:T(8,128)(2,1)S(1)}, bf16[1056,128]{1,0:T(8,128)(2,1)}, u32[]{:S(2)}, u32[]{:S(2)}) collective-permute-start(bf16[1056,128]{1,0:T(8,128)(2,1)S(1)} %collective-permute-done.7.refs_9_.refs_17_), channel_id=1, source_target_pairs={{0,128},{16,144},{32,160},{48,176},{64,192},{80,208},{96,224},{112... | collective-permute-start | bytes 811016 | tf_op jit(solution)/shard_map/ppermute | solution.py:332
  67.9 1.2 copy-done.5
  69.2 1.2 copy-done.7
  70.4 6.1 %attend_more.5 = (f32[2048,128]{1,0:T(8,128)S(1)}, f32[2048,128]{1,0:T(8,128)S(1)}) custom-call(s32[8]{0:T(128)S(1)} %pad_add_fusion.refs_0_, bf16[256,1024]{1,0:T(8,128)(2,1)S(1)} %copy-done.1, bf16[528,128]{1,0:T(8,128)(2,1)S(1)} %pad_maximum_fusion.3.own_ref.refs_2_.refs_3_, f32[2048,128]{1,0:T(8,128)S(1)} %copy-done.5, f32[2048,128]{1,0:T(8,128)S(1)} %copy-done.7, ...), custom_call_target="tpu_custom_call" | custom-call | flops 4096 | bytes 1 | tf_op jit(solution)/shard_map/attend_more/pallas_call | solution.py:297
  76.5 107.4 %attend_last.1 = bf16[256,1024]{1,0:T(8,128)(2,1)} custom-call(s32[6]{0:T(128)S(1)} %broadcast_5_refs_0_.2.refs_0_, s32[21]{0:T(128)S(1)} %stack.12.refs_1_, bf16[256,1024]{1,0:T(8,128)(2,1)S(1)} %copy-done.1, bf16[528,128]{1,0:T(8,128)(2,1)S(1)} %pad_maximum_fusion.3.own_ref.refs_2_.refs_3_, f32[2048,128]{1,0:T(8,128)S(1)} %get-tuple-element.63.refs_4_, ...), custom_call_target="tpu_custom_call" | custom-call | flops 3072 | bytes 1 | tf_op jit(solution)/shard_map/attend_last/pallas_call | solution.py:311
  (37 shorter events, 5.5 us)
Async XLA Ops:
  1.6 21.4 %collective-permute-start = (bf16[528,128]{1,0:T(8,128)(2,1)S(1)}, bf16[528,128]{1,0:T(8,128)(2,1)S(1)}, u32[]{:S(2)}, u32[]{:S(2)}) collective-permute-start(bf16[528,128]{1,0:T(8,128)(2,1)S(1)} %pad_maximum_fusion.3.own_ref.refs_2_.refs_3_), channel_id=1, source_target_pairs={{0,64},{16,80},{32,96},{48,112},{64,0},{80,16},{96,32},{112,48},{1... | collective-permute-start | bytes 405512 | tf_op jit(solution)/shard_map/ppermute | solution.py:328
  10.7 1.0 copy-start
  11.7 11.2 %copy-start.8 = (bf16[256,128]{1,0:T(8,128)(2,1)S(1)}, bf16[256,128]{1,0:T(8,128)(2,1)}, u32[]{:S(2)}) copy-start(bf16[256,128]{1,0:T(8,128)(2,1)} %param.6) | copy-start | bytes 196612
  11.7 11.2 %copy-start.9 = (bf16[256,128]{1,0:T(8,128)(2,1)S(1)}, bf16[256,128]{1,0:T(8,128)(2,1)}, u32[]{:S(2)}) copy-start(bf16[256,128]{1,0:T(8,128)(2,1)} %param.5) | copy-start | bytes 196612
  11.7 17.6 %copy-start.1 = (bf16[256,1024]{1,0:T(8,128)(2,1)S(1)}, bf16[256,1024]{1,0:T(8,128)(2,1)}, u32[]{:S(2)}) copy-start(bf16[256,1024]{1,0:T(8,128)(2,1)} %refs_2_.1) | copy-start | bytes 1572868
  12.7 1.0 copy-start.2
  23.0 12.9 %collective-permute-start.3 = (bf16[1056,128]{1,0:T(8,128)(2,1)S(1)}, bf16[1056,128]{1,0:T(8,128)(2,1)S(1)}, u32[]{:S(2)}, u32[]{:S(2)}) collective-permute-start(bf16[1056,128]{1,0:T(8,128)(2,1)S(1)} %pad_maximum_fusion), channel_id=1, source_target_pairs={{0,256},{16,272},{32,288},{48,304},{64,320},{80,336},{96,352},{112... | collective-permute-start | bytes 811016 | tf_op jit(solution)/shard_map/ppermute | solution.py:332
  24.3 15.6 %collective-permute-start.2 = (bf16[1056,128]{1,0:T(8,128)(2,1)S(1)}, bf16[1056,128]{1,0:T(8,128)(2,1)S(1)}, u32[]{:S(2)}, u32[]{:S(2)}) collective-permute-start(bf16[1056,128]{1,0:T(8,128)(2,1)S(1)} %pad_maximum_fusion), channel_id=1, source_target_pairs={{0,128},{16,144},{32,160},{48,176},{64,192},{80,208},{96,224},{112... | collective-permute-start | bytes 811016 | tf_op jit(solution)/shard_map/ppermute | solution.py:332
  27.4 16.0 %collective-permute-start.1 = (bf16[1056,128]{1,0:T(8,128)(2,1)S(1)}, bf16[1056,128]{1,0:T(8,128)(2,1)S(1)}, u32[]{:S(2)}, u32[]{:S(2)}) collective-permute-start(bf16[1056,128]{1,0:T(8,128)(2,1)S(1)} %pad_maximum_fusion), channel_id=1, source_target_pairs={{0,32},{16,48},{32,0},{48,16},{64,96},{80,112},{96,64},{112,80},{1... | collective-permute-start | bytes 811016 | tf_op jit(solution)/shard_map/ppermute | solution.py:328
  29.3 1.2 copy-start.3
  43.4 18.3 %collective-permute-start.7 = (bf16[1056,128]{1,0:T(8,128)(2,1)S(1)}, bf16[1056,128]{1,0:T(8,128)(2,1)S(1)}, u32[]{:S(2)}, u32[]{:S(2)}) collective-permute-start(bf16[1056,128]{1,0:T(8,128)(2,1)S(1)} %collective-permute-done.1.refs_6_.refs_11_), channel_id=1, source_target_pairs={{0,16},{16,0},{32,48},{48,32},{64,80},{80,64},{96,112},{112,96},{1... | collective-permute-start | bytes 811016 | tf_op jit(solution)/shard_map/ppermute | solution.py:328
  45.3 16.4 %collective-permute-start.6 = (bf16[1056,128]{1,0:T(8,128)(2,1)S(1)}, bf16[1056,128]{1,0:T(8,128)(2,1)S(1)}, u32[]{:S(2)}, u32[]{:S(2)}) collective-permute-start(bf16[1056,128]{1,0:T(8,128)(2,1)S(1)} %collective-permute-done.1.refs_6_.refs_11_), channel_id=1, source_target_pairs={{0,256},{16,272},{32,288},{48,304},{64,320},{80,336},{96,352},{112... | collective-permute-start | bytes 811016 | tf_op jit(solution)/shard_map/ppermute | solution.py:332
  46.6 15.6 %collective-permute-start.5 = (bf16[1056,128]{1,0:T(8,128)(2,1)S(1)}, bf16[1056,128]{1,0:T(8,128)(2,1)S(1)}, u32[]{:S(2)}, u32[]{:S(2)}) collective-permute-start(bf16[1056,128]{1,0:T(8,128)(2,1)S(1)} %collective-permute-done.1.refs_6_.refs_11_), channel_id=1, source_target_pairs={{0,128},{16,144},{32,160},{48,176},{64,192},{80,208},{96,224},{112... | collective-permute-start | bytes 811016 | tf_op jit(solution)/shard_map/ppermute | solution.py:332
  48.6 13.6 %collective-permute-start.4 = (bf16[1056,128]{1,0:T(8,128)(2,1)S(1)}, bf16[1056,128]{1,0:T(8,128)(2,1)S(1)}, u32[]{:S(2)}, u32[]{:S(2)}) collective-permute-start(bf16[1056,128]{1,0:T(8,128)(2,1)S(1)} %pad_maximum_fusion.1), channel_id=1, source_target_pairs={{0,16},{16,0},{32,48},{48,32},{64,80},{80,64},{96,112},{112,96},{1... | collective-permute-start | bytes 811016 | tf_op jit(solution)/shard_map/ppermute | solution.py:328
  53.4 23.1 %collective-permute-start.8 = (bf16[1056,128]{1,0:T(8,128)(2,1)}, bf16[1056,128]{1,0:T(8,128)(2,1)S(1)}, u32[]{:S(2)}, u32[]{:S(2)}) collective-permute-start(bf16[1056,128]{1,0:T(8,128)(2,1)} %pad_maximum_fusion.2), channel_id=1, source_target_pairs={{0,16},{16,0},{32,48},{48,32},{64,80},{80,64},{96,112},{112,96},{1... | collective-permute-start | bytes 811016 | tf_op jit(solution)/shard_map/ppermute | solution.py:328
  59.7 1.0 copy-start.4
  60.7 1.0 copy-start.6
  62.2 14.3 %collective-permute-start.10 = (bf16[1056,128]{1,0:T(8,128)(2,1)S(1)}, bf16[1056,128]{1,0:T(8,128)(2,1)S(1)}, u32[]{:S(2)}, u32[]{:S(2)}) collective-permute-start(bf16[1056,128]{1,0:T(8,128)(2,1)S(1)} %collective-permute-done.6.refs_8_.refs_16_), channel_id=1, source_target_pairs={{0,16},{16,0},{32,48},{48,32},{64,80},{80,64},{96,112},{112,96},{1... | collective-permute-start | bytes 811016 | tf_op jit(solution)/shard_map/ppermute | solution.py:328
  65.8 10.7 %collective-permute-start.9 = (bf16[1056,128]{1,0:T(8,128)(2,1)S(1)}, bf16[1056,128]{1,0:T(8,128)(2,1)}, u32[]{:S(2)}, u32[]{:S(2)}) collective-permute-start(bf16[1056,128]{1,0:T(8,128)(2,1)S(1)} %collective-permute-done.7.refs_9_.refs_17_), channel_id=1, source_target_pairs={{0,128},{16,144},{32,160},{48,176},{64,192},{80,208},{96,224},{112... | collective-permute-start | bytes 811016 | tf_op jit(solution)/shard_map/ppermute | solution.py:332
  67.9 1.2 copy-start.5
  69.2 1.2 copy-start.7

commit v3 on v2

--- a/solution.py
+++ b/solution.py
@@ -18,7 +18,7 @@
 NX, NZ = 4, 8
 NEGATIVE = -1e30
 FACTOR = HEAD**-0.5 * math.log2(math.e)
-LOW, HIGH = 2.0**-80, 2.0**100
+HIGH = 2.0**100
 
 
 def contract_last(a, b):
@@ -44,19 +44,23 @@
     return visible, in_first
 
 
-def own_kernel(q_ref, own_ref, l_ref, acc_ref, first_ref):
+def own_kernel(q_ref, own_ref, shift_ref, l_ref, acc_ref):
     visible, in_first = own_masks(own_ref)
-    first_ref[...] = jnp.where(in_first, 1.0, 0.0)
     keys = own_ref[:BLOCK, :]
     values = own_ref[BLOCK : 2 * BLOCK, :]
     for h in range(HEADS):
         rows = pl.ds(h * BLOCK, BLOCK)
         scores = contract_last(q_ref[:, h * HEAD : (h + 1) * HEAD], keys) * FACTOR
-        weights = jnp.exp2(jnp.where(visible, scores, NEGATIVE))
+        scores = jnp.where(visible, scores, NEGATIVE)
+        top = jnp.max(scores, axis=1, keepdims=True)
+        weights = jnp.exp2(scores - top)
         l_ref[rows, :] = lane_sum(weights)
         acc_ref[rows, :] = jnp.dot(
             weights.astype(jnp.bfloat16), values, preferred_element_type=jnp.float32
         )
+        shift_ref[rows, :] = jnp.where(
+            in_first, jnp.broadcast_to(top, (BLOCK, HEAD)), -NEGATIVE
+        )
 
 
 def seen_rows(first_id, ids):
@@ -64,7 +68,7 @@
     return jnp.sum(jnp.where(ids == first_id, 1.0, 0.0)).astype(jnp.int32)
 
 
-def add_blocks(slots, counts, ok_ref, q_ref, own_ref, l_sum, acc_sum, k_buf, v_buf, part):
+def add_blocks(slots, counts, ok_ref, q_ref, own_ref, shift_ref, l_ref, acc_ref, k_buf, v_buf, part):
     first_id = own_ref[2 * BLOCK :, :].astype(jnp.float32)[0:1, 0:1]
     full = jnp.int32(0)
     partial = jnp.int32(0)
@@ -98,20 +102,15 @@
             scores = contract_last(jnp.concatenate(some, axis=0), keys) * FACTOR
             if limit is not None:
                 scores = scores + limit
-            weights = jnp.exp2(scores)
-            l_sum[rows, :] += lane_sum(weights)
-            acc_sum[rows, :] += jnp.dot(
+            shift = shift_ref[rows, :]
+            weights = jnp.exp2(scores - jnp.concatenate([shift] * (WIDE // HEAD), axis=1))
+            l_ref[rows, :] += lane_sum(weights)
+            acc_ref[rows, :] += jnp.dot(
                 weights.astype(jnp.bfloat16), values, preferred_element_type=jnp.float32
             )
 
-    found = (full > 0) | (partial > 0)
     pairs = full // 2
     odd = full - 2 * pairs
-
-    @pl.when(found)
-    def _():
-        l_sum[...] = jnp.zeros_like(l_sum)
-        acc_sum[...] = jnp.zeros_like(acc_sum)
 
     @pl.loop(0, pairs)
     def _(chunk):
@@ -142,57 +141,39 @@
         shown = ((k_pos < BLOCK) & (odd > 0)) | (k_pos >= WIDE - partial)
         attend(pairs, jnp.where(shown, 0.0, NEGATIVE))
 
-    return found
-
 
 def more_kernel(counts, *refs):
     n = len(counts)
-    ok_ref, q_ref, own_ref, l_in, acc_in, first_ref = refs[:6]
+    ok_ref, q_ref, own_ref, shift_ref, l_in, acc_in = refs[:6]
     slots = refs[6 : 6 + n]
-    l_ref, acc_ref, l_sum, acc_sum, k_buf, v_buf, part = refs[6 + n :]
-    found = add_blocks(
-        slots, counts, ok_ref, q_ref, own_ref, l_sum, acc_sum, k_buf, v_buf, part
+    l_ref, acc_ref, k_buf, v_buf, part = refs[6 + n :]
+    l_ref[...] = l_in[...]
+    acc_ref[...] = acc_in[...]
+    add_blocks(
+        slots, counts, ok_ref, q_ref, own_ref, shift_ref, l_ref, acc_ref, k_buf, v_buf, part
     )
-
-    @pl.when(found)
-    def _():
-        keep = first_ref[...] > 0.0
-        for h in range(HEADS):
-            rows = pl.ds(h * BLOCK, BLOCK)
-            l_ref[rows, :] = l_in[rows, :] + jnp.where(keep, l_sum[rows, :], 0.0)
-            acc_ref[rows, :] = acc_in[rows, :] + jnp.where(keep, acc_sum[rows, :], 0.0)
-
-    @pl.when(jnp.logical_not(found))
-    def _():
-        l_ref[...] = l_in[...]
-        acc_ref[...] = acc_in[...]
 
 
 def last_kernel(counts, all_counts, *refs):
     n, m = len(counts), len(all_counts)
-    ok_ref, all_ok_ref, q_ref, own_ref, l_in, acc_in, first_ref = refs[:7]
+    ok_ref, all_ok_ref, q_ref, own_ref, shift_ref, l_in, acc_in = refs[:7]
     slots, everything = refs[7 : 7 + n], refs[7 + n : 7 + n + m]
-    out_ref, l_sum, acc_sum, k_buf, v_buf, part, store, top, sem = refs[7 + n + m :]
-    found = add_blocks(
-        slots, counts, ok_ref, q_ref, own_ref, l_sum, acc_sum, k_buf, v_buf, part
+    out_ref, l_ref, acc_ref, k_buf, v_buf, part, store, top, sem = refs[7 + n + m :]
+    l_ref[...] = l_in[...]
+    acc_ref[...] = acc_in[...]
+    add_blocks(
+        slots, counts, ok_ref, q_ref, own_ref, shift_ref, l_ref, acc_ref, k_buf, v_buf, part
     )
-
-    @pl.when(jnp.logical_not(found))
-    def _():
-        l_sum[...] = jnp.zeros_like(l_sum)
-        acc_sum[...] = jnp.zeros_like(acc_sum)
-
-    keep = first_ref[...] > 0.0
-    fine = jnp.ones((BLOCK, 1), jnp.float32)
+    most = jnp.zeros((BLOCK, 1), jnp.float32)
     for h in range(HEADS):
         rows = pl.ds(h * BLOCK, BLOCK)
-        total = l_in[rows, :] + jnp.where(keep, l_sum[rows, :], 0.0)
-        total = jnp.sum(total, axis=1, keepdims=True)
-        fine = jnp.where((total >= LOW) & (total <= HIGH), fine, 0.0)
-        weighted = acc_in[rows, :] + jnp.where(keep, acc_sum[rows, :], 0.0)
-        out_ref[:, h * HEAD : (h + 1) * HEAD] = (weighted / total).astype(jnp.bfloat16)
-
-    @pl.when(jnp.min(fine) < 0.5)
+        total = jnp.sum(l_ref[rows, :], axis=1, keepdims=True)
+        most = jnp.where(total <= HIGH, most, 1.0)
+        out_ref[:, h * HEAD : (h + 1) * HEAD] = (acc_ref[rows, :] * (1.0 / total)).astype(
+            jnp.bfloat16
+        )
+
+    @pl.when(jnp.max(most) > 0.5)
     def _():
         at = 0
         for ref, count in zip(everything, all_counts):
@@ -203,7 +184,7 @@
                 copy.start()
                 copy.wait()
                 at += 1
-        with_maximum(at, all_ok_ref, q_ref, own_ref, store, top, l_sum, acc_sum, out_ref)
+        with_maximum(at, all_ok_ref, q_ref, own_ref, store, top, l_ref, acc_ref, out_ref)
 
 
 def with_maximum(count, ok_ref, q_ref, own_ref, store, top, l_sum, acc_sum, out_ref):
@@ -249,7 +230,7 @@
         lax.fori_loop(0, count, block, 0)
         total = jnp.sum(l_sum[:BLOCK, :], axis=1, keepdims=True)
         out_ref[:, pl.ds(pl.multiple_of(h * HEAD, HEAD), HEAD)] = (
-            acc_sum[:BLOCK, :] / total
+            acc_sum[:BLOCK, :] * (1.0 / total)
         ).astype(jnp.bfloat16)
         return carry
 
@@ -259,22 +240,16 @@
 VMEM = pl.BlockSpec(memory_space=pltpu.VMEM)
 SMEM = pl.BlockSpec(memory_space=pltpu.SMEM)
 SUMS = jax.ShapeDtypeStruct((HEADS * BLOCK, HEAD), jnp.float32)
-FIRST = jax.ShapeDtypeStruct((BLOCK, HEAD), jnp.float32)
-PARAMS = pltpu.CompilerParams(vmem_limit_bytes=24 * 1024 * 1024)
-
-
-def cost(blocks):
-    pairs = blocks
-    return pl.CostEstimate(
-        flops=4 * HEAD * pairs, bytes_accessed=1, transcendentals=pairs
-    )
+COST = pl.CostEstimate(flops=1, bytes_accessed=1, transcendentals=0)
+
+
+def params(mib):
+    return pltpu.CompilerParams(vmem_limit_bytes=mib * 1024 * 1024)
 
 
 def buffers(blocks):
     rows = (blocks + blocks % 2 + 2) * BLOCK
     return [
-        pltpu.VMEM(SUMS.shape, jnp.float32),
-        pltpu.VMEM(SUMS.shape, jnp.float32),
         pltpu.VMEM((rows, HEAD), jnp.bfloat16),
         pltpu.VMEM((rows, HEAD), jnp.bfloat16),
         pltpu.VMEM((2 * BLOCK, HEAD), jnp.bfloat16),
@@ -283,8 +258,8 @@
 
 def attend_own(q, own):
     return pl.pallas_call(
-        own_kernel, out_shape=[SUMS, SUMS, FIRST], in_specs=[VMEM] * 2, out_specs=[VMEM] * 3,
-        compiler_params=PARAMS, cost_estimate=cost(1), name="attend_own",
+        own_kernel, out_shape=[SUMS] * 3, in_specs=[VMEM] * 2, out_specs=[VMEM] * 3,
+        compiler_params=params(12), cost_estimate=COST, name="attend_own",
     )(q, own)
 
 
@@ -296,13 +271,13 @@
     counts = [a.shape[0] // SLOT for a in arrays]
     sums = pl.pallas_call(
         functools.partial(more_kernel, counts),
-        out_shape=[SUMS, SUMS],
+        out_shape=[SUMS] * 2,
         in_specs=[SMEM] + [VMEM] * (5 + len(arrays)),
         out_specs=[VMEM] * 2,
         scratch_shapes=buffers(sum(counts)),
-        compiler_params=PARAMS, cost_estimate=cost(sum(counts)), name="attend_more",
+        compiler_params=params(12), cost_estimate=COST, name="attend_more",
     )(stack_ok(ok), q, own, *state, *arrays)
-    return *sums, state[2]
+    return state[0], *sums
 
 
 def attend_last(state, q, own, arrays, ok, everything, all_ok):
@@ -314,13 +289,14 @@
         in_specs=[SMEM] * 2 + [VMEM] * (5 + len(arrays))
         + [pl.BlockSpec(memory_space=pl.ANY)] * len(everything),
         out_specs=VMEM,
-        scratch_shapes=buffers(sum(counts))
+        scratch_shapes=[pltpu.VMEM(SUMS.shape, jnp.float32)] * 2
+        + buffers(sum(counts))
         + [
             pltpu.VMEM((sum(all_counts), SLOT, HEAD), jnp.bfloat16),
             pltpu.VMEM((BLOCK, HEAD), jnp.float32),
             pltpu.SemaphoreType.DMA,
         ],
-        compiler_params=PARAMS, cost_estimate=cost(sum(counts)), name="attend_last",
+        compiler_params=params(16), cost_estimate=COST, name="attend_last",
     )(stack_ok(ok), stack_ok(all_ok), q, own, *state, *arrays, *everything)
 
 
@@ -345,37 +321,38 @@
     own = jnp.concatenate([keys, values, ids], axis=0)
     q = queries
 
-    p1 = exchange(own, 4)
+    p4 = exchange(own, 4)
+    p2 = exchange(own, 2)
     state = attend_own(q, own)
-    state, p1 = together(state, p1)
-
-    pair = jnp.concatenate([own, p1])
-    b01 = along_x(pair, 1)
-    c01 = along_x(pair, 2)
-    p2 = exchange(pair, 2)
-    state = attend_more(state, q, own, [p1], [bit[2]])
-    state, p2, b01, c01 = together(state, p2, b01, c01)
-
-    send = jnp.where(bit[0] == 0, own, c01[:SLOT])
-    near0 = exchange(jnp.concatenate([b01[:SLOT], send]), 1)
-    b2 = along_x(p2, 1)
-    c2 = along_x(p2, 2)
-    p3 = exchange(p2, 1)
-    state = attend_more(state, q, own, [p2, b01, c01], [bit[1], bit[2]] + [one] * 4)
-    state, near0, b2, c2, p3 = together(state, near0, b2, c2, p3)
-
-    send = jnp.where(bit[2] == 1, p1, c01[SLOT:])
-    near1 = exchange(jnp.concatenate([b01[SLOT:], send]), 1)
-    b3 = along_x(p3, 1)
-    c3 = exchange(c2, 1)
-    state = attend_more(
-        state, q, own, [near0, b2, c2, p3], [one] * 6 + [bit[1], bit[2]]
-    )
-    state, near1, b3, c3 = together(state, near1, b3, c3)
-
-    arrays = [p1, p2, b01, c01, near0, b2, c2, p3, near1, b3, c3]
-    ok = [bit[2], bit[1], bit[2]] + [one] * 10 + [bit[1], bit[2]] + [one] * 6
-    return attend_last(state, q, own, [near1, b3, c3], [one] * 6, arrays, ok)
+    state, out = together(state, own)
+    b0 = along_x(out, 1)
+    c0 = along_x(out, 2)
+    state, p2, p4, b0, c0 = together(state, p2, p4, b0, c0)
+
+    near1 = exchange(jnp.concatenate([b0, jnp.where(bit[0] == 0, own, c0)]), 1)
+    pair = jnp.concatenate([p2, p4])
+    b24 = along_x(pair, 1)
+    c24 = along_x(pair, 2)
+    p6 = exchange(p4, 2)
+    state = attend_more(state, q, own, [p2, p4, b0, c0], [bit[1], bit[2], one, one])
+    state, p6, b24, c24 = together(state, p6, b24, c24)
+
+    sent = [
+        b24,
+        jnp.where(bit[1] == 1, p2, c24[:SLOT]),
+        jnp.where(bit[2] == 1, p4, c24[SLOT:]),
+    ]
+    near35 = exchange(jnp.concatenate(sent), 1)
+    b6 = along_x(p6, 1)
+    c6 = along_x(p6, 2)
+    state = attend_more(state, q, own, [near1, b24, c24, p6], [one] * 6 + [bit[2]])
+    state, b6, c6 = together(state, b6, c6)
+
+    near7 = exchange(jnp.concatenate([b6, jnp.where(bit[2] == 1, p6, c6)]), 1)
+    state = attend_more(state, q, own, [near35, b6, c6], [one] * 6)
+    arrays = [p2, p4, b0, c0, near1, b24, c24, p6, near35, b6, c6, near7]
+    ok = [bit[1], bit[2]] + [one] * 8 + [bit[2]] + [one] * 8
+    return attend_last(state, q, own, [near7], [one] * 2, arrays, ok)
 
 
 def solution(mesh):

time: 185 us -> 84 us (0.45)
  the two profiles are of different devices: /device:TPU:4 before, /device:TPU:68 now
where the time goes in v3:
time: 84 us; the launch traced here: 83.3 us
  starting transfers between devices  37.8 us (45%)
  Pallas kernels  18.7 us (22%)
  local copies, waits for them, and re-layouts  11.8 us (14%)
  waiting for transfers between devices  11.1 us (13%)
  other arithmetic  3.45 us (4%)
    ppermute x6, starting transfers between devices, exchange(): return lax.ppermute(v, 'ctx', [(i, i ^ mask) for i in range(NX * NZ)])  27 us
    pallas_call x3, Pallas kernels, attend_more(): pl.pallas_call(functools.partial(more_kernel, counts), out_shape=[SUMS] *...  13.3 us
    unnamed x39, local copies, waits for them, and re-layouts  11.7 us
    ppermute x6, starting transfers between devices, along_x(): lax.ppermute(v, 'ctx', [(i, i + NZ * steps) for i in range((NX - steps) *...  10.8 us
    ppermute x6, waiting for transfers between devices, along_x(): lax.ppermute(v, 'ctx', [(i, i + NZ * steps) for i in range((NX - steps) *...  9.5 us
    pallas_call x1, Pallas kernels, attend_last(): pl.pallas_call(functools.partial(last_kernel, counts, all_counts), out_sh...  4.19 us
  transfers between devices with their start and end apart: 12, of which 4 were waited for; matrix products, arithmetic and copies ran while one was open for 2% of the time, Pallas kernels for 17%

profile of v3, /device:TPU:68, one launch (start us, length us, event | category | flops | bytes accessed | tf_op | source)
XLA Modules:
  0.0 83.3 jit_solution(8785081110107132895)
XLA Ops:
  1.6 1.9 %collective-permute-start = (bf16[528,128]{1,0:T(8,128)(2,1)S(1)}, bf16[528,128]{1,0:T(8,128)(2,1)S(1)}, u32[]{:S(2)}, u32[]{:S(2)}) collective-permute-start(bf16[528,128]{1,0:T(8,128)(2,1)S(1)} %fusion.1.own_ref.refs_2_.refs_3_), channel_id=1, source_target_pairs={{0,32},{16,48},{32,0},{48,16},{64,96},{80,112},{96,64},{112,80},{1... | collective-permute-start | bytes 405512 | tf_op jit(solution)/shard_map/ppermute | solution.py:304
  3.5 9.1 %collective-permute-start.1 = (bf16[528,128]{1,0:T(8,128)(2,1)S(1)}, bf16[528,128]{1,0:T(8,128)(2,1)S(1)}, u32[]{:S(2)}, u32[]{:S(2)}) collective-permute-start(bf16[528,128]{1,0:T(8,128)(2,1)S(1)} %fusion.1.own_ref.refs_2_.refs_3_), channel_id=1, source_target_pairs={{0,64},{16,80},{32,96},{48,112},{64,0},{80,16},{96,32},{112,48},{1... | collective-permute-start | bytes 405512 | tf_op jit(solution)/shard_map/ppermute | solution.py:304
  12.7 1.0 %copy-done = bf16[256,1024]{1,0:T(8,128)(2,1)S(1)} copy-done((bf16[256,1024]{1,0:T(8,128)(2,1)S(1)}, bf16[256,1024]{1,0:T(8,128)(2,1)}, u32[]{:S(2)}) %copy-start) | copy-done | bytes 524312
  13.7 1.2 %attend_own.1 = (f32[2048,128]{1,0:T(8,128)S(1)}, f32[2048,128]{1,0:T(8,128)S(1)}, f32[2048,128]{1,0:T(8,128)S(1)}) custom-call(bf16[256,1024]{1,0:T(8,128)(2,1)S(1)} %copy-done, bf16[528,128]{1,0:T(8,128)(2,1)S(1)} %fusion.1.own_ref.refs_2_.refs_3_), custom_call_target="tpu_custom_call" | custom-call | flops 1 | bytes 1 | tf_op jit(solution)/shard_map/attend_own/pallas_call | solution.py:260
  16.8 3.1 %collective-permute-start.2 = (bf16[528,128]{1,0:T(8,128)(2,1)S(1)}, bf16[528,128]{1,0:T(8,128)(2,1)S(1)}, u32[]{:S(2)}, u32[]{:S(2)}) collective-permute-start(bf16[528,128]{1,0:T(8,128)(2,1)S(1)} %fusion.1.own_ref.refs_2_.refs_3_), channel_id=1, source_target_pairs={{0,128},{16,144},{32,160},{48,176},{64,192},{80,208},{96,224},{112... | collective-permute-start | bytes 405512 | tf_op jit(solution)/shard_map/ppermute | solution.py:308
  19.9 1.3 %collective-permute-start.3 = (bf16[528,128]{1,0:T(8,128)(2,1)S(1)}, bf16[528,128]{1,0:T(8,128)(2,1)S(1)}, u32[]{:S(2)}, u32[]{:S(2)}) collective-permute-start(bf16[528,128]{1,0:T(8,128)(2,1)S(1)} %fusion.1.own_ref.refs_2_.refs_3_), channel_id=1, source_target_pairs={{0,256},{16,272},{32,288},{48,304},{64,320},{80,336},{96,352},{112... | collective-permute-start | bytes 405512 | tf_op jit(solution)/shard_map/ppermute | solution.py:308
  21.4 1.5 %collective-permute-done.1.refs_7_.refs_9_ = bf16[528,128]{1,0:T(8,128)(2,1)S(1)} collective-permute-done((bf16[528,128]{1,0:T(8,128)(2,1)S(1)}, bf16[528,128]{1,0:T(8,128)(2,1)S(1)}, u32[]{:S(2)}, u32[]{:S(2)}) %collective-permute-start.1) | collective-permute-done | bytes 135200 | tf_op jit(solution)/shard_map/ppermute | solution.py:304
  23.8 4.6 %collective-permute-done.3.refs_9_.refs_11_ = bf16[528,128]{1,0:T(8,128)(2,1)S(1)} collective-permute-done((bf16[528,128]{1,0:T(8,128)(2,1)S(1)}, bf16[528,128]{1,0:T(8,128)(2,1)S(1)}, u32[]{:S(2)}, u32[]{:S(2)}) %collective-permute-start.3) | collective-permute-done | bytes 135200 | tf_op jit(solution)/shard_map/ppermute | solution.py:308
  28.4 4.8 %collective-permute-start.4 = (bf16[528,128]{1,0:T(8,128)(2,1)S(1)}, bf16[528,128]{1,0:T(8,128)(2,1)S(1)}, u32[]{:S(2)}, u32[]{:S(2)}) collective-permute-start(bf16[528,128]{1,0:T(8,128)(2,1)S(1)} %collective-permute-done.1.refs_7_.refs_9_), channel_id=1, source_target_pairs={{0,32},{16,48},{32,0},{48,16},{64,96},{80,112},{96,64},{112,80},{1... | collective-permute-start | bytes 405512 | tf_op jit(solution)/shard_map/ppermute | solution.py:304
  33.2 1.9 %collective-permute-start.5 = (bf16[1056,128]{1,0:T(8,128)(2,1)S(1)}, bf16[1056,128]{1,0:T(8,128)(2,1)S(1)}, u32[]{:S(2)}, u32[]{:S(2)}) collective-permute-start(bf16[1056,128]{1,0:T(8,128)(2,1)S(1)} %constant_dynamic-update-slice_fusion), channel_id=1, source_target_pairs={{0,128},{16,144},{32,160},{48,176},{64,192},{80,208},{96,224},{112... | collective-permute-start | bytes 811016 | tf_op jit(solution)/shard_map/ppermute | solution.py:308
  35.1 1.3 %collective-permute-start.6 = (bf16[1056,128]{1,0:T(8,128)(2,1)S(1)}, bf16[1056,128]{1,0:T(8,128)(2,1)S(1)}, u32[]{:S(2)}, u32[]{:S(2)}) collective-permute-start(bf16[1056,128]{1,0:T(8,128)(2,1)S(1)} %constant_dynamic-update-slice_fusion), channel_id=1, source_target_pairs={{0,256},{16,272},{32,288},{48,304},{64,320},{80,336},{96,352},{112... | collective-permute-start | bytes 811016 | tf_op jit(solution)/shard_map/ppermute | solution.py:308
  36.5 3.8 %collective-permute-start.7 = (bf16[1056,128]{1,0:T(8,128)(2,1)S(1)}, bf16[1056,128]{1,0:T(8,128)(2,1)S(1)}, u32[]{:S(2)}, u32[]{:S(2)}) collective-permute-start(bf16[1056,128]{1,0:T(8,128)(2,1)S(1)} %pad_maximum_fusion.1), channel_id=1, source_target_pairs={{0,16},{16,0},{32,48},{48,32},{64,80},{80,64},{96,112},{112,96},{1... | collective-permute-start | bytes 811016 | tf_op jit(solution)/shard_map/ppermute | solution.py:304
  40.4 1.2 %copy-done.12 = f32[2048,128]{1,0:T(8,128)S(1)} copy-done((f32[2048,128]{1,0:T(8,128)S(1)}, f32[2048,128]{1,0:T(8,128)}, u32[]{:S(2)}) %copy-start.12) | copy-done | bytes 1048600
  41.6 2.6 %attend_more.3 = (f32[2048,128]{1,0:T(8,128)S(1)}, f32[2048,128]{1,0:T(8,128)S(1)}) custom-call(s32[4]{0:T(128)S(1)} %pad_add_fusion.refs_0_, bf16[256,1024]{1,0:T(8,128)(2,1)S(1)} %copy-done.1, bf16[528,128]{1,0:T(8,128)(2,1)S(1)} %fusion.1.own_ref.refs_2_.refs_3_, f32[2048,128]{1,0:T(8,128)S(1)} %get-tuple-element.60.refs_3_.refs_4_, ...), custom_call_target="tpu_custom_call" | custom-call | flops 1 | bytes 1 | tf_op jit(solution)/shard_map/attend_more/pallas_call | solution.py:272
  44.3 4.1 %collective-permute-done.5.refs_7_.refs_13_ = bf16[1056,128]{1,0:T(8,128)(2,1)S(1)} collective-permute-done((bf16[1056,128]{1,0:T(8,128)(2,1)S(1)}, bf16[1056,128]{1,0:T(8,128)(2,1)S(1)}, u32[]{:S(2)}, u32[]{:S(2)}) %collective-permute-start.5) | collective-permute-done | bytes 270368 | tf_op jit(solution)/shard_map/ppermute | solution.py:308
  48.4 1.9 %collective-permute-start.8 = (bf16[528,128]{1,0:T(8,128)(2,1)S(1)}, bf16[528,128]{1,0:T(8,128)(2,1)S(1)}, u32[]{:S(2)}, u32[]{:S(2)}) collective-permute-start(bf16[528,128]{1,0:T(8,128)(2,1)S(1)} %collective-permute-done.4.refs_9_.refs_15_), channel_id=1, source_target_pairs={{0,128},{16,144},{32,160},{48,176},{64,192},{80,208},{96,224},{112... | collective-permute-start | bytes 405512 | tf_op jit(solution)/shard_map/ppermute | solution.py:308
  50.3 1.3 %collective-permute-start.9 = (bf16[528,128]{1,0:T(8,128)(2,1)S(1)}, bf16[528,128]{1,0:T(8,128)(2,1)S(1)}, u32[]{:S(2)}, u32[]{:S(2)}) collective-permute-start(bf16[528,128]{1,0:T(8,128)(2,1)S(1)} %collective-permute-done.4.refs_9_.refs_15_), channel_id=1, source_target_pairs={{0,256},{16,272},{32,288},{48,304},{64,320},{80,336},{96,352},{112... | collective-permute-start | bytes 405512 | tf_op jit(solution)/shard_map/ppermute | solution.py:308
  52.5 4.1 %collective-permute-start.10 = (bf16[2112,128]{1,0:T(8,128)(2,1)}, bf16[2112,128]{1,0:T(8,128)(2,1)S(1)}, u32[]{:S(2)}, u32[]{:S(2)}) collective-permute-start(bf16[2112,128]{1,0:T(8,128)(2,1)} %pad_maximum_fusion), channel_id=1, source_target_pairs={{0,16},{16,0},{32,48},{48,32},{64,80},{80,64},{96,112},{112,96},{1... | collective-permute-start | bytes 1622024 | tf_op jit(solution)/shard_map/ppermute | solution.py:304
  56.6 4.6 %attend_more.4 = (f32[2048,128]{1,0:T(8,128)S(1)}, f32[2048,128]{1,0:T(8,128)S(1)}) custom-call(s32[7]{0:T(128)S(1)} %pad_add_fusion.1.refs_0_, bf16[256,1024]{1,0:T(8,128)(2,1)S(1)} %copy-done.1, bf16[528,128]{1,0:T(8,128)(2,1)S(1)} %fusion.1.own_ref.refs_2_.refs_3_, f32[2048,128]{1,0:T(8,128)S(1)} %get-tuple-element.60.refs_3_.refs_4_, ...), custom_call_target="tpu_custom_call" | custom-call | flops 1 | bytes 1 | tf_op jit(solution)/shard_map/attend_more/pallas_call | solution.py:272
  65.2 3.3 %collective-permute-start.11 = (bf16[1056,128]{1,0:T(8,128)(2,1)}, bf16[1056,128]{1,0:T(8,128)(2,1)}, u32[]{:S(2)}, u32[]{:S(2)}) collective-permute-start(bf16[1056,128]{1,0:T(8,128)(2,1)} %pad_maximum_fusion.2), channel_id=1, source_target_pairs={{0,16},{16,0},{32,48},{48,32},{64,80},{80,64},{96,112},{112,96},{1... | collective-permute-start | bytes 811016 | tf_op jit(solution)/shard_map/ppermute | solution.py:304
  70.5 1.2 %copy-done.14 = f32[2048,128]{1,0:T(8,128)S(1)} copy-done((f32[2048,128]{1,0:T(8,128)S(1)}, f32[2048,128]{1,0:T(8,128)}, u32[]{:S(2)}) %copy-start.14) | copy-done | bytes 1048600
  71.7 1.2 %copy-done.16 = f32[2048,128]{1,0:T(8,128)S(1)} copy-done((f32[2048,128]{1,0:T(8,128)S(1)}, f32[2048,128]{1,0:T(8,128)}, u32[]{:S(2)}) %copy-start.16) | copy-done | bytes 1048600
  72.9 6.0 %attend_more.5 = (f32[2048,128]{1,0:T(8,128)S(1)}, f32[2048,128]{1,0:T(8,128)S(1)}) custom-call(s32[6]{0:T(128)S(1)} %broadcast_5_refs_0_.2.refs_0_, bf16[256,1024]{1,0:T(8,128)(2,1)S(1)} %copy-done.1, bf16[528,128]{1,0:T(8,128)(2,1)S(1)} %fusion.1.own_ref.refs_2_.refs_3_, f32[2048,128]{1,0:T(8,128)S(1)} %get-tuple-element.60.refs_3_.refs_4_, ...), custom_call_target="tpu_custom_call" | custom-call | flops 1 | bytes 1 | tf_op jit(solution)/shard_map/attend_more/pallas_call | solution.py:272
  79.0 4.2 %attend_last.1 = bf16[256,1024]{1,0:T(8,128)(2,1)} custom-call(s32[2]{0:T(128)S(1)} %broadcast_7_refs_0_.2.refs_0_, s32[19]{0:T(128)S(1)} %stack.21.refs_1_, bf16[256,1024]{1,0:T(8,128)(2,1)S(1)} %copy-done.1, bf16[528,128]{1,0:T(8,128)(2,1)S(1)} %fusion.1.own_ref.refs_2_.refs_3_, f32[2048,128]{1,0:T(8,128)S(1)} %get-tuple-element.60.refs_3_.refs_4_, ...), custom_call_target="tpu_custom_call" | custom-call | flops 1 | bytes 1 | tf_op jit(solution)/shard_map/attend_last/pallas_call | solution.py:286
  (60 shorter events, 11.4 us)
Async XLA Ops:
  0.0 36.4 %copy-start.17 = (bf16[256,128]{1,0:T(8,128)(2,1)S(1)}, bf16[256,128]{1,0:T(8,128)(2,1)}, u32[]{:S(2)}) copy-start(bf16[256,128]{1,0:T(8,128)(2,1)} %param.6) | copy-start | bytes 196612
  0.0 36.5 %copy-start.18 = (bf16[256,128]{1,0:T(8,128)(2,1)S(1)}, bf16[256,128]{1,0:T(8,128)(2,1)}, u32[]{:S(2)}) copy-start(bf16[256,128]{1,0:T(8,128)(2,1)} %param.5) | copy-start | bytes 196612
  1.6 19.8 %collective-permute-start = (bf16[528,128]{1,0:T(8,128)(2,1)S(1)}, bf16[528,128]{1,0:T(8,128)(2,1)S(1)}, u32[]{:S(2)}, u32[]{:S(2)}) collective-permute-start(bf16[528,128]{1,0:T(8,128)(2,1)S(1)} %fusion.1.own_ref.refs_2_.refs_3_), channel_id=1, source_target_pairs={{0,32},{16,48},{32,0},{48,16},{64,96},{80,112},{96,64},{112,80},{1... | collective-permute-start | bytes 405512 | tf_op jit(solution)/shard_map/ppermute | solution.py:304
  3.5 19.4 %collective-permute-start.1 = (bf16[528,128]{1,0:T(8,128)(2,1)S(1)}, bf16[528,128]{1,0:T(8,128)(2,1)S(1)}, u32[]{:S(2)}, u32[]{:S(2)}) collective-permute-start(bf16[528,128]{1,0:T(8,128)(2,1)S(1)} %fusion.1.own_ref.refs_2_.refs_3_), channel_id=1, source_target_pairs={{0,64},{16,80},{32,96},{48,112},{64,0},{80,16},{96,32},{112,48},{1... | collective-permute-start | bytes 405512 | tf_op jit(solution)/shard_map/ppermute | solution.py:304
  12.6 1.0 %copy-start = (bf16[256,1024]{1,0:T(8,128)(2,1)S(1)}, bf16[256,1024]{1,0:T(8,128)(2,1)}, u32[]{:S(2)}) copy-start(bf16[256,1024]{1,0:T(8,128)(2,1)} %refs_2_.1) | copy-start | bytes 1572868
  13.7 26.7 %copy-start.1 = (bf16[256,1024]{1,0:T(8,128)(2,1)S(1)}, bf16[256,1024]{1,0:T(8,128)(2,1)}, u32[]{:S(2)}) copy-start(bf16[256,1024]{1,0:T(8,128)(2,1)} %refs_2_.1) | copy-start | bytes 1572868
  14.9 1.0 %copy-start.9 = (f32[2048,128]{1,0:T(8,128)}, f32[2048,128]{1,0:T(8,128)S(1)}, u32[]{:S(2)}) copy-start(f32[2048,128]{1,0:T(8,128)S(1)} %get-tuple-element.44.refs_4_) | copy-start | bytes 3145732
  16.8 6.9 %collective-permute-start.2 = (bf16[528,128]{1,0:T(8,128)(2,1)S(1)}, bf16[528,128]{1,0:T(8,128)(2,1)S(1)}, u32[]{:S(2)}, u32[]{:S(2)}) collective-permute-start(bf16[528,128]{1,0:T(8,128)(2,1)S(1)} %fusion.1.own_ref.refs_2_.refs_3_), channel_id=1, source_target_pairs={{0,128},{16,144},{32,160},{48,176},{64,192},{80,208},{96,224},{112... | collective-permute-start | bytes 405512 | tf_op jit(solution)/shard_map/ppermute | solution.py:308
  19.9 8.4 %collective-permute-start.3 = (bf16[528,128]{1,0:T(8,128)(2,1)S(1)}, bf16[528,128]{1,0:T(8,128)(2,1)S(1)}, u32[]{:S(2)}, u32[]{:S(2)}) collective-permute-start(bf16[528,128]{1,0:T(8,128)(2,1)S(1)} %fusion.1.own_ref.refs_2_.refs_3_), channel_id=1, source_target_pairs={{0,256},{16,272},{32,288},{48,304},{64,320},{80,336},{96,352},{112... | collective-permute-start | bytes 405512 | tf_op jit(solution)/shard_map/ppermute | solution.py:308
  21.3 19.0 %copy-start.10 = (f32[2048,128]{1,0:T(8,128)S(1)}, f32[2048,128]{1,0:T(8,128)}, u32[]{:S(2)}) copy-start(f32[2048,128]{1,0:T(8,128)} %copy-done.9) | copy-start | bytes 3145732
  28.4 15.9 %collective-permute-start.4 = (bf16[528,128]{1,0:T(8,128)(2,1)S(1)}, bf16[528,128]{1,0:T(8,128)(2,1)S(1)}, u32[]{:S(2)}, u32[]{:S(2)}) collective-permute-start(bf16[528,128]{1,0:T(8,128)(2,1)S(1)} %collective-permute-done.1.refs_7_.refs_9_), channel_id=1, source_target_pairs={{0,32},{16,48},{32,0},{48,16},{64,96},{80,112},{96,64},{112,80},{1... | collective-permute-start | bytes 405512 | tf_op jit(solution)/shard_map/ppermute | solution.py:304
  33.2 15.2 %collective-permute-start.5 = (bf16[1056,128]{1,0:T(8,128)(2,1)S(1)}, bf16[1056,128]{1,0:T(8,128)(2,1)S(1)}, u32[]{:S(2)}, u32[]{:S(2)}) collective-permute-start(bf16[1056,128]{1,0:T(8,128)(2,1)S(1)} %constant_dynamic-update-slice_fusion), channel_id=1, source_target_pairs={{0,128},{16,144},{32,160},{48,176},{64,192},{80,208},{96,224},{112... | collective-permute-start | bytes 811016 | tf_op jit(solution)/shard_map/ppermute | solution.py:308
  35.1 13.3 %collective-permute-start.6 = (bf16[1056,128]{1,0:T(8,128)(2,1)S(1)}, bf16[1056,128]{1,0:T(8,128)(2,1)S(1)}, u32[]{:S(2)}, u32[]{:S(2)}) collective-permute-start(bf16[1056,128]{1,0:T(8,128)(2,1)S(1)} %constant_dynamic-update-slice_fusion), channel_id=1, source_target_pairs={{0,256},{16,272},{32,288},{48,304},{64,320},{80,336},{96,352},{112... | collective-permute-start | bytes 811016 | tf_op jit(solution)/shard_map/ppermute | solution.py:308
  36.5 20.0 %collective-permute-start.7 = (bf16[1056,128]{1,0:T(8,128)(2,1)S(1)}, bf16[1056,128]{1,0:T(8,128)(2,1)S(1)}, u32[]{:S(2)}, u32[]{:S(2)}) collective-permute-start(bf16[1056,128]{1,0:T(8,128)(2,1)S(1)} %pad_maximum_fusion.1), channel_id=1, source_target_pairs={{0,16},{16,0},{32,48},{48,32},{64,80},{80,64},{96,112},{112,96},{1... | collective-permute-start | bytes 811016 | tf_op jit(solution)/shard_map/ppermute | solution.py:304
  40.4 1.2 %copy-start.12 = (f32[2048,128]{1,0:T(8,128)S(1)}, f32[2048,128]{1,0:T(8,128)}, u32[]{:S(2)}) copy-start(f32[2048,128]{1,0:T(8,128)} %copy-done.11) | copy-start | bytes 3145732
  48.4 14.8 %collective-permute-start.8 = (bf16[528,128]{1,0:T(8,128)(2,1)S(1)}, bf16[528,128]{1,0:T(8,128)(2,1)S(1)}, u32[]{:S(2)}, u32[]{:S(2)}) collective-permute-start(bf16[528,128]{1,0:T(8,128)(2,1)S(1)} %collective-permute-done.4.refs_9_.refs_15_), channel_id=1, source_target_pairs={{0,128},{16,144},{32,160},{48,176},{64,192},{80,208},{96,224},{112... | collective-permute-start | bytes 405512 | tf_op jit(solution)/shard_map/ppermute | solution.py:308
  50.3 12.9 %collective-permute-start.9 = (bf16[528,128]{1,0:T(8,128)(2,1)S(1)}, bf16[528,128]{1,0:T(8,128)(2,1)S(1)}, u32[]{:S(2)}, u32[]{:S(2)}) collective-permute-start(bf16[528,128]{1,0:T(8,128)(2,1)S(1)} %collective-permute-done.4.refs_9_.refs_15_), channel_id=1, source_target_pairs={{0,256},{16,272},{32,288},{48,304},{64,320},{80,336},{96,352},{112... | collective-permute-start | bytes 405512 | tf_op jit(solution)/shard_map/ppermute | solution.py:308
  52.5 16.1 %collective-permute-start.10 = (bf16[2112,128]{1,0:T(8,128)(2,1)}, bf16[2112,128]{1,0:T(8,128)(2,1)S(1)}, u32[]{:S(2)}, u32[]{:S(2)}) collective-permute-start(bf16[2112,128]{1,0:T(8,128)(2,1)} %pad_maximum_fusion), channel_id=1, source_target_pairs={{0,16},{16,0},{32,48},{48,32},{64,80},{80,64},{96,112},{112,96},{1... | collective-permute-start | bytes 1622024 | tf_op jit(solution)/shard_map/ppermute | solution.py:304
  56.6 4.6 %copy-start.7 = (bf16[1056,128]{1,0:T(8,128)(2,1)}, bf16[1056,128]{1,0:T(8,128)(2,1)S(1)}, u32[]{:S(2)}) copy-start(bf16[1056,128]{1,0:T(8,128)(2,1)S(1)} %collective-permute-done.7.refs_6_.refs_12_) | copy-start | bytes 811012
  65.2 13.7 %collective-permute-start.11 = (bf16[1056,128]{1,0:T(8,128)(2,1)}, bf16[1056,128]{1,0:T(8,128)(2,1)}, u32[]{:S(2)}, u32[]{:S(2)}) collective-permute-start(bf16[1056,128]{1,0:T(8,128)(2,1)} %pad_maximum_fusion.2), channel_id=1, source_target_pairs={{0,16},{16,0},{32,48},{48,32},{64,80},{80,64},{96,112},{112,96},{1... | collective-permute-start | bytes 811016 | tf_op jit(solution)/shard_map/ppermute | solution.py:304
  70.5 1.2 %copy-start.14 = (f32[2048,128]{1,0:T(8,128)S(1)}, f32[2048,128]{1,0:T(8,128)}, u32[]{:S(2)}) copy-start(f32[2048,128]{1,0:T(8,128)} %copy-done.13) | copy-start | bytes 3145732
  71.7 1.2 %copy-start.16 = (f32[2048,128]{1,0:T(8,128)S(1)}, f32[2048,128]{1,0:T(8,128)}, u32[]{:S(2)}) copy-start(f32[2048,128]{1,0:T(8,128)} %copy-done.15) | copy-start | bytes 3145732
  72.9 6.1 %copy-start.6 = (bf16[528,128]{1,0:T(8,128)(2,1)S(1)}, bf16[528,128]{1,0:T(8,128)(2,1)}, u32[]{:S(2)}) copy-start(bf16[528,128]{1,0:T(8,128)(2,1)} %copy-done.4) | copy-start | bytes 405508
  72.9 6.1 %copy-start.8 = (bf16[1056,128]{1,0:T(8,128)(2,1)S(1)}, bf16[1056,128]{1,0:T(8,128)(2,1)}, u32[]{:S(2)}) copy-start(bf16[1056,128]{1,0:T(8,128)(2,1)} %copy-done.7) | copy-start | bytes 811012
  (7 other events, 6.0 us)

commit v4 on v3

--- a/solution.py
+++ b/solution.py
@@ -19,6 +19,7 @@
 NEGATIVE = -1e30
 FACTOR = HEAD**-0.5 * math.log2(math.e)
 HIGH = 2.0**100
+VMEM_MIB = 16
 
 
 def contract_last(a, b):
@@ -44,7 +45,7 @@
     return visible, in_first
 
 
-def own_kernel(q_ref, own_ref, shift_ref, l_ref, acc_ref):
+def add_own(q_ref, own_ref, shift_ref, l_ref, acc_ref):
     visible, in_first = own_masks(own_ref)
     keys = own_ref[:BLOCK, :]
     values = own_ref[BLOCK : 2 * BLOCK, :]
@@ -68,7 +69,7 @@
     return jnp.sum(jnp.where(ids == first_id, 1.0, 0.0)).astype(jnp.int32)
 
 
-def add_blocks(slots, counts, ok_ref, q_ref, own_ref, shift_ref, l_ref, acc_ref, k_buf, v_buf, part):
+def gather(slots, counts, ok_ref, own_ref, k_buf, v_buf, part):
     first_id = own_ref[2 * BLOCK :, :].astype(jnp.float32)[0:1, 0:1]
     full = jnp.int32(0)
     partial = jnp.int32(0)
@@ -92,7 +93,10 @@
 
             full = full + whole.astype(jnp.int32)
             partial = partial + jnp.where(whole, 0, seen)
-
+    return full, partial
+
+
+def add_blocks(full, partial, q_ref, shift_ref, l_ref, acc_ref, k_buf, v_buf, part):
     def attend(chunk, limit):
         at = pl.ds(pl.multiple_of(chunk * WIDE, WIDE), WIDE)
         keys, values = k_buf[at, :], v_buf[at, :]
@@ -142,34 +146,69 @@
         attend(pairs, jnp.where(shown, 0.0, NEGATIVE))
 
 
+def copies(pairs, sems):
+    return [pltpu.make_async_copy(a, b, sems.at[i]) for i, (a, b) in enumerate(pairs)]
+
+
+def run(moves):
+    for move in moves:
+        move.start()
+    for move in moves:
+        move.wait()
+
+
+def first_kernel(counts, *refs):
+    n = len(counts)
+    ok_ref, q_hbm, own_ref = refs[:3]
+    slots = refs[3 : 3 + n]
+    shift_out, l_out, acc_out, q, shift, l_sum, acc_sum, k_buf, v_buf, part, sems = refs[3 + n :]
+    fetch, *keep = copies(
+        [(q_hbm, q), (shift, shift_out), (l_sum, l_out), (acc_sum, acc_out)], sems
+    )
+    fetch.start()
+    full, partial = gather(slots, counts, ok_ref, own_ref, k_buf, v_buf, part)
+    fetch.wait()
+    add_own(q, own_ref, shift, l_sum, acc_sum)
+    keep[0].start()
+    add_blocks(full, partial, q, shift, l_sum, acc_sum, k_buf, v_buf, part)
+    keep[1].start()
+    keep[2].start()
+    for move in keep:
+        move.wait()
+
+
 def more_kernel(counts, *refs):
     n = len(counts)
-    ok_ref, q_ref, own_ref, shift_ref, l_in, acc_in = refs[:6]
+    ok_ref, q_hbm, own_ref, shift_in, l_in, acc_in = refs[:6]
     slots = refs[6 : 6 + n]
-    l_ref, acc_ref, k_buf, v_buf, part = refs[6 + n :]
-    l_ref[...] = l_in[...]
-    acc_ref[...] = acc_in[...]
-    add_blocks(
-        slots, counts, ok_ref, q_ref, own_ref, shift_ref, l_ref, acc_ref, k_buf, v_buf, part
-    )
+    l_out, acc_out, q, shift, l_sum, acc_sum, k_buf, v_buf, part, sems = refs[6 + n :]
+    full, partial = gather(slots, counts, ok_ref, own_ref, k_buf, v_buf, part)
+
+    @pl.when((full > 0) | (partial > 0))
+    def _():
+        run(copies([(q_hbm, q), (shift_in, shift), (l_in, l_sum), (acc_in, acc_sum)], sems))
+        add_blocks(full, partial, q, shift, l_sum, acc_sum, k_buf, v_buf, part)
+        run(copies([(l_sum, l_out), (acc_sum, acc_out)], sems))
 
 
 def last_kernel(counts, all_counts, *refs):
     n, m = len(counts), len(all_counts)
-    ok_ref, all_ok_ref, q_ref, own_ref, shift_ref, l_in, acc_in = refs[:7]
+    ok_ref, all_ok_ref, q_hbm, own_ref, shift_in, l_in, acc_in = refs[:7]
     slots, everything = refs[7 : 7 + n], refs[7 + n : 7 + n + m]
-    out_ref, l_ref, acc_ref, k_buf, v_buf, part, store, top, sem = refs[7 + n + m :]
-    l_ref[...] = l_in[...]
-    acc_ref[...] = acc_in[...]
-    add_blocks(
-        slots, counts, ok_ref, q_ref, own_ref, shift_ref, l_ref, acc_ref, k_buf, v_buf, part
-    )
+    out_ref, q, shift, l_sum, acc_sum, k_buf, v_buf, part, sems, store, top = refs[7 + n + m :]
+    moves = copies([(q_hbm, q), (shift_in, shift), (l_in, l_sum), (acc_in, acc_sum)], sems)
+    for move in moves:
+        move.start()
+    full, partial = gather(slots, counts, ok_ref, own_ref, k_buf, v_buf, part)
+    for move in moves:
+        move.wait()
+    add_blocks(full, partial, q, shift, l_sum, acc_sum, k_buf, v_buf, part)
     most = jnp.zeros((BLOCK, 1), jnp.float32)
     for h in range(HEADS):
         rows = pl.ds(h * BLOCK, BLOCK)
-        total = jnp.sum(l_ref[rows, :], axis=1, keepdims=True)
+        total = jnp.sum(l_sum[rows, :], axis=1, keepdims=True)
         most = jnp.where(total <= HIGH, most, 1.0)
-        out_ref[:, h * HEAD : (h + 1) * HEAD] = (acc_ref[rows, :] * (1.0 / total)).astype(
+        out_ref[:, h * HEAD : (h + 1) * HEAD] = (acc_sum[rows, :] * (1.0 / total)).astype(
             jnp.bfloat16
         )
 
@@ -178,13 +217,9 @@
         at = 0
         for ref, count in zip(everything, all_counts):
             for k in range(count):
-                copy = pltpu.make_async_copy(
-                    ref.at[k * SLOT : (k + 1) * SLOT, :], store.at[at], sem
-                )
-                copy.start()
-                copy.wait()
+                run(copies([(ref.at[k * SLOT : (k + 1) * SLOT, :], store.at[at])], sems))
                 at += 1
-        with_maximum(at, all_ok_ref, q_ref, own_ref, store, top, l_ref, acc_ref, out_ref)
+        with_maximum(at, all_ok_ref, q, own_ref, store, top, l_sum, acc_sum, out_ref)
 
 
 def with_maximum(count, ok_ref, q_ref, own_ref, store, top, l_sum, acc_sum, out_ref):
@@ -239,6 +274,7 @@
 
 VMEM = pl.BlockSpec(memory_space=pltpu.VMEM)
 SMEM = pl.BlockSpec(memory_space=pltpu.SMEM)
+HBM = pl.BlockSpec(memory_space=pltpu.HBM)
 SUMS = jax.ShapeDtypeStruct((HEADS * BLOCK, HEAD), jnp.float32)
 COST = pl.CostEstimate(flops=1, bytes_accessed=1, transcendentals=0)
 
@@ -250,33 +286,48 @@
 def buffers(blocks):
     rows = (blocks + blocks % 2 + 2) * BLOCK
     return [
+        pltpu.VMEM((BLOCK, HEADS * HEAD), jnp.bfloat16),
+        pltpu.VMEM(SUMS.shape, jnp.float32),
+        pltpu.VMEM(SUMS.shape, jnp.float32),
+        pltpu.VMEM(SUMS.shape, jnp.float32),
         pltpu.VMEM((rows, HEAD), jnp.bfloat16),
         pltpu.VMEM((rows, HEAD), jnp.bfloat16),
         pltpu.VMEM((2 * BLOCK, HEAD), jnp.bfloat16),
+        pltpu.SemaphoreType.DMA((4,)),
     ]
 
 
-def attend_own(q, own):
-    return pl.pallas_call(
-        own_kernel, out_shape=[SUMS] * 3, in_specs=[VMEM] * 2, out_specs=[VMEM] * 3,
-        compiler_params=params(12), cost_estimate=COST, name="attend_own",
-    )(q, own)
+def in_hbm(*arrays):
+    return [pltpu.with_memory_space_constraint(a, pltpu.HBM) for a in arrays]
 
 
 def stack_ok(ok):
     return jnp.stack([jnp.asarray(o, jnp.int32) for o in ok])
+
+
+def attend_first(q, own, arrays, ok):
+    counts = [a.shape[0] // SLOT for a in arrays]
+    return pl.pallas_call(
+        functools.partial(first_kernel, counts),
+        out_shape=[pltpu.HBM(SUMS.shape, SUMS.dtype)] * 3,
+        in_specs=[SMEM, HBM, VMEM] + [VMEM] * len(arrays),
+        out_specs=[HBM] * 3,
+        scratch_shapes=buffers(sum(counts)),
+        compiler_params=params(VMEM_MIB), cost_estimate=COST, name="attend_first",
+    )(stack_ok(ok), *in_hbm(q), own, *arrays)
 
 
 def attend_more(state, q, own, arrays, ok):
     counts = [a.shape[0] // SLOT for a in arrays]
     sums = pl.pallas_call(
         functools.partial(more_kernel, counts),
-        out_shape=[SUMS] * 2,
-        in_specs=[SMEM] + [VMEM] * (5 + len(arrays)),
-        out_specs=[VMEM] * 2,
+        out_shape=[pltpu.HBM(SUMS.shape, SUMS.dtype)] * 2,
+        in_specs=[SMEM, HBM, VMEM] + [HBM] * 3 + [VMEM] * len(arrays),
+        out_specs=[HBM] * 2,
         scratch_shapes=buffers(sum(counts)),
-        compiler_params=params(12), cost_estimate=COST, name="attend_more",
-    )(stack_ok(ok), q, own, *state, *arrays)
+        input_output_aliases={4: 0, 5: 1},
+        compiler_params=params(VMEM_MIB), cost_estimate=COST, name="attend_more",
+    )(stack_ok(ok), *in_hbm(q), own, *in_hbm(*state), *arrays)
     return state[0], *sums
 
 
@@ -286,18 +337,18 @@
     return pl.pallas_call(
         functools.partial(last_kernel, counts, all_counts),
         out_shape=jax.ShapeDtypeStruct((BLOCK, HEADS * HEAD), jnp.bfloat16),
-        in_specs=[SMEM] * 2 + [VMEM] * (5 + len(arrays))
+        in_specs=[SMEM] * 2 + [HBM, VMEM] + [HBM] * 3 + [VMEM] * len(arrays)
         + [pl.BlockSpec(memory_space=pl.ANY)] * len(everything),
         out_specs=VMEM,
-        scratch_shapes=[pltpu.VMEM(SUMS.shape, jnp.float32)] * 2
-        + buffers(sum(counts))
+        scratch_shapes=buffers(sum(counts))
         + [
             pltpu.VMEM((sum(all_counts), SLOT, HEAD), jnp.bfloat16),
             pltpu.VMEM((BLOCK, HEAD), jnp.float32),
-            pltpu.SemaphoreType.DMA,
         ],
-        compiler_params=params(16), cost_estimate=COST, name="attend_last",
-    )(stack_ok(ok), stack_ok(all_ok), q, own, *state, *arrays, *everything)
+        compiler_params=params(VMEM_MIB), cost_estimate=COST, name="attend_last",
+    )(
+        stack_ok(ok), stack_ok(all_ok), *in_hbm(q), own, *in_hbm(*state), *arrays, *everything
+    )
 
 
 def exchange(v, mask):
@@ -321,20 +372,18 @@
     own = jnp.concatenate([keys, values, ids], axis=0)
     q = queries
 
+    b0 = along_x(own, 1)
+    c0 = along_x(own, 2)
+    p2 = exchange(own, 2)
     p4 = exchange(own, 4)
-    p2 = exchange(own, 2)
-    state = attend_own(q, own)
-    state, out = together(state, own)
-    b0 = along_x(out, 1)
-    c0 = along_x(out, 2)
-    state, p2, p4, b0, c0 = together(state, p2, p4, b0, c0)
+    p4, p2, b0, c0 = together(p4, p2, b0, c0)
 
     near1 = exchange(jnp.concatenate([b0, jnp.where(bit[0] == 0, own, c0)]), 1)
     pair = jnp.concatenate([p2, p4])
     b24 = along_x(pair, 1)
     c24 = along_x(pair, 2)
     p6 = exchange(p4, 2)
-    state = attend_more(state, q, own, [p2, p4, b0, c0], [bit[1], bit[2], one, one])
+    state = attend_first(q, own, [p4, p2, b0, c0], [bit[2], bit[1], one, one])
     state, p6, b24, c24 = together(state, p6, b24, c24)
 
     sent = [
@@ -345,11 +394,12 @@
     near35 = exchange(jnp.concatenate(sent), 1)
     b6 = along_x(p6, 1)
     c6 = along_x(p6, 2)
-    state = attend_more(state, q, own, [near1, b24, c24, p6], [one] * 6 + [bit[2]])
-    state, b6, c6 = together(state, b6, c6)
+    b6, c6 = together(b6, c6)
 
     near7 = exchange(jnp.concatenate([b6, jnp.where(bit[2] == 1, p6, c6)]), 1)
-    state = attend_more(state, q, own, [near35, b6, c6], [one] * 6)
+    state = attend_more(
+        state, q, own, [near1, b24, c24, p6, b6, c6, near35], [one] * 6 + [bit[2]] + [one] * 6
+    )
     arrays = [p2, p4, b0, c0, near1, b24, c24, p6, near35, b6, c6, near7]
     ok = [bit[1], bit[2]] + [one] * 8 + [bit[2]] + [one] * 8
     return attend_last(state, q, own, [near7], [one] * 2, arrays, ok)

time: 84 us -> 82.2 us (0.979)
  the two profiles are of different devices: /device:TPU:68 before, /device:TPU:28 now
where the time goes in v4:
time: 82.2 us; the launch traced here: 81.6 us
  starting transfers between devices  38.5 us (47%)
  Pallas kernels  23.3 us (28%)
  waiting for transfers between devices  16 us (19%)
  other arithmetic  3.41 us (4%)
    ppermute x6, starting transfers between devices, exchange(): return lax.ppermute(v, 'ctx', [(i, i ^ mask) for i in range(NX * NZ)])  27.7 us
    pallas_call x1, Pallas kernels, attend_more(): pl.pallas_call(functools.partial(more_kernel, counts), out_shape=[pltpu.H...  12.6 us
    ppermute x6, starting transfers between devices, along_x(): lax.ppermute(v, 'ctx', [(i, i + NZ * steps) for i in range((NX - steps) *...  10.8 us
    ppermute x6, waiting for transfers between devices, exchange(): return lax.ppermute(v, 'ctx', [(i, i ^ mask) for i in range(NX * NZ)])  8.6 us
    ppermute x6, waiting for transfers between devices, along_x(): lax.ppermute(v, 'ctx', [(i, i + NZ * steps) for i in range((NX - steps) *...  7.41 us
    pallas_call x1, Pallas kernels, attend_first(): pl.pallas_call(functools.partial(first_kernel, counts), out_shape=[pltpu....  5.63 us
    pallas_call x1, Pallas kernels, attend_last(): pl.pallas_call(functools.partial(last_kernel, counts, all_counts), out_sh...  5.14 us
  transfers between devices with their start and end apart: 12, of which 7 were waited for; matrix products, arithmetic and copies ran while one was open for 3% of the time, Pallas kernels for 22%

profile of v4, /device:TPU:28, one launch (start us, length us, event | category | flops | bytes accessed | tf_op | source)
XLA Modules:
  0.0 81.6 jit_solution(12091736574472117597)
XLA Ops:
  0.7 0.9 %fusion.1.refs_2_.refs_3_ = bf16[528,128]{1,0:T(8,128)(2,1)S(1)} fusion(bf16[2,128]{1,0:T(2,128)(2,1)S(1)} %fusion.2, bf16[256,128]{1,0:T(8,128)(2,1)} %param.6, bf16[256,128]{1,0:T(8,128)(2,1)} %param.5), kind=kLoop, calls=%fused_computation.5 | loop fusion | flops 540672 | bytes 266752 | tf_op jit(solution)/shard_map/concatenate | solution.py:372
  1.6 9.1 %collective-permute-start = (bf16[528,128]{1,0:T(8,128)(2,1)S(1)}, bf16[528,128]{1,0:T(8,128)(2,1)S(1)}, u32[]{:S(2)}, u32[]{:S(2)}) collective-permute-start(bf16[528,128]{1,0:T(8,128)(2,1)S(1)} %fusion.1.refs_2_.refs_3_), channel_id=1, source_target_pairs={{0,64},{16,80},{32,96},{48,112},{64,0},{80,16},{96,32},{112,48},{1... | collective-permute-start | bytes 405512 | tf_op jit(solution)/shard_map/ppermute | solution.py:355
  10.7 5.2 %collective-permute-start.1 = (bf16[528,128]{1,0:T(8,128)(2,1)S(1)}, bf16[528,128]{1,0:T(8,128)(2,1)S(1)}, u32[]{:S(2)}, u32[]{:S(2)}) collective-permute-start(bf16[528,128]{1,0:T(8,128)(2,1)S(1)} %fusion.1.refs_2_.refs_3_), channel_id=1, source_target_pairs={{0,32},{16,48},{32,0},{48,16},{64,96},{80,112},{96,64},{112,80},{1... | collective-permute-start | bytes 405512 | tf_op jit(solution)/shard_map/ppermute | solution.py:355
  15.9 3.1 %collective-permute-start.2 = (bf16[528,128]{1,0:T(8,128)(2,1)S(1)}, bf16[528,128]{1,0:T(8,128)(2,1)S(1)}, u32[]{:S(2)}, u32[]{:S(2)}) collective-permute-start(bf16[528,128]{1,0:T(8,128)(2,1)S(1)} %fusion.1.refs_2_.refs_3_), channel_id=1, source_target_pairs={{0,128},{16,144},{32,160},{48,176},{64,192},{80,208},{96,224},{112... | collective-permute-start | bytes 405512 | tf_op jit(solution)/shard_map/ppermute | solution.py:359
  19.0 1.3 %collective-permute-start.3 = (bf16[528,128]{1,0:T(8,128)(2,1)S(1)}, bf16[528,128]{1,0:T(8,128)(2,1)S(1)}, u32[]{:S(2)}, u32[]{:S(2)}) collective-permute-start(bf16[528,128]{1,0:T(8,128)(2,1)S(1)} %fusion.1.refs_2_.refs_3_), channel_id=1, source_target_pairs={{0,256},{16,272},{32,288},{48,304},{64,320},{80,336},{96,352},{112... | collective-permute-start | bytes 405512 | tf_op jit(solution)/shard_map/ppermute | solution.py:359
  20.4 1.9 %collective-permute-done.refs_3_.refs_9_ = bf16[528,128]{1,0:T(8,128)(2,1)S(1)} collective-permute-done((bf16[528,128]{1,0:T(8,128)(2,1)S(1)}, bf16[528,128]{1,0:T(8,128)(2,1)S(1)}, u32[]{:S(2)}, u32[]{:S(2)}) %collective-permute-start) | collective-permute-done | bytes 135200 | tf_op jit(solution)/shard_map/ppermute | solution.py:355
  22.2 1.4 %collective-permute-done.1.refs_4_.refs_8_ = bf16[528,128]{1,0:T(8,128)(2,1)S(1)} collective-permute-done((bf16[528,128]{1,0:T(8,128)(2,1)S(1)}, bf16[528,128]{1,0:T(8,128)(2,1)S(1)}, u32[]{:S(2)}, u32[]{:S(2)}) %collective-permute-start.1) | collective-permute-done | bytes 135200 | tf_op jit(solution)/shard_map/ppermute | solution.py:355
  23.6 3.7 %collective-permute-done.3.refs_6_.refs_11_ = bf16[528,128]{1,0:T(8,128)(2,1)S(1)} collective-permute-done((bf16[528,128]{1,0:T(8,128)(2,1)S(1)}, bf16[528,128]{1,0:T(8,128)(2,1)S(1)}, u32[]{:S(2)}, u32[]{:S(2)}) %collective-permute-start.3) | collective-permute-done | bytes 135200 | tf_op jit(solution)/shard_map/ppermute | solution.py:359
  27.4 1.9 %collective-permute-start.4 = (bf16[528,128]{1,0:T(8,128)(2,1)S(1)}, bf16[528,128]{1,0:T(8,128)(2,1)S(1)}, u32[]{:S(2)}, u32[]{:S(2)}) collective-permute-start(bf16[528,128]{1,0:T(8,128)(2,1)S(1)} %collective-permute-done.refs_3_.refs_9_), channel_id=1, source_target_pairs={{0,32},{16,48},{32,0},{48,16},{64,96},{80,112},{96,64},{112,80},{1... | collective-permute-start | bytes 405512 | tf_op jit(solution)/shard_map/ppermute | solution.py:355
  29.3 1.9 %collective-permute-start.5 = (bf16[1056,128]{1,0:T(8,128)(2,1)S(1)}, bf16[1056,128]{1,0:T(8,128)(2,1)S(1)}, u32[]{:S(2)}, u32[]{:S(2)}) collective-permute-start(bf16[1056,128]{1,0:T(8,128)(2,1)S(1)} %constant_dynamic-update-slice_fusion), channel_id=1, source_target_pairs={{0,128},{16,144},{32,160},{48,176},{64,192},{80,208},{96,224},{112... | collective-permute-start | bytes 811016 | tf_op jit(solution)/shard_map/ppermute | solution.py:359
  31.3 1.3 %collective-permute-start.6 = (bf16[1056,128]{1,0:T(8,128)(2,1)S(1)}, bf16[1056,128]{1,0:T(8,128)(2,1)S(1)}, u32[]{:S(2)}, u32[]{:S(2)}) collective-permute-start(bf16[1056,128]{1,0:T(8,128)(2,1)S(1)} %constant_dynamic-update-slice_fusion), channel_id=1, source_target_pairs={{0,256},{16,272},{32,288},{48,304},{64,320},{80,336},{96,352},{112... | collective-permute-start | bytes 811016 | tf_op jit(solution)/shard_map/ppermute | solution.py:359
  32.6 0.9 %broadcast_select_fusion.1 = bf16[528,128]{1,0:T(8,128)(2,1)S(1)} fusion(bf16[528,128]{1,0:T(8,128)(2,1)S(1)} %collective-permute-done.3.refs_6_.refs_11_, pred[]{:T(512)S(6)} %eq.12, bf16[2,128]{1,0:T(2,128)(2,1)S(1)} %fusion.2, bf16[256,128]{1,0:T(8,128)(2,1)} %param.6, bf16[256,128]{1,0:T(8,128)(2,1)} %param.5), kind=kLoop, calls=%fused_computation.9 | loop fusion | flops 608256 | bytes 401921 | tf_op jit(solution)/shard_map/jit(_where)/select_n | solution.py:381
  33.5 3.8 %collective-permute-start.7 = (bf16[1056,128]{1,0:T(8,128)(2,1)S(1)}, bf16[1056,128]{1,0:T(8,128)(2,1)S(1)}, u32[]{:S(2)}, u32[]{:S(2)}) collective-permute-start(bf16[1056,128]{1,0:T(8,128)(2,1)S(1)} %pad_maximum_fusion.1), channel_id=1, source_target_pairs={{0,16},{16,0},{32,48},{48,32},{64,80},{80,64},{96,112},{112,96},{1... | collective-permute-start | bytes 811016 | tf_op jit(solution)/shard_map/ppermute | solution.py:355
  37.4 5.6 %attend_first.1 = (f32[2048,128]{1,0:T(8,128)}, f32[2048,128]{1,0:T(8,128)}, f32[2048,128]{1,0:T(8,128)}) custom-call(s32[4]{0:T(128)S(1)} %pad_add_fusion.refs_0_, bf16[256,1024]{1,0:T(8,128)(2,1)} %refs_2_.1, bf16[528,128]{1,0:T(8,128)(2,1)S(1)} %fusion.1.refs_2_.refs_3_, bf16[528,128]{1,0:T(8,128)(2,1)S(1)} %collective-permute-done.refs_3_.refs_9_, ...), custom_call_target="tpu_custom_call" | custom-call | flops 1 | bytes 1 | tf_op jit(solution)/shard_map/attend_first/pallas_call | solution.py:310
  43.5 1.9 %collective-permute-start.8 = (bf16[528,128]{1,0:T(8,128)(2,1)S(1)}, bf16[528,128]{1,0:T(8,128)(2,1)S(1)}, u32[]{:S(2)}, u32[]{:S(2)}) collective-permute-start(bf16[528,128]{1,0:T(8,128)(2,1)S(1)} %collective-permute-done.4.refs_9_.refs_15_), channel_id=1, source_target_pairs={{0,128},{16,144},{32,160},{48,176},{64,192},{80,208},{96,224},{112... | collective-permute-start | bytes 405512 | tf_op jit(solution)/shard_map/ppermute | solution.py:359
  45.4 1.3 %collective-permute-start.9 = (bf16[528,128]{1,0:T(8,128)(2,1)S(1)}, bf16[528,128]{1,0:T(8,128)(2,1)S(1)}, u32[]{:S(2)}, u32[]{:S(2)}) collective-permute-start(bf16[528,128]{1,0:T(8,128)(2,1)S(1)} %collective-permute-done.4.refs_9_.refs_15_), channel_id=1, source_target_pairs={{0,256},{16,272},{32,288},{48,304},{64,320},{80,336},{96,352},{112... | collective-permute-start | bytes 405512 | tf_op jit(solution)/shard_map/ppermute | solution.py:359
  46.8 3.8 %collective-permute-start.10 = (bf16[2112,128]{1,0:T(8,128)(2,1)S(1)}, bf16[2112,128]{1,0:T(8,128)(2,1)S(1)}, u32[]{:S(2)}, u32[]{:S(2)}) collective-permute-start(bf16[2112,128]{1,0:T(8,128)(2,1)S(1)} %pad_maximum_fusion), channel_id=1, source_target_pairs={{0,16},{16,0},{32,48},{48,32},{64,80},{80,64},{96,112},{112,96},{1... | collective-permute-start | bytes 1622024 | tf_op jit(solution)/shard_map/ppermute | solution.py:355
  50.6 1.2 %collective-permute-done.8.refs_10_.refs_17_ = bf16[528,128]{1,0:T(8,128)(2,1)S(1)} collective-permute-done((bf16[528,128]{1,0:T(8,128)(2,1)S(1)}, bf16[528,128]{1,0:T(8,128)(2,1)S(1)}, u32[]{:S(2)}, u32[]{:S(2)}) %collective-permute-start.8) | collective-permute-done | bytes 135200 | tf_op jit(solution)/shard_map/ppermute | solution.py:359
  51.8 2.0 %collective-permute-done.9.refs_11_.refs_18_ = bf16[528,128]{1,0:T(8,128)(2,1)S(1)} collective-permute-done((bf16[528,128]{1,0:T(8,128)(2,1)S(1)}, bf16[528,128]{1,0:T(8,128)(2,1)S(1)}, u32[]{:S(2)}, u32[]{:S(2)}) %collective-permute-start.9) | collective-permute-done | bytes 135200 | tf_op jit(solution)/shard_map/ppermute | solution.py:359
  53.9 0.7 pad_maximum_fusion.2
  54.6 3.8 %collective-permute-start.11 = (bf16[1056,128]{1,0:T(8,128)(2,1)}, bf16[1056,128]{1,0:T(8,128)(2,1)S(1)}, u32[]{:S(2)}, u32[]{:S(2)}) collective-permute-start(bf16[1056,128]{1,0:T(8,128)(2,1)} %pad_maximum_fusion.2), channel_id=1, source_target_pairs={{0,16},{16,0},{32,48},{48,32},{64,80},{80,64},{96,112},{112,96},{1... | collective-permute-start | bytes 811016 | tf_op jit(solution)/shard_map/ppermute | solution.py:355
  58.6 5.3 %collective-permute-done.10.refs_12_.refs_16_ = bf16[2112,128]{1,0:T(8,128)(2,1)S(1)} collective-permute-done((bf16[2112,128]{1,0:T(8,128)(2,1)S(1)}, bf16[2112,128]{1,0:T(8,128)(2,1)S(1)}, u32[]{:S(2)}, u32[]{:S(2)}) %collective-permute-start.10) | collective-permute-done | bytes 540704 | tf_op jit(solution)/shard_map/ppermute | solution.py:355
  63.9 12.6 %attend_more.1 = (f32[2048,128]{1,0:T(8,128)}, f32[2048,128]{1,0:T(8,128)}) custom-call(s32[13]{0:T(128)S(1)} %stack.23.refs_0_, bf16[256,1024]{1,0:T(8,128)(2,1)} %refs_2_.1, bf16[528,128]{1,0:T(8,128)(2,1)S(1)} %fusion.1.refs_2_.refs_3_, f32[2048,128]{1,0:T(8,128)} %get-tuple-element.29.refs_3_.refs_4_, ...), custom_call_target="tpu_custom_call", output_to_operand_aliasing={{0}: (4, {}), {1}: (5, {})} | custom-call | flops 1 | bytes 1 | tf_op jit(solution)/shard_map/attend_more/pallas_call | solution.py:322
  76.5 5.1 %attend_last.1 = bf16[256,1024]{1,0:T(8,128)(2,1)} custom-call(s32[2]{0:T(128)S(1)} %broadcast_5_refs_0_.2.refs_0_, s32[19]{0:T(128)S(1)} %stack.21.refs_1_, bf16[256,1024]{1,0:T(8,128)(2,1)} %refs_2_.1, bf16[528,128]{1,0:T(8,128)(2,1)S(1)} %fusion.1.refs_2_.refs_3_, f32[2048,128]{1,0:T(8,128)} %get-tuple-element.29.refs_3_.refs_4_, ...), custom_call_target="tpu_custom_call" | custom-call | flops 1 | bytes 1 | tf_op jit(solution)/shard_map/attend_last/pallas_call | solution.py:337
  (19 shorter events, 1.6 us)
Async XLA Ops:
  1.6 20.7 %collective-permute-start = (bf16[528,128]{1,0:T(8,128)(2,1)S(1)}, bf16[528,128]{1,0:T(8,128)(2,1)S(1)}, u32[]{:S(2)}, u32[]{:S(2)}) collective-permute-start(bf16[528,128]{1,0:T(8,128)(2,1)S(1)} %fusion.1.refs_2_.refs_3_), channel_id=1, source_target_pairs={{0,64},{16,80},{32,96},{48,112},{64,0},{80,16},{96,32},{112,48},{1... | collective-permute-start | bytes 405512 | tf_op jit(solution)/shard_map/ppermute | solution.py:355
  10.7 13.0 %collective-permute-start.1 = (bf16[528,128]{1,0:T(8,128)(2,1)S(1)}, bf16[528,128]{1,0:T(8,128)(2,1)S(1)}, u32[]{:S(2)}, u32[]{:S(2)}) collective-permute-start(bf16[528,128]{1,0:T(8,128)(2,1)S(1)} %fusion.1.refs_2_.refs_3_), channel_id=1, source_target_pairs={{0,32},{16,48},{32,0},{48,16},{64,96},{80,112},{96,64},{112,80},{1... | collective-permute-start | bytes 405512 | tf_op jit(solution)/shard_map/ppermute | solution.py:355
  15.9 7.8 %collective-permute-start.2 = (bf16[528,128]{1,0:T(8,128)(2,1)S(1)}, bf16[528,128]{1,0:T(8,128)(2,1)S(1)}, u32[]{:S(2)}, u32[]{:S(2)}) collective-permute-start(bf16[528,128]{1,0:T(8,128)(2,1)S(1)} %fusion.1.refs_2_.refs_3_), channel_id=1, source_target_pairs={{0,128},{16,144},{32,160},{48,176},{64,192},{80,208},{96,224},{112... | collective-permute-start | bytes 405512 | tf_op jit(solution)/shard_map/ppermute | solution.py:359
  19.0 8.4 %collective-permute-start.3 = (bf16[528,128]{1,0:T(8,128)(2,1)S(1)}, bf16[528,128]{1,0:T(8,128)(2,1)S(1)}, u32[]{:S(2)}, u32[]{:S(2)}) collective-permute-start(bf16[528,128]{1,0:T(8,128)(2,1)S(1)} %fusion.1.refs_2_.refs_3_), channel_id=1, source_target_pairs={{0,256},{16,272},{32,288},{48,304},{64,320},{80,336},{96,352},{112... | collective-permute-start | bytes 405512 | tf_op jit(solution)/shard_map/ppermute | solution.py:359
  27.4 15.6 %collective-permute-start.4 = (bf16[528,128]{1,0:T(8,128)(2,1)S(1)}, bf16[528,128]{1,0:T(8,128)(2,1)S(1)}, u32[]{:S(2)}, u32[]{:S(2)}) collective-permute-start(bf16[528,128]{1,0:T(8,128)(2,1)S(1)} %collective-permute-done.refs_3_.refs_9_), channel_id=1, source_target_pairs={{0,32},{16,48},{32,0},{48,16},{64,96},{80,112},{96,64},{112,80},{1... | collective-permute-start | bytes 405512 | tf_op jit(solution)/shard_map/ppermute | solution.py:355
  29.3 14.1 %collective-permute-start.5 = (bf16[1056,128]{1,0:T(8,128)(2,1)S(1)}, bf16[1056,128]{1,0:T(8,128)(2,1)S(1)}, u32[]{:S(2)}, u32[]{:S(2)}) collective-permute-start(bf16[1056,128]{1,0:T(8,128)(2,1)S(1)} %constant_dynamic-update-slice_fusion), channel_id=1, source_target_pairs={{0,128},{16,144},{32,160},{48,176},{64,192},{80,208},{96,224},{112... | collective-permute-start | bytes 811016 | tf_op jit(solution)/shard_map/ppermute | solution.py:359
  31.3 12.2 %collective-permute-start.6 = (bf16[1056,128]{1,0:T(8,128)(2,1)S(1)}, bf16[1056,128]{1,0:T(8,128)(2,1)S(1)}, u32[]{:S(2)}, u32[]{:S(2)}) collective-permute-start(bf16[1056,128]{1,0:T(8,128)(2,1)S(1)} %constant_dynamic-update-slice_fusion), channel_id=1, source_target_pairs={{0,256},{16,272},{32,288},{48,304},{64,320},{80,336},{96,352},{112... | collective-permute-start | bytes 811016 | tf_op jit(solution)/shard_map/ppermute | solution.py:359
  33.5 25.1 %collective-permute-start.7 = (bf16[1056,128]{1,0:T(8,128)(2,1)S(1)}, bf16[1056,128]{1,0:T(8,128)(2,1)S(1)}, u32[]{:S(2)}, u32[]{:S(2)}) collective-permute-start(bf16[1056,128]{1,0:T(8,128)(2,1)S(1)} %pad_maximum_fusion.1), channel_id=1, source_target_pairs={{0,16},{16,0},{32,48},{48,32},{64,80},{80,64},{96,112},{112,96},{1... | collective-permute-start | bytes 811016 | tf_op jit(solution)/shard_map/ppermute | solution.py:355
  43.5 8.3 %collective-permute-start.8 = (bf16[528,128]{1,0:T(8,128)(2,1)S(1)}, bf16[528,128]{1,0:T(8,128)(2,1)S(1)}, u32[]{:S(2)}, u32[]{:S(2)}) collective-permute-start(bf16[528,128]{1,0:T(8,128)(2,1)S(1)} %collective-permute-done.4.refs_9_.refs_15_), channel_id=1, source_target_pairs={{0,128},{16,144},{32,160},{48,176},{64,192},{80,208},{96,224},{112... | collective-permute-start | bytes 405512 | tf_op jit(solution)/shard_map/ppermute | solution.py:359
  45.4 8.4 %collective-permute-start.9 = (bf16[528,128]{1,0:T(8,128)(2,1)S(1)}, bf16[528,128]{1,0:T(8,128)(2,1)S(1)}, u32[]{:S(2)}, u32[]{:S(2)}) collective-permute-start(bf16[528,128]{1,0:T(8,128)(2,1)S(1)} %collective-permute-done.4.refs_9_.refs_15_), channel_id=1, source_target_pairs={{0,256},{16,272},{32,288},{48,304},{64,320},{80,336},{96,352},{112... | collective-permute-start | bytes 405512 | tf_op jit(solution)/shard_map/ppermute | solution.py:359
  46.8 17.1 %collective-permute-start.10 = (bf16[2112,128]{1,0:T(8,128)(2,1)S(1)}, bf16[2112,128]{1,0:T(8,128)(2,1)S(1)}, u32[]{:S(2)}, u32[]{:S(2)}) collective-permute-start(bf16[2112,128]{1,0:T(8,128)(2,1)S(1)} %pad_maximum_fusion), channel_id=1, source_target_pairs={{0,16},{16,0},{32,48},{48,32},{64,80},{80,64},{96,112},{112,96},{1... | collective-permute-start | bytes 1622024 | tf_op jit(solution)/shard_map/ppermute | solution.py:355
  54.6 21.9 %collective-permute-start.11 = (bf16[1056,128]{1,0:T(8,128)(2,1)}, bf16[1056,128]{1,0:T(8,128)(2,1)S(1)}, u32[]{:S(2)}, u32[]{:S(2)}) collective-permute-start(bf16[1056,128]{1,0:T(8,128)(2,1)} %pad_maximum_fusion.2), channel_id=1, source_target_pairs={{0,16},{16,0},{32,48},{48,32},{64,80},{80,64},{96,112},{112,96},{1... | collective-permute-start | bytes 811016 | tf_op jit(solution)/shard_map/ppermute | solution.py:355

commit v5 on v4

--- a/solution.py
+++ b/solution.py
@@ -71,28 +71,26 @@
 
 def gather(slots, counts, ok_ref, own_ref, k_buf, v_buf, part):
     first_id = own_ref[2 * BLOCK :, :].astype(jnp.float32)[0:1, 0:1]
+    places = [(ref, k * SLOT) for ref, count in zip(slots, counts) for k in range(count)]
+    seen = [seen_rows(first_id, ref[at + 2 * BLOCK : at + SLOT, :]) for ref, at in places]
+    seen = [rows * ok_ref[i] for i, rows in enumerate(seen)]
     full = jnp.int32(0)
     partial = jnp.int32(0)
-    at = 0
-    for ref, count in zip(slots, counts):
-        for k in range(count):
-            base = k * SLOT
-            seen = seen_rows(first_id, ref[base + 2 * BLOCK : base + SLOT, :]) * ok_ref[at]
-            at += 1
-            whole = seen == BLOCK
-
-            @pl.when(whole)
-            def _():
-                to = pl.ds(pl.multiple_of(full * BLOCK, BLOCK), BLOCK)
-                k_buf[to, :] = ref[base : base + BLOCK, :]
-                v_buf[to, :] = ref[base + BLOCK : base + 2 * BLOCK, :]
-
-            @pl.when((seen > 0) & (seen < BLOCK))
-            def _():
-                part[...] = ref[base : base + 2 * BLOCK, :]
-
-            full = full + whole.astype(jnp.int32)
-            partial = partial + jnp.where(whole, 0, seen)
+    for rows, (ref, at) in zip(seen, places):
+        whole = rows == BLOCK
+
+        @pl.when(whole)
+        def _():
+            to = pl.ds(pl.multiple_of(full * BLOCK, BLOCK), BLOCK)
+            k_buf[to, :] = ref[at : at + BLOCK, :]
+            v_buf[to, :] = ref[at + BLOCK : at + 2 * BLOCK, :]
+
+        @pl.when((rows > 0) & (rows < BLOCK))
+        def _():
+            part[...] = ref[at : at + 2 * BLOCK, :]
+
+        full = full + whole.astype(jnp.int32)
+        partial = partial + jnp.where(whole, 0, rows)
     return full, partial
 
 
@@ -181,27 +179,24 @@
     n = len(counts)
     ok_ref, q_hbm, own_ref, shift_in, l_in, acc_in = refs[:6]
     slots = refs[6 : 6 + n]
-    l_out, acc_out, q, shift, l_sum, acc_sum, k_buf, v_buf, part, sems = refs[6 + n :]
-    full, partial = gather(slots, counts, ok_ref, own_ref, k_buf, v_buf, part)
-
-    @pl.when((full > 0) | (partial > 0))
-    def _():
-        run(copies([(q_hbm, q), (shift_in, shift), (l_in, l_sum), (acc_in, acc_sum)], sems))
-        add_blocks(full, partial, q, shift, l_sum, acc_sum, k_buf, v_buf, part)
-        run(copies([(l_sum, l_out), (acc_sum, acc_out)], sems))
-
-
-def last_kernel(counts, all_counts, *refs):
-    n, m = len(counts), len(all_counts)
-    ok_ref, all_ok_ref, q_hbm, own_ref, shift_in, l_in, acc_in = refs[:7]
-    slots, everything = refs[7 : 7 + n], refs[7 + n : 7 + n + m]
-    out_ref, q, shift, l_sum, acc_sum, k_buf, v_buf, part, sems, store, top = refs[7 + n + m :]
-    moves = copies([(q_hbm, q), (shift_in, shift), (l_in, l_sum), (acc_in, acc_sum)], sems)
+    l_sum, acc_sum, q, shift, k_buf, v_buf, part, sems = refs[6 + n :]
+    moves = copies([(l_in, l_sum), (acc_in, acc_sum), (q_hbm, q), (shift_in, shift)], sems)
     for move in moves:
         move.start()
     full, partial = gather(slots, counts, ok_ref, own_ref, k_buf, v_buf, part)
     for move in moves:
         move.wait()
+    add_blocks(full, partial, q, shift, l_sum, acc_sum, k_buf, v_buf, part)
+
+
+def last_kernel(counts, all_counts, *refs):
+    n, m = len(counts), len(all_counts)
+    ok_ref, all_ok_ref, q, own_ref, shift, l_in, acc_in = refs[:7]
+    slots, everything = refs[7 : 7 + n], refs[7 + n : 7 + n + m]
+    out_ref, l_sum, acc_sum, k_buf, v_buf, part, store, top, sems = refs[7 + n + m :]
+    full, partial = gather(slots, counts, ok_ref, own_ref, k_buf, v_buf, part)
+    l_sum[...] = l_in[...]
+    acc_sum[...] = acc_in[...]
     add_blocks(full, partial, q, shift, l_sum, acc_sum, k_buf, v_buf, part)
     most = jnp.zeros((BLOCK, 1), jnp.float32)
     for h in range(HEADS):
@@ -286,15 +281,15 @@
 def buffers(blocks):
     rows = (blocks + blocks % 2 + 2) * BLOCK
     return [
-        pltpu.VMEM((BLOCK, HEADS * HEAD), jnp.bfloat16),
-        pltpu.VMEM(SUMS.shape, jnp.float32),
-        pltpu.VMEM(SUMS.shape, jnp.float32),
-        pltpu.VMEM(SUMS.shape, jnp.float32),
         pltpu.VMEM((rows, HEAD), jnp.bfloat16),
         pltpu.VMEM((rows, HEAD), jnp.bfloat16),
         pltpu.VMEM((2 * BLOCK, HEAD), jnp.bfloat16),
-        pltpu.SemaphoreType.DMA((4,)),
     ]
+
+
+QUERIES = pltpu.VMEM((BLOCK, HEADS * HEAD), jnp.bfloat16)
+SUM = pltpu.VMEM(SUMS.shape, jnp.float32)
+SEMS = pltpu.SemaphoreType.DMA((4,))
 
 
 def in_hbm(*arrays):
@@ -312,7 +307,7 @@
         out_shape=[pltpu.HBM(SUMS.shape, SUMS.dtype)] * 3,
         in_specs=[SMEM, HBM, VMEM] + [VMEM] * len(arrays),
         out_specs=[HBM] * 3,
-        scratch_shapes=buffers(sum(counts)),
+        scratch_shapes=[QUERIES] + [SUM] * 3 + buffers(sum(counts)) + [SEMS],
         compiler_params=params(VMEM_MIB), cost_estimate=COST, name="attend_first",
     )(stack_ok(ok), *in_hbm(q), own, *arrays)
 
@@ -321,11 +316,10 @@
     counts = [a.shape[0] // SLOT for a in arrays]
     sums = pl.pallas_call(
         functools.partial(more_kernel, counts),
-        out_shape=[pltpu.HBM(SUMS.shape, SUMS.dtype)] * 2,
+        out_shape=[SUMS] * 2,
         in_specs=[SMEM, HBM, VMEM] + [HBM] * 3 + [VMEM] * len(arrays),
-        out_specs=[HBM] * 2,
-        scratch_shapes=buffers(sum(counts)),
-        input_output_aliases={4: 0, 5: 1},
+        out_specs=[VMEM] * 2,
+        scratch_shapes=[QUERIES, SUM] + buffers(sum(counts)) + [SEMS],
         compiler_params=params(VMEM_MIB), cost_estimate=COST, name="attend_more",
     )(stack_ok(ok), *in_hbm(q), own, *in_hbm(*state), *arrays)
     return state[0], *sums
@@ -337,18 +331,17 @@
     return pl.pallas_call(
         functools.partial(last_kernel, counts, all_counts),
         out_shape=jax.ShapeDtypeStruct((BLOCK, HEADS * HEAD), jnp.bfloat16),
-        in_specs=[SMEM] * 2 + [HBM, VMEM] + [HBM] * 3 + [VMEM] * len(arrays)
+        in_specs=[SMEM] * 2 + [VMEM] * 5 + [VMEM] * len(arrays)
         + [pl.BlockSpec(memory_space=pl.ANY)] * len(everything),
         out_specs=VMEM,
-        scratch_shapes=buffers(sum(counts))
+        scratch_shapes=[SUM] * 2 + buffers(sum(counts))
         + [
             pltpu.VMEM((sum(all_counts), SLOT, HEAD), jnp.bfloat16),
             pltpu.VMEM((BLOCK, HEAD), jnp.float32),
+            SEMS,
         ],
         compiler_params=params(VMEM_MIB), cost_estimate=COST, name="attend_last",
-    )(
-        stack_ok(ok), stack_ok(all_ok), *in_hbm(q), own, *in_hbm(*state), *arrays, *everything
-    )
+    )(stack_ok(ok), stack_ok(all_ok), q, own, *state, *arrays, *everything)
 
 
 def exchange(v, mask):
@@ -376,7 +369,7 @@
     c0 = along_x(own, 2)
     p2 = exchange(own, 2)
     p4 = exchange(own, 4)
-    p4, p2, b0, c0 = together(p4, p2, b0, c0)
+    p4, p2 = together(p4, p2)
 
     near1 = exchange(jnp.concatenate([b0, jnp.where(bit[0] == 0, own, c0)]), 1)
     pair = jnp.concatenate([p2, p4])
@@ -384,25 +377,26 @@
     c24 = along_x(pair, 2)
     p6 = exchange(p4, 2)
     state = attend_first(q, own, [p4, p2, b0, c0], [bit[2], bit[1], one, one])
-    state, p6, b24, c24 = together(state, p6, b24, c24)
+    state, p6, near1, b24, c24 = together(state, p6, near1, b24, c24)
 
     sent = [
         b24,
         jnp.where(bit[1] == 1, p2, c24[:SLOT]),
         jnp.where(bit[2] == 1, p4, c24[SLOT:]),
     ]
-    near35 = exchange(jnp.concatenate(sent), 1)
+    sent, p6 = together(jnp.concatenate(sent), p6)
+    near35 = exchange(sent, 1)
     b6 = along_x(p6, 1)
     c6 = along_x(p6, 2)
     b6, c6 = together(b6, c6)
 
     near7 = exchange(jnp.concatenate([b6, jnp.where(bit[2] == 1, p6, c6)]), 1)
     state = attend_more(
-        state, q, own, [near1, b24, c24, p6, b6, c6, near35], [one] * 6 + [bit[2]] + [one] * 6
+        state, q, own, [near1, b24, c24, p6, b6, c6], [one] * 6 + [bit[2]] + [one] * 2
     )
     arrays = [p2, p4, b0, c0, near1, b24, c24, p6, near35, b6, c6, near7]
     ok = [bit[1], bit[2]] + [one] * 8 + [bit[2]] + [one] * 8
-    return attend_last(state, q, own, [near7], [one] * 2, arrays, ok)
+    return attend_last(state, q, own, [near35, near7], [one] * 6, arrays, ok)
 
 
 def solution(mesh):

time: 82.2 us -> 74.8 us (0.910)
  the two profiles are of different devices: /device:TPU:28 before, /device:TPU:490 now
where the time goes in v5:
time: 74.8 us; the launch traced here: 74.3 us
  starting transfers between devices  32.4 us (43%)
  waiting for transfers between devices  21 us (28%)
  Pallas kernels  17.6 us (24%)
  other arithmetic  2.79 us (4%)
    ppermute x6, starting transfers between devices, exchange(): return lax.ppermute(v, 'ctx', [(i, i ^ mask) for i in range(NX * NZ)])  17.3 us
    ppermute x6, waiting for transfers between devices, exchange(): return lax.ppermute(v, 'ctx', [(i, i ^ mask) for i in range(NX * NZ)])  16.5 us
    ppermute x6, starting transfers between devices, along_x(): lax.ppermute(v, 'ctx', [(i, i + NZ * steps) for i in range((NX - steps) *...  15.1 us
    pallas_call x1, Pallas kernels, attend_first(): pl.pallas_call(functools.partial(first_kernel, counts), out_shape=[pltpu....  6.97 us
    pallas_call x1, Pallas kernels, attend_more(): pl.pallas_call(functools.partial(more_kernel, counts), out_shape=[SUMS] *...  5.54 us
    pallas_call x1, Pallas kernels, attend_last(): pl.pallas_call(functools.partial(last_kernel, counts, all_counts), out_sh...  5.11 us
    ppermute x6, waiting for transfers between devices, along_x(): lax.ppermute(v, 'ctx', [(i, i + NZ * steps) for i in range((NX - steps) *...  4.56 us
  transfers between devices with their start and end apart: 12, of which 4 were waited for; matrix products, arithmetic and copies ran while one was open for 2% of the time, Pallas kernels for 17%

profile of v5, /device:TPU:490, one launch (start us, length us, event | category | flops | bytes accessed | tf_op | source)
XLA Modules:
  0.0 74.3 jit_solution(11742550061905186974)
XLA Ops:
  0.0 0.7 fusion.2
  0.7 0.9 %fusion.1.refs_2_.refs_3_ = bf16[528,128]{1,0:T(8,128)(2,1)S(1)} fusion(bf16[2,128]{1,0:T(2,128)(2,1)S(1)} %fusion.2, bf16[256,128]{1,0:T(8,128)(2,1)} %param.6, bf16[256,128]{1,0:T(8,128)(2,1)} %param.5), kind=kLoop, calls=%fused_computation.5 | loop fusion | flops 540672 | bytes 266752 | tf_op jit(solution)/shard_map/concatenate | solution.py:365
  1.6 3.4 %collective-permute-start.1 = (bf16[528,128]{1,0:T(8,128)(2,1)S(1)}, bf16[528,128]{1,0:T(8,128)(2,1)S(1)}, u32[]{:S(2)}, u32[]{:S(2)}) collective-permute-start(bf16[528,128]{1,0:T(8,128)(2,1)S(1)} %fusion.1.refs_2_.refs_3_), channel_id=1, source_target_pairs={{0,32},{16,48},{32,0},{48,16},{64,96},{80,112},{96,64},{112,80},{1... | collective-permute-start | bytes 405512 | tf_op jit(solution)/shard_map/ppermute | solution.py:348
  4.9 5.5 %collective-permute-start = (bf16[528,128]{1,0:T(8,128)(2,1)S(1)}, bf16[528,128]{1,0:T(8,128)(2,1)S(1)}, u32[]{:S(2)}, u32[]{:S(2)}) collective-permute-start(bf16[528,128]{1,0:T(8,128)(2,1)S(1)} %fusion.1.refs_2_.refs_3_), channel_id=1, source_target_pairs={{0,64},{16,80},{32,96},{48,112},{64,0},{80,16},{96,32},{112,48},{1... | collective-permute-start | bytes 405512 | tf_op jit(solution)/shard_map/ppermute | solution.py:348
  10.4 4.0 %collective-permute-start.3 = (bf16[528,128]{1,0:T(8,128)(2,1)S(1)}, bf16[528,128]{1,0:T(8,128)(2,1)S(1)}, u32[]{:S(2)}, u32[]{:S(2)}) collective-permute-start(bf16[528,128]{1,0:T(8,128)(2,1)S(1)} %fusion.1.refs_2_.refs_3_), channel_id=1, source_target_pairs={{0,256},{16,272},{32,288},{48,304},{64,320},{80,336},{96,352},{112... | collective-permute-start | bytes 405512 | tf_op jit(solution)/shard_map/ppermute | solution.py:352
  14.4 1.9 %collective-permute-start.2 = (bf16[528,128]{1,0:T(8,128)(2,1)S(1)}, bf16[528,128]{1,0:T(8,128)(2,1)S(1)}, u32[]{:S(2)}, u32[]{:S(2)}) collective-permute-start(bf16[528,128]{1,0:T(8,128)(2,1)S(1)} %fusion.1.refs_2_.refs_3_), channel_id=1, source_target_pairs={{0,128},{16,144},{32,160},{48,176},{64,192},{80,208},{96,224},{112... | collective-permute-start | bytes 405512 | tf_op jit(solution)/shard_map/ppermute | solution.py:352
  16.4 8.1 %collective-permute-done.refs_3_.refs_10_ = bf16[528,128]{1,0:T(8,128)(2,1)S(1)} collective-permute-done((bf16[528,128]{1,0:T(8,128)(2,1)S(1)}, bf16[528,128]{1,0:T(8,128)(2,1)S(1)}, u32[]{:S(2)}, u32[]{:S(2)}) %collective-permute-start) | collective-permute-done | bytes 135200 | tf_op jit(solution)/shard_map/ppermute | solution.py:348
  24.5 4.0 %collective-permute-start.7 = (bf16[1056,128]{1,0:T(8,128)(2,1)S(1)}, bf16[1056,128]{1,0:T(8,128)(2,1)S(1)}, u32[]{:S(2)}, u32[]{:S(2)}) collective-permute-start(bf16[1056,128]{1,0:T(8,128)(2,1)S(1)} %constant_dynamic-update-slice_fusion), channel_id=1, source_target_pairs={{0,256},{16,272},{32,288},{48,304},{64,320},{80,336},{96,352},{112... | collective-permute-start | bytes 811016 | tf_op jit(solution)/shard_map/ppermute | solution.py:352
  28.6 1.9 %collective-permute-start.6 = (bf16[1056,128]{1,0:T(8,128)(2,1)S(1)}, bf16[1056,128]{1,0:T(8,128)(2,1)S(1)}, u32[]{:S(2)}, u32[]{:S(2)}) collective-permute-start(bf16[1056,128]{1,0:T(8,128)(2,1)S(1)} %constant_dynamic-update-slice_fusion), channel_id=1, source_target_pairs={{0,128},{16,144},{32,160},{48,176},{64,192},{80,208},{96,224},{112... | collective-permute-start | bytes 811016 | tf_op jit(solution)/shard_map/ppermute | solution.py:352
  30.5 0.9 %broadcast_select_fusion.1 = bf16[528,128]{1,0:T(8,128)(2,1)S(1)} fusion(bf16[528,128]{1,0:T(8,128)(2,1)S(1)} %collective-permute-done.3.refs_6_.refs_12_, pred[]{:T(512)S(6)} %eq.12, bf16[2,128]{1,0:T(2,128)(2,1)S(1)} %fusion.2, bf16[256,128]{1,0:T(8,128)(2,1)} %param.6, bf16[256,128]{1,0:T(8,128)(2,1)} %param.5), kind=kLoop, calls=%fused_computation.9 | loop fusion | flops 608256 | bytes 401921 | tf_op jit(solution)/shard_map/jit(_where)/select_n | solution.py:374
  31.5 2.3 %collective-permute-start.5 = (bf16[1056,128]{1,0:T(8,128)(2,1)S(1)}, bf16[1056,128]{1,0:T(8,128)(2,1)S(1)}, u32[]{:S(2)}, u32[]{:S(2)}) collective-permute-start(bf16[1056,128]{1,0:T(8,128)(2,1)S(1)} %pad_maximum_fusion.1), channel_id=1, source_target_pairs={{0,16},{16,0},{32,48},{48,32},{64,80},{80,64},{96,112},{112,96},{1... | collective-permute-start | bytes 811016 | tf_op jit(solution)/shard_map/ppermute | solution.py:348
  33.7 1.9 %collective-permute-start.4 = (bf16[528,128]{1,0:T(8,128)(2,1)S(1)}, bf16[528,128]{1,0:T(8,128)(2,1)S(1)}, u32[]{:S(2)}, u32[]{:S(2)}) collective-permute-start(bf16[528,128]{1,0:T(8,128)(2,1)S(1)} %collective-permute-done.refs_3_.refs_10_), channel_id=1, source_target_pairs={{0,32},{16,48},{32,0},{48,16},{64,96},{80,112},{96,64},{112,80},{1... | collective-permute-start | bytes 405512 | tf_op jit(solution)/shard_map/ppermute | solution.py:348
  35.8 7.0 %attend_first.1 = (f32[2048,128]{1,0:T(8,128)}, f32[2048,128]{1,0:T(8,128)}, f32[2048,128]{1,0:T(8,128)}) custom-call(s32[4]{0:T(128)S(1)} %pad_add_fusion.refs_0_, bf16[256,1024]{1,0:T(8,128)(2,1)} %refs_2_.1, bf16[528,128]{1,0:T(8,128)(2,1)S(1)} %fusion.1.refs_2_.refs_3_, bf16[528,128]{1,0:T(8,128)(2,1)S(1)} %collective-permute-done.refs_3_.refs_10_, ...), custom_call_target="tpu_custom_call" | custom-call | flops 1 | bytes 1 | tf_op jit(solution)/shard_map/attend_first/pallas_call | solution.py:305
  42.7 1.4 %collective-permute-done.4.refs_9_.refs_16_ = bf16[528,128]{1,0:T(8,128)(2,1)S(1)} collective-permute-done((bf16[528,128]{1,0:T(8,128)(2,1)S(1)}, bf16[528,128]{1,0:T(8,128)(2,1)S(1)}, u32[]{:S(2)}, u32[]{:S(2)}) %collective-permute-start.4) | collective-permute-done | bytes 135200 | tf_op jit(solution)/shard_map/ppermute | solution.py:348
  44.3 1.3 %collective-permute-start.9 = (bf16[528,128]{1,0:T(8,128)(2,1)S(1)}, bf16[528,128]{1,0:T(8,128)(2,1)S(1)}, u32[]{:S(2)}, u32[]{:S(2)}) collective-permute-start(bf16[528,128]{1,0:T(8,128)(2,1)S(1)} %collective-permute-done.4.refs_9_.refs_16_), channel_id=1, source_target_pairs={{0,256},{16,272},{32,288},{48,304},{64,320},{80,336},{96,352},{112... | collective-permute-start | bytes 405512 | tf_op jit(solution)/shard_map/ppermute | solution.py:352
  45.6 1.9 %collective-permute-start.8 = (bf16[528,128]{1,0:T(8,128)(2,1)S(1)}, bf16[528,128]{1,0:T(8,128)(2,1)S(1)}, u32[]{:S(2)}, u32[]{:S(2)}) collective-permute-start(bf16[528,128]{1,0:T(8,128)(2,1)S(1)} %collective-permute-done.4.refs_9_.refs_16_), channel_id=1, source_target_pairs={{0,128},{16,144},{32,160},{48,176},{64,192},{80,208},{96,224},{112... | collective-permute-start | bytes 405512 | tf_op jit(solution)/shard_map/ppermute | solution.py:352
  47.5 2.2 %collective-permute-start.10 = (bf16[2112,128]{1,0:T(8,128)(2,1)S(1)}, bf16[2112,128]{1,0:T(8,128)(2,1)S(1)}, u32[]{:S(2)}, u32[]{:S(2)}) collective-permute-start(bf16[2112,128]{1,0:T(8,128)(2,1)S(1)} %pad_maximum_fusion), channel_id=1, source_target_pairs={{0,16},{16,0},{32,48},{48,32},{64,80},{80,64},{96,112},{112,96},{1... | collective-permute-start | bytes 1622024 | tf_op jit(solution)/shard_map/ppermute | solution.py:348
  49.7 4.6 %collective-permute-done.8.refs_10_.refs_18_ = bf16[528,128]{1,0:T(8,128)(2,1)S(1)} collective-permute-done((bf16[528,128]{1,0:T(8,128)(2,1)S(1)}, bf16[528,128]{1,0:T(8,128)(2,1)S(1)}, u32[]{:S(2)}, u32[]{:S(2)}) %collective-permute-start.8) | collective-permute-done | bytes 135200 | tf_op jit(solution)/shard_map/ppermute | solution.py:352
  54.3 2.1 %collective-permute-start.11 = (bf16[1056,128]{1,0:T(8,128)(2,1)S(1)}, bf16[1056,128]{1,0:T(8,128)(2,1)S(1)}, u32[]{:S(2)}, u32[]{:S(2)}) collective-permute-start(bf16[1056,128]{1,0:T(8,128)(2,1)S(1)} %pad_maximum_fusion.2), channel_id=1, source_target_pairs={{0,16},{16,0},{32,48},{48,32},{64,80},{80,64},{96,112},{112,96},{1... | collective-permute-start | bytes 811016 | tf_op jit(solution)/shard_map/ppermute | solution.py:348
  56.4 0.1 stack.21.refs_1_
  56.5 0.1 pad_add_fusion.1.refs_0_
  56.6 5.5 %attend_more.1 = (f32[2048,128]{1,0:T(8,128)S(1)}, f32[2048,128]{1,0:T(8,128)S(1)}) custom-call(s32[9]{0:T(128)S(1)} %pad_add_fusion.1.refs_0_, bf16[256,1024]{1,0:T(8,128)(2,1)} %refs_2_.1, bf16[528,128]{1,0:T(8,128)(2,1)S(1)} %fusion.1.refs_2_.refs_3_, f32[2048,128]{1,0:T(8,128)} %get-tuple-element.28.refs_3_.refs_4_, ...), custom_call_target="tpu_custom_call" | custom-call | flops 1 | bytes 1 | tf_op jit(solution)/shard_map/attend_more/pallas_call | solution.py:317
  62.1 7.0 %collective-permute-done.11.refs_8_.refs_20_ = bf16[1056,128]{1,0:T(8,128)(2,1)S(1)} collective-permute-done((bf16[1056,128]{1,0:T(8,128)(2,1)S(1)}, bf16[1056,128]{1,0:T(8,128)(2,1)S(1)}, u32[]{:S(2)}, u32[]{:S(2)}) %collective-permute-start.11) | collective-permute-done | bytes 270368 | tf_op jit(solution)/shard_map/ppermute | solution.py:348
  69.2 5.1 %attend_last.1 = bf16[256,1024]{1,0:T(8,128)(2,1)} custom-call(s32[6]{0:T(128)S(1)} %broadcast_5_refs_0_.2.refs_0_, s32[19]{0:T(128)S(1)} %stack.21.refs_1_, bf16[256,1024]{1,0:T(8,128)(2,1)S(1)} %copy-done, bf16[528,128]{1,0:T(8,128)(2,1)S(1)} %fusion.1.refs_2_.refs_3_, f32[2048,128]{1,0:T(8,128)S(1)} %copy-done.1, ...), custom_call_target="tpu_custom_call" | custom-call | flops 1 | bytes 1 | tf_op jit(solution)/shard_map/attend_last/pallas_call | solution.py:331
  (24 shorter events, 0.3 us)
Async XLA Ops:
  1.6 14.8 %collective-permute-start.1 = (bf16[528,128]{1,0:T(8,128)(2,1)S(1)}, bf16[528,128]{1,0:T(8,128)(2,1)S(1)}, u32[]{:S(2)}, u32[]{:S(2)}) collective-permute-start(bf16[528,128]{1,0:T(8,128)(2,1)S(1)} %fusion.1.refs_2_.refs_3_), channel_id=1, source_target_pairs={{0,32},{16,48},{32,0},{48,16},{64,96},{80,112},{96,64},{112,80},{1... | collective-permute-start | bytes 405512 | tf_op jit(solution)/shard_map/ppermute | solution.py:348
  4.9 19.5 %collective-permute-start = (bf16[528,128]{1,0:T(8,128)(2,1)S(1)}, bf16[528,128]{1,0:T(8,128)(2,1)S(1)}, u32[]{:S(2)}, u32[]{:S(2)}) collective-permute-start(bf16[528,128]{1,0:T(8,128)(2,1)S(1)} %fusion.1.refs_2_.refs_3_), channel_id=1, source_target_pairs={{0,64},{16,80},{32,96},{48,112},{64,0},{80,16},{96,32},{112,48},{1... | collective-permute-start | bytes 405512 | tf_op jit(solution)/shard_map/ppermute | solution.py:348
  10.4 20.1 %collective-permute-start.3 = (bf16[528,128]{1,0:T(8,128)(2,1)S(1)}, bf16[528,128]{1,0:T(8,128)(2,1)S(1)}, u32[]{:S(2)}, u32[]{:S(2)}) collective-permute-start(bf16[528,128]{1,0:T(8,128)(2,1)S(1)} %fusion.1.refs_2_.refs_3_), channel_id=1, source_target_pairs={{0,256},{16,272},{32,288},{48,304},{64,320},{80,336},{96,352},{112... | collective-permute-start | bytes 405512 | tf_op jit(solution)/shard_map/ppermute | solution.py:352
  14.4 17.0 %collective-permute-start.2 = (bf16[528,128]{1,0:T(8,128)(2,1)S(1)}, bf16[528,128]{1,0:T(8,128)(2,1)S(1)}, u32[]{:S(2)}, u32[]{:S(2)}) collective-permute-start(bf16[528,128]{1,0:T(8,128)(2,1)S(1)} %fusion.1.refs_2_.refs_3_), channel_id=1, source_target_pairs={{0,128},{16,144},{32,160},{48,176},{64,192},{80,208},{96,224},{112... | collective-permute-start | bytes 405512 | tf_op jit(solution)/shard_map/ppermute | solution.py:352
  24.5 19.6 %collective-permute-start.7 = (bf16[1056,128]{1,0:T(8,128)(2,1)S(1)}, bf16[1056,128]{1,0:T(8,128)(2,1)S(1)}, u32[]{:S(2)}, u32[]{:S(2)}) collective-permute-start(bf16[1056,128]{1,0:T(8,128)(2,1)S(1)} %constant_dynamic-update-slice_fusion), channel_id=1, source_target_pairs={{0,256},{16,272},{32,288},{48,304},{64,320},{80,336},{96,352},{112... | collective-permute-start | bytes 811016 | tf_op jit(solution)/shard_map/ppermute | solution.py:352
  28.6 15.6 %collective-permute-start.6 = (bf16[1056,128]{1,0:T(8,128)(2,1)S(1)}, bf16[1056,128]{1,0:T(8,128)(2,1)S(1)}, u32[]{:S(2)}, u32[]{:S(2)}) collective-permute-start(bf16[1056,128]{1,0:T(8,128)(2,1)S(1)} %constant_dynamic-update-slice_fusion), channel_id=1, source_target_pairs={{0,128},{16,144},{32,160},{48,176},{64,192},{80,208},{96,224},{112... | collective-permute-start | bytes 811016 | tf_op jit(solution)/shard_map/ppermute | solution.py:352
  31.5 12.7 %collective-permute-start.5 = (bf16[1056,128]{1,0:T(8,128)(2,1)S(1)}, bf16[1056,128]{1,0:T(8,128)(2,1)S(1)}, u32[]{:S(2)}, u32[]{:S(2)}) collective-permute-start(bf16[1056,128]{1,0:T(8,128)(2,1)S(1)} %pad_maximum_fusion.1), channel_id=1, source_target_pairs={{0,16},{16,0},{32,48},{48,32},{64,80},{80,64},{96,112},{112,96},{1... | collective-permute-start | bytes 811016 | tf_op jit(solution)/shard_map/ppermute | solution.py:348
  33.7 10.4 %collective-permute-start.4 = (bf16[528,128]{1,0:T(8,128)(2,1)S(1)}, bf16[528,128]{1,0:T(8,128)(2,1)S(1)}, u32[]{:S(2)}, u32[]{:S(2)}) collective-permute-start(bf16[528,128]{1,0:T(8,128)(2,1)S(1)} %collective-permute-done.refs_3_.refs_10_), channel_id=1, source_target_pairs={{0,32},{16,48},{32,0},{48,16},{64,96},{80,112},{96,64},{112,80},{1... | collective-permute-start | bytes 405512 | tf_op jit(solution)/shard_map/ppermute | solution.py:348
  44.3 5.5 %collective-permute-start.9 = (bf16[528,128]{1,0:T(8,128)(2,1)S(1)}, bf16[528,128]{1,0:T(8,128)(2,1)S(1)}, u32[]{:S(2)}, u32[]{:S(2)}) collective-permute-start(bf16[528,128]{1,0:T(8,128)(2,1)S(1)} %collective-permute-done.4.refs_9_.refs_16_), channel_id=1, source_target_pairs={{0,256},{16,272},{32,288},{48,304},{64,320},{80,336},{96,352},{112... | collective-permute-start | bytes 405512 | tf_op jit(solution)/shard_map/ppermute | solution.py:352
  45.6 8.7 %collective-permute-start.8 = (bf16[528,128]{1,0:T(8,128)(2,1)S(1)}, bf16[528,128]{1,0:T(8,128)(2,1)S(1)}, u32[]{:S(2)}, u32[]{:S(2)}) collective-permute-start(bf16[528,128]{1,0:T(8,128)(2,1)S(1)} %collective-permute-done.4.refs_9_.refs_16_), channel_id=1, source_target_pairs={{0,128},{16,144},{32,160},{48,176},{64,192},{80,208},{96,224},{112... | collective-permute-start | bytes 405512 | tf_op jit(solution)/shard_map/ppermute | solution.py:352
  47.5 21.6 %collective-permute-start.10 = (bf16[2112,128]{1,0:T(8,128)(2,1)S(1)}, bf16[2112,128]{1,0:T(8,128)(2,1)S(1)}, u32[]{:S(2)}, u32[]{:S(2)}) collective-permute-start(bf16[2112,128]{1,0:T(8,128)(2,1)S(1)} %pad_maximum_fusion), channel_id=1, source_target_pairs={{0,16},{16,0},{32,48},{48,32},{64,80},{80,64},{96,112},{112,96},{1... | collective-permute-start | bytes 1622024 | tf_op jit(solution)/shard_map/ppermute | solution.py:348
  54.3 14.8 %collective-permute-start.11 = (bf16[1056,128]{1,0:T(8,128)(2,1)S(1)}, bf16[1056,128]{1,0:T(8,128)(2,1)S(1)}, u32[]{:S(2)}, u32[]{:S(2)}) collective-permute-start(bf16[1056,128]{1,0:T(8,128)(2,1)S(1)} %pad_maximum_fusion.2), channel_id=1, source_target_pairs={{0,16},{16,0},{32,48},{48,32},{64,80},{80,64},{96,112},{112,96},{1... | collective-permute-start | bytes 811016 | tf_op jit(solution)/shard_map/ppermute | solution.py:348
  56.6 12.6 %copy-start = (bf16[256,1024]{1,0:T(8,128)(2,1)S(1)}, bf16[256,1024]{1,0:T(8,128)(2,1)}, u32[]{:S(2)}) copy-start(bf16[256,1024]{1,0:T(8,128)(2,1)} %refs_2_.1) | copy-start | bytes 1572868
  56.6 12.6 %copy-start.1 = (f32[2048,128]{1,0:T(8,128)S(1)}, f32[2048,128]{1,0:T(8,128)}, u32[]{:S(2)}) copy-start(f32[2048,128]{1,0:T(8,128)} %get-tuple-element.28.refs_3_.refs_4_) | copy-start | bytes 3145732

commit v6 on v5

--- a/solution.py
+++ b/solution.py
@@ -175,6 +175,20 @@
         move.wait()
 
 
+def middle_kernel(counts, *refs):
+    n = len(counts)
+    ok_ref, q_hbm, own_ref, shift_in, l_in, acc_in = refs[:6]
+    slots = refs[6 : 6 + n]
+    l_out, acc_out, q, shift, l_sum, acc_sum, k_buf, v_buf, part, sems = refs[6 + n :]
+    full, partial = gather(slots, counts, ok_ref, own_ref, k_buf, v_buf, part)
+
+    @pl.when((full > 0) | (partial > 0))
+    def _():
+        run(copies([(q_hbm, q), (shift_in, shift), (l_in, l_sum), (acc_in, acc_sum)], sems))
+        add_blocks(full, partial, q, shift, l_sum, acc_sum, k_buf, v_buf, part)
+        run(copies([(l_sum, l_out), (acc_sum, acc_out)], sems))
+
+
 def more_kernel(counts, *refs):
     n = len(counts)
     ok_ref, q_hbm, own_ref, shift_in, l_in, acc_in = refs[:6]
@@ -312,15 +326,18 @@
     )(stack_ok(ok), *in_hbm(q), own, *arrays)
 
 
-def attend_more(state, q, own, arrays, ok):
+def attend_more(state, q, own, arrays, ok, final):
     counts = [a.shape[0] // SLOT for a in arrays]
+    scratch = [QUERIES, SUM] if final else [QUERIES] + [SUM] * 3
     sums = pl.pallas_call(
-        functools.partial(more_kernel, counts),
-        out_shape=[SUMS] * 2,
+        functools.partial(more_kernel if final else middle_kernel, counts),
+        out_shape=[SUMS if final else pltpu.HBM(SUMS.shape, SUMS.dtype)] * 2,
         in_specs=[SMEM, HBM, VMEM] + [HBM] * 3 + [VMEM] * len(arrays),
-        out_specs=[VMEM] * 2,
-        scratch_shapes=[QUERIES, SUM] + buffers(sum(counts)) + [SEMS],
-        compiler_params=params(VMEM_MIB), cost_estimate=COST, name="attend_more",
+        out_specs=[VMEM if final else HBM] * 2,
+        scratch_shapes=scratch + buffers(sum(counts)) + [SEMS],
+        input_output_aliases={} if final else {4: 0, 5: 1},
+        compiler_params=params(VMEM_MIB), cost_estimate=COST,
+        name="attend_more" if final else "attend_middle",
     )(stack_ok(ok), *in_hbm(q), own, *in_hbm(*state), *arrays)
     return state[0], *sums
 
@@ -369,7 +386,7 @@
     c0 = along_x(own, 2)
     p2 = exchange(own, 2)
     p4 = exchange(own, 4)
-    p4, p2 = together(p4, p2)
+    c0, b0, p2, p4 = together(c0, b0, p2, p4)
 
     near1 = exchange(jnp.concatenate([b0, jnp.where(bit[0] == 0, own, c0)]), 1)
     pair = jnp.concatenate([p2, p4])
@@ -377,26 +394,24 @@
     c24 = along_x(pair, 2)
     p6 = exchange(p4, 2)
     state = attend_first(q, own, [p4, p2, b0, c0], [bit[2], bit[1], one, one])
-    state, p6, near1, b24, c24 = together(state, p6, near1, b24, c24)
+    state, near1, c24, b24, p6 = together(state, near1, c24, b24, p6)
 
     sent = [
         b24,
         jnp.where(bit[1] == 1, p2, c24[:SLOT]),
         jnp.where(bit[2] == 1, p4, c24[SLOT:]),
     ]
-    sent, p6 = together(jnp.concatenate(sent), p6)
-    near35 = exchange(sent, 1)
+    near35 = exchange(jnp.concatenate(sent), 1)
     b6 = along_x(p6, 1)
     c6 = along_x(p6, 2)
-    b6, c6 = together(b6, c6)
+    state = attend_more(state, q, own, [near1, b24, c24, p6], [one] * 6 + [bit[2]], False)
+    state, near35, b6, c6 = together(state, near35, b6, c6)
 
     near7 = exchange(jnp.concatenate([b6, jnp.where(bit[2] == 1, p6, c6)]), 1)
-    state = attend_more(
-        state, q, own, [near1, b24, c24, p6, b6, c6], [one] * 6 + [bit[2]] + [one] * 2
-    )
+    state = attend_more(state, q, own, [near35, b6, c6], [one] * 6, True)
     arrays = [p2, p4, b0, c0, near1, b24, c24, p6, near35, b6, c6, near7]
     ok = [bit[1], bit[2]] + [one] * 8 + [bit[2]] + [one] * 8
-    return attend_last(state, q, own, [near35, near7], [one] * 6, arrays, ok)
+    return attend_last(state, q, own, [near7], [one] * 2, arrays, ok)
 
 
 def solution(mesh):

time: 74.8 us -> 72.7 us (0.972)
  the two profiles are of different devices: /device:TPU:490 before, /device:TPU:26 now
where the time goes in v6:
time: 72.7 us; the launch traced here: 72.2 us
  starting transfers between devices  43 us (59%)
  Pallas kernels  22 us (30%)
  waiting for transfers between devices  3.76 us (5%)
  other arithmetic  2.78 us (4%)
    ppermute x6, starting transfers between devices, exchange(): return lax.ppermute(v, 'ctx', [(i, i ^ mask) for i in range(NX * NZ)])  25.8 us
    ppermute x6, starting transfers between devices, along_x(): lax.ppermute(v, 'ctx', [(i, i + NZ * steps) for i in range((NX - steps) *...  17.2 us
    pallas_call x2, Pallas kernels, attend_more(): pl.pallas_call(functools.partial(more_kernel if final else middle_kernel,...  12.5 us
    pallas_call x1, Pallas kernels, attend_first(): pl.pallas_call(functools.partial(first_kernel, counts), out_shape=[pltpu....  5.63 us
    pallas_call x1, Pallas kernels, attend_last(): pl.pallas_call(functools.partial(last_kernel, counts, all_counts), out_sh...  3.87 us
    ppermute x6, waiting for transfers between devices, exchange(): return lax.ppermute(v, 'ctx', [(i, i ^ mask) for i in range(NX * NZ)])  3.65 us
  transfers between devices with their start and end apart: 12, of which 4 were waited for; matrix products, arithmetic and copies ran while one was open for 2% of the time, Pallas kernels for 25%

profile of v6, /device:TPU:26, one launch (start us, length us, event | category | flops | bytes accessed | tf_op | source)
XLA Modules:
  0.0 72.2 jit_solution(8310536889595663723)
XLA Ops:
  0.0 0.7 fusion.2
  0.7 0.9 %fusion.1.refs_2_.refs_3_ = bf16[528,128]{1,0:T(8,128)(2,1)S(1)} fusion(bf16[2,128]{1,0:T(2,128)(2,1)S(1)} %fusion.2, bf16[256,128]{1,0:T(8,128)(2,1)} %param.6, bf16[256,128]{1,0:T(8,128)(2,1)} %param.5), kind=kLoop, calls=%fused_computation.5 | loop fusion | flops 540672 | bytes 266752 | tf_op jit(solution)/shard_map/concatenate | solution.py:382
  1.6 9.1 %collective-permute-start.3 = (bf16[528,128]{1,0:T(8,128)(2,1)S(1)}, bf16[528,128]{1,0:T(8,128)(2,1)S(1)}, u32[]{:S(2)}, u32[]{:S(2)}) collective-permute-start(bf16[528,128]{1,0:T(8,128)(2,1)S(1)} %fusion.1.refs_2_.refs_3_), channel_id=1, source_target_pairs={{0,64},{16,80},{32,96},{48,112},{64,0},{80,16},{96,32},{112,48},{1... | collective-permute-start | bytes 405512 | tf_op jit(solution)/shard_map/ppermute | solution.py:365
  10.7 5.2 %collective-permute-start.2 = (bf16[528,128]{1,0:T(8,128)(2,1)S(1)}, bf16[528,128]{1,0:T(8,128)(2,1)S(1)}, u32[]{:S(2)}, u32[]{:S(2)}) collective-permute-start(bf16[528,128]{1,0:T(8,128)(2,1)S(1)} %fusion.1.refs_2_.refs_3_), channel_id=1, source_target_pairs={{0,32},{16,48},{32,0},{48,16},{64,96},{80,112},{96,64},{112,80},{1... | collective-permute-start | bytes 405512 | tf_op jit(solution)/shard_map/ppermute | solution.py:365
  15.9 3.4 %collective-permute-start.1 = (bf16[528,128]{1,0:T(8,128)(2,1)S(1)}, bf16[528,128]{1,0:T(8,128)(2,1)S(1)}, u32[]{:S(2)}, u32[]{:S(2)}) collective-permute-start(bf16[528,128]{1,0:T(8,128)(2,1)S(1)} %fusion.1.refs_2_.refs_3_), channel_id=1, source_target_pairs={{0,128},{16,144},{32,160},{48,176},{64,192},{80,208},{96,224},{112... | collective-permute-start | bytes 405512 | tf_op jit(solution)/shard_map/ppermute | solution.py:369
  19.3 1.9 %collective-permute-start = (bf16[528,128]{1,0:T(8,128)(2,1)S(1)}, bf16[528,128]{1,0:T(8,128)(2,1)S(1)}, u32[]{:S(2)}, u32[]{:S(2)}) collective-permute-start(bf16[528,128]{1,0:T(8,128)(2,1)S(1)} %fusion.1.refs_2_.refs_3_), channel_id=1, source_target_pairs={{0,256},{16,272},{32,288},{48,304},{64,320},{80,336},{96,352},{112... | collective-permute-start | bytes 405512 | tf_op jit(solution)/shard_map/ppermute | solution.py:369
  21.2 1.0 %collective-permute-done.3.refs_3_.refs_9_ = bf16[528,128]{1,0:T(8,128)(2,1)S(1)} collective-permute-done((bf16[528,128]{1,0:T(8,128)(2,1)S(1)}, bf16[528,128]{1,0:T(8,128)(2,1)S(1)}, u32[]{:S(2)}, u32[]{:S(2)}) %collective-permute-start.3) | collective-permute-done | bytes 135200 | tf_op jit(solution)/shard_map/ppermute | solution.py:365
  22.2 1.4 %collective-permute-done.2.refs_4_.refs_8_ = bf16[528,128]{1,0:T(8,128)(2,1)S(1)} collective-permute-done((bf16[528,128]{1,0:T(8,128)(2,1)S(1)}, bf16[528,128]{1,0:T(8,128)(2,1)S(1)}, u32[]{:S(2)}, u32[]{:S(2)}) %collective-permute-start.2) | collective-permute-done | bytes 135200 | tf_op jit(solution)/shard_map/ppermute | solution.py:365
  23.6 0.1 collective-permute-done.refs_6_.refs_11_
  23.8 7.1 %collective-permute-start.6 = (bf16[1056,128]{1,0:T(8,128)(2,1)S(1)}, bf16[1056,128]{1,0:T(8,128)(2,1)S(1)}, u32[]{:S(2)}, u32[]{:S(2)}) collective-permute-start(bf16[1056,128]{1,0:T(8,128)(2,1)S(1)} %constant_dynamic-update-slice_fusion), channel_id=1, source_target_pairs={{0,128},{16,144},{32,160},{48,176},{64,192},{80,208},{96,224},{112... | collective-permute-start | bytes 811016 | tf_op jit(solution)/shard_map/ppermute | solution.py:369
  30.9 1.3 %collective-permute-start.5 = (bf16[1056,128]{1,0:T(8,128)(2,1)S(1)}, bf16[1056,128]{1,0:T(8,128)(2,1)S(1)}, u32[]{:S(2)}, u32[]{:S(2)}) collective-permute-start(bf16[1056,128]{1,0:T(8,128)(2,1)S(1)} %constant_dynamic-update-slice_fusion), channel_id=1, source_target_pairs={{0,256},{16,272},{32,288},{48,304},{64,320},{80,336},{96,352},{112... | collective-permute-start | bytes 811016 | tf_op jit(solution)/shard_map/ppermute | solution.py:369
  32.2 0.9 %broadcast_select_fusion.1 = bf16[528,128]{1,0:T(8,128)(2,1)S(1)} fusion(bf16[528,128]{1,0:T(8,128)(2,1)S(1)} %collective-permute-done.refs_6_.refs_11_, pred[]{:T(512)S(6)} %eq.12, bf16[2,128]{1,0:T(2,128)(2,1)S(1)} %fusion.2, bf16[256,128]{1,0:T(8,128)(2,1)} %param.6, bf16[256,128]{1,0:T(8,128)(2,1)} %param.5), kind=kLoop, calls=%fused_computation.9 | loop fusion | flops 608256 | bytes 401921 | tf_op jit(solution)/shard_map/jit(_where)/select_n | solution.py:391
  33.2 3.8 %collective-permute-start.4 = (bf16[1056,128]{1,0:T(8,128)(2,1)S(1)}, bf16[1056,128]{1,0:T(8,128)(2,1)S(1)}, u32[]{:S(2)}, u32[]{:S(2)}) collective-permute-start(bf16[1056,128]{1,0:T(8,128)(2,1)S(1)} %pad_maximum_fusion.1), channel_id=1, source_target_pairs={{0,16},{16,0},{32,48},{48,32},{64,80},{80,64},{96,112},{112,96},{1... | collective-permute-start | bytes 811016 | tf_op jit(solution)/shard_map/ppermute | solution.py:365
  36.9 1.9 %collective-permute-start.7 = (bf16[528,128]{1,0:T(8,128)(2,1)S(1)}, bf16[528,128]{1,0:T(8,128)(2,1)S(1)}, u32[]{:S(2)}, u32[]{:S(2)}) collective-permute-start(bf16[528,128]{1,0:T(8,128)(2,1)S(1)} %collective-permute-done.3.refs_3_.refs_9_), channel_id=1, source_target_pairs={{0,32},{16,48},{32,0},{48,16},{64,96},{80,112},{96,64},{112,80},{1... | collective-permute-start | bytes 405512 | tf_op jit(solution)/shard_map/ppermute | solution.py:365
  39.0 5.6 %attend_first.1 = (f32[2048,128]{1,0:T(8,128)}, f32[2048,128]{1,0:T(8,128)}, f32[2048,128]{1,0:T(8,128)}) custom-call(s32[4]{0:T(128)S(1)} %pad_add_fusion.refs_0_, bf16[256,1024]{1,0:T(8,128)(2,1)} %refs_2_.1, bf16[528,128]{1,0:T(8,128)(2,1)S(1)} %fusion.1.refs_2_.refs_3_, bf16[528,128]{1,0:T(8,128)(2,1)S(1)} %collective-permute-done.3.refs_3_.refs_9_, ...), custom_call_target="tpu_custom_call" | custom-call | flops 1 | bytes 1 | tf_op jit(solution)/shard_map/attend_first/pallas_call | solution.py:319
  44.6 1.2 %collective-permute-done.7.refs_9_.refs_15_ = bf16[528,128]{1,0:T(8,128)(2,1)S(1)} collective-permute-done((bf16[528,128]{1,0:T(8,128)(2,1)S(1)}, bf16[528,128]{1,0:T(8,128)(2,1)S(1)}, u32[]{:S(2)}, u32[]{:S(2)}) %collective-permute-start.7) | collective-permute-done | bytes 135200 | tf_op jit(solution)/shard_map/ppermute | solution.py:365
  45.9 1.9 %collective-permute-start.8 = (bf16[2112,128]{1,0:T(8,128)(2,1)S(1)}, bf16[2112,128]{1,0:T(8,128)(2,1)S(1)}, u32[]{:S(2)}, u32[]{:S(2)}) collective-permute-start(bf16[2112,128]{1,0:T(8,128)(2,1)S(1)} %pad_maximum_fusion), channel_id=1, source_target_pairs={{0,16},{16,0},{32,48},{48,32},{64,80},{80,64},{96,112},{112,96},{1... | collective-permute-start | bytes 1622024 | tf_op jit(solution)/shard_map/ppermute | solution.py:365
  47.8 1.3 %collective-permute-start.10 = (bf16[528,128]{1,0:T(8,128)(2,1)S(1)}, bf16[528,128]{1,0:T(8,128)(2,1)S(1)}, u32[]{:S(2)}, u32[]{:S(2)}) collective-permute-start(bf16[528,128]{1,0:T(8,128)(2,1)S(1)} %collective-permute-done.7.refs_9_.refs_15_), channel_id=1, source_target_pairs={{0,256},{16,272},{32,288},{48,304},{64,320},{80,336},{96,352},{112... | collective-permute-start | bytes 405512 | tf_op jit(solution)/shard_map/ppermute | solution.py:369
  49.1 2.2 %collective-permute-start.9 = (bf16[528,128]{1,0:T(8,128)(2,1)S(1)}, bf16[528,128]{1,0:T(8,128)(2,1)S(1)}, u32[]{:S(2)}, u32[]{:S(2)}) collective-permute-start(bf16[528,128]{1,0:T(8,128)(2,1)S(1)} %collective-permute-done.7.refs_9_.refs_15_), channel_id=1, source_target_pairs={{0,128},{16,144},{32,160},{48,176},{64,192},{80,208},{96,224},{112... | collective-permute-start | bytes 405512 | tf_op jit(solution)/shard_map/ppermute | solution.py:369
  51.4 7.0 %attend_middle.1 = (f32[2048,128]{1,0:T(8,128)}, f32[2048,128]{1,0:T(8,128)}) custom-call(s32[7]{0:T(128)S(1)} %pad_add_fusion.1.refs_0_, bf16[256,1024]{1,0:T(8,128)(2,1)} %refs_2_.1, bf16[528,128]{1,0:T(8,128)(2,1)S(1)} %fusion.1.refs_2_.refs_3_, f32[2048,128]{1,0:T(8,128)} %get-tuple-element.45.refs_3_.refs_4_, ...), custom_call_target="tpu_custom_call", output_to_operand_aliasing={{0}: (4, {}), {1}: (5, {})} | custom-call | flops 1 | bytes 1 | tf_op jit(solution)/shard_map/attend_middle/pallas_call | solution.py:332
  58.5 3.9 %collective-permute-start.11 = (bf16[1056,128]{1,0:T(8,128)(2,1)S(1)}, bf16[1056,128]{1,0:T(8,128)(2,1)S(1)}, u32[]{:S(2)}, u32[]{:S(2)}) collective-permute-start(bf16[1056,128]{1,0:T(8,128)(2,1)S(1)} %pad_maximum_fusion.2), channel_id=1, source_target_pairs={{0,16},{16,0},{32,48},{48,32},{64,80},{80,64},{96,112},{112,96},{1... | collective-permute-start | bytes 811016 | tf_op jit(solution)/shard_map/ppermute | solution.py:365
  62.5 0.1 stack.21.refs_1_
  62.6 5.5 %attend_more.1 = (f32[2048,128]{1,0:T(8,128)S(1)}, f32[2048,128]{1,0:T(8,128)S(1)}) custom-call(s32[6]{0:T(128)S(1)} %broadcast_5_refs_0_.2.refs_0_, bf16[256,1024]{1,0:T(8,128)(2,1)} %refs_2_.1, bf16[528,128]{1,0:T(8,128)(2,1)S(1)} %fusion.1.refs_2_.refs_3_, f32[2048,128]{1,0:T(8,128)} %get-tuple-element.45.refs_3_.refs_4_, ...), custom_call_target="tpu_custom_call" | custom-call | flops 1 | bytes 1 | tf_op jit(solution)/shard_map/attend_more/pallas_call | solution.py:332
  68.1 3.9 %attend_last.1 = bf16[256,1024]{1,0:T(8,128)(2,1)} custom-call(s32[2]{0:T(128)S(1)} %broadcast_7_refs_0_.2.refs_0_, s32[19]{0:T(128)S(1)} %stack.21.refs_1_, bf16[256,1024]{1,0:T(8,128)(2,1)S(1)} %copy-done.1, bf16[528,128]{1,0:T(8,128)(2,1)S(1)} %fusion.1.refs_2_.refs_3_, f32[2048,128]{1,0:T(8,128)S(1)} %copy-done, ...), custom_call_target="tpu_custom_call" | custom-call | flops 1 | bytes 1 | tf_op jit(solution)/shard_map/attend_last/pallas_call | solution.py:348
  (25 shorter events, 0.4 us)
Async XLA Ops:
  1.6 20.7 %collective-permute-start.3 = (bf16[528,128]{1,0:T(8,128)(2,1)S(1)}, bf16[528,128]{1,0:T(8,128)(2,1)S(1)}, u32[]{:S(2)}, u32[]{:S(2)}) collective-permute-start(bf16[528,128]{1,0:T(8,128)(2,1)S(1)} %fusion.1.refs_2_.refs_3_), channel_id=1, source_target_pairs={{0,64},{16,80},{32,96},{48,112},{64,0},{80,16},{96,32},{112,48},{1... | collective-permute-start | bytes 405512 | tf_op jit(solution)/shard_map/ppermute | solution.py:365
  10.7 13.0 %collective-permute-start.2 = (bf16[528,128]{1,0:T(8,128)(2,1)S(1)}, bf16[528,128]{1,0:T(8,128)(2,1)S(1)}, u32[]{:S(2)}, u32[]{:S(2)}) collective-permute-start(bf16[528,128]{1,0:T(8,128)(2,1)S(1)} %fusion.1.refs_2_.refs_3_), channel_id=1, source_target_pairs={{0,32},{16,48},{32,0},{48,16},{64,96},{80,112},{96,64},{112,80},{1... | collective-permute-start | bytes 405512 | tf_op jit(solution)/shard_map/ppermute | solution.py:365
  15.9 7.8 %collective-permute-start.1 = (bf16[528,128]{1,0:T(8,128)(2,1)S(1)}, bf16[528,128]{1,0:T(8,128)(2,1)S(1)}, u32[]{:S(2)}, u32[]{:S(2)}) collective-permute-start(bf16[528,128]{1,0:T(8,128)(2,1)S(1)} %fusion.1.refs_2_.refs_3_), channel_id=1, source_target_pairs={{0,128},{16,144},{32,160},{48,176},{64,192},{80,208},{96,224},{112... | collective-permute-start | bytes 405512 | tf_op jit(solution)/shard_map/ppermute | solution.py:369
  19.3 4.5 %collective-permute-start = (bf16[528,128]{1,0:T(8,128)(2,1)S(1)}, bf16[528,128]{1,0:T(8,128)(2,1)S(1)}, u32[]{:S(2)}, u32[]{:S(2)}) collective-permute-start(bf16[528,128]{1,0:T(8,128)(2,1)S(1)} %fusion.1.refs_2_.refs_3_), channel_id=1, source_target_pairs={{0,256},{16,272},{32,288},{48,304},{64,320},{80,336},{96,352},{112... | collective-permute-start | bytes 405512 | tf_op jit(solution)/shard_map/ppermute | solution.py:369
  23.8 22.0 %collective-permute-start.6 = (bf16[1056,128]{1,0:T(8,128)(2,1)S(1)}, bf16[1056,128]{1,0:T(8,128)(2,1)S(1)}, u32[]{:S(2)}, u32[]{:S(2)}) collective-permute-start(bf16[1056,128]{1,0:T(8,128)(2,1)S(1)} %constant_dynamic-update-slice_fusion), channel_id=1, source_target_pairs={{0,128},{16,144},{32,160},{48,176},{64,192},{80,208},{96,224},{112... | collective-permute-start | bytes 811016 | tf_op jit(solution)/shard_map/ppermute | solution.py:369
  30.9 14.9 %collective-permute-start.5 = (bf16[1056,128]{1,0:T(8,128)(2,1)S(1)}, bf16[1056,128]{1,0:T(8,128)(2,1)S(1)}, u32[]{:S(2)}, u32[]{:S(2)}) collective-permute-start(bf16[1056,128]{1,0:T(8,128)(2,1)S(1)} %constant_dynamic-update-slice_fusion), channel_id=1, source_target_pairs={{0,256},{16,272},{32,288},{48,304},{64,320},{80,336},{96,352},{112... | collective-permute-start | bytes 811016 | tf_op jit(solution)/shard_map/ppermute | solution.py:369
  33.2 12.6 %collective-permute-start.4 = (bf16[1056,128]{1,0:T(8,128)(2,1)S(1)}, bf16[1056,128]{1,0:T(8,128)(2,1)S(1)}, u32[]{:S(2)}, u32[]{:S(2)}) collective-permute-start(bf16[1056,128]{1,0:T(8,128)(2,1)S(1)} %pad_maximum_fusion.1), channel_id=1, source_target_pairs={{0,16},{16,0},{32,48},{48,32},{64,80},{80,64},{96,112},{112,96},{1... | collective-permute-start | bytes 811016 | tf_op jit(solution)/shard_map/ppermute | solution.py:365
  36.9 8.9 %collective-permute-start.7 = (bf16[528,128]{1,0:T(8,128)(2,1)S(1)}, bf16[528,128]{1,0:T(8,128)(2,1)S(1)}, u32[]{:S(2)}, u32[]{:S(2)}) collective-permute-start(bf16[528,128]{1,0:T(8,128)(2,1)S(1)} %collective-permute-done.3.refs_3_.refs_9_), channel_id=1, source_target_pairs={{0,32},{16,48},{32,0},{48,16},{64,96},{80,112},{96,64},{112,80},{1... | collective-permute-start | bytes 405512 | tf_op jit(solution)/shard_map/ppermute | solution.py:365
  45.9 12.6 %collective-permute-start.8 = (bf16[2112,128]{1,0:T(8,128)(2,1)S(1)}, bf16[2112,128]{1,0:T(8,128)(2,1)S(1)}, u32[]{:S(2)}, u32[]{:S(2)}) collective-permute-start(bf16[2112,128]{1,0:T(8,128)(2,1)S(1)} %pad_maximum_fusion), channel_id=1, source_target_pairs={{0,16},{16,0},{32,48},{48,32},{64,80},{80,64},{96,112},{112,96},{1... | collective-permute-start | bytes 1622024 | tf_op jit(solution)/shard_map/ppermute | solution.py:365
  47.8 10.6 %collective-permute-start.10 = (bf16[528,128]{1,0:T(8,128)(2,1)S(1)}, bf16[528,128]{1,0:T(8,128)(2,1)S(1)}, u32[]{:S(2)}, u32[]{:S(2)}) collective-permute-start(bf16[528,128]{1,0:T(8,128)(2,1)S(1)} %collective-permute-done.7.refs_9_.refs_15_), channel_id=1, source_target_pairs={{0,256},{16,272},{32,288},{48,304},{64,320},{80,336},{96,352},{112... | collective-permute-start | bytes 405512 | tf_op jit(solution)/shard_map/ppermute | solution.py:369
  49.1 9.3 %collective-permute-start.9 = (bf16[528,128]{1,0:T(8,128)(2,1)S(1)}, bf16[528,128]{1,0:T(8,128)(2,1)S(1)}, u32[]{:S(2)}, u32[]{:S(2)}) collective-permute-start(bf16[528,128]{1,0:T(8,128)(2,1)S(1)} %collective-permute-done.7.refs_9_.refs_15_), channel_id=1, source_target_pairs={{0,128},{16,144},{32,160},{48,176},{64,192},{80,208},{96,224},{112... | collective-permute-start | bytes 405512 | tf_op jit(solution)/shard_map/ppermute | solution.py:369
  58.5 9.6 %collective-permute-start.11 = (bf16[1056,128]{1,0:T(8,128)(2,1)S(1)}, bf16[1056,128]{1,0:T(8,128)(2,1)S(1)}, u32[]{:S(2)}, u32[]{:S(2)}) collective-permute-start(bf16[1056,128]{1,0:T(8,128)(2,1)S(1)} %pad_maximum_fusion.2), channel_id=1, source_target_pairs={{0,16},{16,0},{32,48},{48,32},{64,80},{80,64},{96,112},{112,96},{1... | collective-permute-start | bytes 811016 | tf_op jit(solution)/shard_map/ppermute | solution.py:365
  62.6 5.5 %copy-start = (f32[2048,128]{1,0:T(8,128)S(1)}, f32[2048,128]{1,0:T(8,128)}, u32[]{:S(2)}) copy-start(f32[2048,128]{1,0:T(8,128)} %get-tuple-element.45.refs_3_.refs_4_) | copy-start | bytes 3145732
  62.6 5.6 %copy-start.1 = (bf16[256,1024]{1,0:T(8,128)(2,1)S(1)}, bf16[256,1024]{1,0:T(8,128)(2,1)}, u32[]{:S(2)}) copy-start(bf16[256,1024]{1,0:T(8,128)(2,1)} %refs_2_.1) | copy-start | bytes 1572868

commit v7 on v5

--- a/solution.py
+++ b/solution.py
@@ -181,11 +181,17 @@
     slots = refs[6 : 6 + n]
     l_sum, acc_sum, q, shift, k_buf, v_buf, part, sems = refs[6 + n :]
     moves = copies([(l_in, l_sum), (acc_in, acc_sum), (q_hbm, q), (shift_in, shift)], sems)
-    for move in moves:
-        move.start()
+    moves[0].start()
+    moves[1].start()
     full, partial = gather(slots, counts, ok_ref, own_ref, k_buf, v_buf, part)
-    for move in moves:
-        move.wait()
+    found = (full > 0) | (partial > 0)
+
+    @pl.when(found)
+    def _():
+        run(moves[2:])
+
+    moves[0].wait()
+    moves[1].wait()
     add_blocks(full, partial, q, shift, l_sum, acc_sum, k_buf, v_buf, part)
 
 
@@ -312,17 +318,20 @@
     )(stack_ok(ok), *in_hbm(q), own, *arrays)
 
 
-def attend_more(state, q, own, arrays, ok):
+def attend_more(state, q, own, arrays, ok, place):
     counts = [a.shape[0] // SLOT for a in arrays]
+    shift, *sums = state
+    if place is HBM:
+        sums = in_hbm(*sums)
     sums = pl.pallas_call(
         functools.partial(more_kernel, counts),
         out_shape=[SUMS] * 2,
-        in_specs=[SMEM, HBM, VMEM] + [HBM] * 3 + [VMEM] * len(arrays),
+        in_specs=[SMEM, HBM, VMEM, HBM] + [place] * 2 + [VMEM] * len(arrays),
         out_specs=[VMEM] * 2,
         scratch_shapes=[QUERIES, SUM] + buffers(sum(counts)) + [SEMS],
         compiler_params=params(VMEM_MIB), cost_estimate=COST, name="attend_more",
-    )(stack_ok(ok), *in_hbm(q), own, *in_hbm(*state), *arrays)
-    return state[0], *sums
+    )(stack_ok(ok), *in_hbm(q), own, *in_hbm(shift), *sums, *arrays)
+    return shift, *sums
 
 
 def attend_last(state, q, own, arrays, ok, everything, all_ok):
@@ -369,34 +378,37 @@
     c0 = along_x(own, 2)
     p2 = exchange(own, 2)
     p4 = exchange(own, 4)
-    p4, p2 = together(p4, p2)
+    p4, p2, b0, c0 = together(p4, p2, b0, c0)
 
     near1 = exchange(jnp.concatenate([b0, jnp.where(bit[0] == 0, own, c0)]), 1)
     pair = jnp.concatenate([p2, p4])
+    p6 = exchange(p4, 2)
     b24 = along_x(pair, 1)
     c24 = along_x(pair, 2)
-    p6 = exchange(p4, 2)
     state = attend_first(q, own, [p4, p2, b0, c0], [bit[2], bit[1], one, one])
-    state, p6, near1, b24, c24 = together(state, p6, near1, b24, c24)
+    state, p6 = together(state, p6)
+
+    b6 = along_x(p6, 1)
+    c6 = along_x(p6, 2)
+    state, b24, c24 = together(state, b24, c24)
 
     sent = [
         b24,
         jnp.where(bit[1] == 1, p2, c24[:SLOT]),
         jnp.where(bit[2] == 1, p4, c24[SLOT:]),
     ]
-    sent, p6 = together(jnp.concatenate(sent), p6)
+    sent = jnp.concatenate(sent)
     near35 = exchange(sent, 1)
-    b6 = along_x(p6, 1)
-    c6 = along_x(p6, 2)
-    b6, c6 = together(b6, c6)
+    b6, c6, sent = together(b6, c6, sent)
 
     near7 = exchange(jnp.concatenate([b6, jnp.where(bit[2] == 1, p6, c6)]), 1)
     state = attend_more(
-        state, q, own, [near1, b24, c24, p6, b6, c6], [one] * 6 + [bit[2]] + [one] * 2
+        state, q, own, [near1, b24, c24, p6, b6, c6], [one] * 6 + [bit[2]] + [one] * 2, HBM
     )
+    state = attend_more(state, q, own, [near35], [one] * 4, VMEM)
     arrays = [p2, p4, b0, c0, near1, b24, c24, p6, near35, b6, c6, near7]
     ok = [bit[1], bit[2]] + [one] * 8 + [bit[2]] + [one] * 8
-    return attend_last(state, q, own, [near35, near7], [one] * 6, arrays, ok)
+    return attend_last(state, q, own, [near7], [one] * 2, arrays, ok)
 
 
 def solution(mesh):

time: 74.8 us -> 75.1 us (level)
  the two profiles are of different devices: /device:TPU:490 before, /device:TPU:76 now
where the time goes in v7:
time: 75.1 us; the launch traced here: 74.5 us
  starting transfers between devices  34.3 us (46%)
  Pallas kernels  24 us (32%)
  waiting for transfers between devices  12.1 us (16%)
  other arithmetic  3.49 us (5%)
    ppermute x6, starting transfers between devices, exchange(): return lax.ppermute(v, 'ctx', [(i, i ^ mask) for i in range(NX * NZ)])  23.5 us
    pallas_call x2, Pallas kernels, attend_more(): pl.pallas_call(functools.partial(more_kernel, counts), out_shape=[SUMS] *...  13.4 us
    ppermute x6, starting transfers between devices, along_x(): lax.ppermute(v, 'ctx', [(i, i + NZ * steps) for i in range((NX - steps) *...  10.8 us
    ppermute x6, waiting for transfers between devices, along_x(): lax.ppermute(v, 'ctx', [(i, i + NZ * steps) for i in range((NX - steps) *...  8.28 us
    pallas_call x1, Pallas kernels, attend_first(): pl.pallas_call(functools.partial(first_kernel, counts), out_shape=[pltpu....  6.97 us
    ppermute x6, waiting for transfers between devices, exchange(): return lax.ppermute(v, 'ctx', [(i, i ^ mask) for i in range(NX * NZ)])  3.8 us
    pallas_call x1, Pallas kernels, attend_last(): pl.pallas_call(functools.partial(last_kernel, counts, all_counts), out_sh...  3.66 us
  transfers between devices with their start and end apart: 12, of which 4 were waited for; matrix products, arithmetic and copies ran while one was open for 3% of the time, Pallas kernels for 27%

profile of v7, /device:TPU:76, one launch (start us, length us, event | category | flops | bytes accessed | tf_op | source)
XLA Modules:
  0.0 74.5 jit_solution(4175797668080309386)
XLA Ops:
  0.0 0.7 fusion.2
  0.7 0.9 %fusion.1.refs_2_.refs_3_ = bf16[528,128]{1,0:T(8,128)(2,1)S(1)} fusion(bf16[2,128]{1,0:T(2,128)(2,1)S(1)} %fusion.2, bf16[256,128]{1,0:T(8,128)(2,1)} %param.6, bf16[256,128]{1,0:T(8,128)(2,1)} %param.5), kind=kLoop, calls=%fused_computation.5 | loop fusion | flops 540672 | bytes 266752 | tf_op jit(solution)/shard_map/concatenate | solution.py:374
  1.6 9.1 %collective-permute-start = (bf16[528,128]{1,0:T(8,128)(2,1)S(1)}, bf16[528,128]{1,0:T(8,128)(2,1)S(1)}, u32[]{:S(2)}, u32[]{:S(2)}) collective-permute-start(bf16[528,128]{1,0:T(8,128)(2,1)S(1)} %fusion.1.refs_2_.refs_3_), channel_id=1, source_target_pairs={{0,64},{16,80},{32,96},{48,112},{64,0},{80,16},{96,32},{112,48},{1... | collective-permute-start | bytes 405512 | tf_op jit(solution)/shard_map/ppermute | solution.py:357
  10.7 1.9 %collective-permute-start.1 = (bf16[528,128]{1,0:T(8,128)(2,1)S(1)}, bf16[528,128]{1,0:T(8,128)(2,1)S(1)}, u32[]{:S(2)}, u32[]{:S(2)}) collective-permute-start(bf16[528,128]{1,0:T(8,128)(2,1)S(1)} %fusion.1.refs_2_.refs_3_), channel_id=1, source_target_pairs={{0,32},{16,48},{32,0},{48,16},{64,96},{80,112},{96,64},{112,80},{1... | collective-permute-start | bytes 405512 | tf_op jit(solution)/shard_map/ppermute | solution.py:357
  12.6 3.1 %collective-permute-start.2 = (bf16[528,128]{1,0:T(8,128)(2,1)S(1)}, bf16[528,128]{1,0:T(8,128)(2,1)S(1)}, u32[]{:S(2)}, u32[]{:S(2)}) collective-permute-start(bf16[528,128]{1,0:T(8,128)(2,1)S(1)} %fusion.1.refs_2_.refs_3_), channel_id=1, source_target_pairs={{0,128},{16,144},{32,160},{48,176},{64,192},{80,208},{96,224},{112... | collective-permute-start | bytes 405512 | tf_op jit(solution)/shard_map/ppermute | solution.py:361
  15.7 1.3 %collective-permute-start.3 = (bf16[528,128]{1,0:T(8,128)(2,1)S(1)}, bf16[528,128]{1,0:T(8,128)(2,1)S(1)}, u32[]{:S(2)}, u32[]{:S(2)}) collective-permute-start(bf16[528,128]{1,0:T(8,128)(2,1)S(1)} %fusion.1.refs_2_.refs_3_), channel_id=1, source_target_pairs={{0,256},{16,272},{32,288},{48,304},{64,320},{80,336},{96,352},{112... | collective-permute-start | bytes 405512 | tf_op jit(solution)/shard_map/ppermute | solution.py:361
  17.1 3.8 %collective-permute-done.refs_3_.refs_9_ = bf16[528,128]{1,0:T(8,128)(2,1)S(1)} collective-permute-done((bf16[528,128]{1,0:T(8,128)(2,1)S(1)}, bf16[528,128]{1,0:T(8,128)(2,1)S(1)}, u32[]{:S(2)}, u32[]{:S(2)}) %collective-permute-start) | collective-permute-done | bytes 135200 | tf_op jit(solution)/shard_map/ppermute | solution.py:357
  20.9 3.2 %collective-permute-done.3.refs_6_.refs_11_ = bf16[528,128]{1,0:T(8,128)(2,1)S(1)} collective-permute-done((bf16[528,128]{1,0:T(8,128)(2,1)S(1)}, bf16[528,128]{1,0:T(8,128)(2,1)S(1)}, u32[]{:S(2)}, u32[]{:S(2)}) %collective-permute-start.3) | collective-permute-done | bytes 135200 | tf_op jit(solution)/shard_map/ppermute | solution.py:361
  24.1 4.8 %collective-permute-start.4 = (bf16[528,128]{1,0:T(8,128)(2,1)S(1)}, bf16[528,128]{1,0:T(8,128)(2,1)S(1)}, u32[]{:S(2)}, u32[]{:S(2)}) collective-permute-start(bf16[528,128]{1,0:T(8,128)(2,1)S(1)} %collective-permute-done.refs_3_.refs_9_), channel_id=1, source_target_pairs={{0,32},{16,48},{32,0},{48,16},{64,96},{80,112},{96,64},{112,80},{1... | collective-permute-start | bytes 405512 | tf_op jit(solution)/shard_map/ppermute | solution.py:357
  29.0 1.9 %collective-permute-start.5 = (bf16[1056,128]{1,0:T(8,128)(2,1)S(1)}, bf16[1056,128]{1,0:T(8,128)(2,1)S(1)}, u32[]{:S(2)}, u32[]{:S(2)}) collective-permute-start(bf16[1056,128]{1,0:T(8,128)(2,1)S(1)} %constant_dynamic-update-slice_fusion), channel_id=1, source_target_pairs={{0,128},{16,144},{32,160},{48,176},{64,192},{80,208},{96,224},{112... | collective-permute-start | bytes 811016 | tf_op jit(solution)/shard_map/ppermute | solution.py:361
  30.9 1.3 %collective-permute-start.6 = (bf16[1056,128]{1,0:T(8,128)(2,1)S(1)}, bf16[1056,128]{1,0:T(8,128)(2,1)S(1)}, u32[]{:S(2)}, u32[]{:S(2)}) collective-permute-start(bf16[1056,128]{1,0:T(8,128)(2,1)S(1)} %constant_dynamic-update-slice_fusion), channel_id=1, source_target_pairs={{0,256},{16,272},{32,288},{48,304},{64,320},{80,336},{96,352},{112... | collective-permute-start | bytes 811016 | tf_op jit(solution)/shard_map/ppermute | solution.py:361
  32.2 0.9 %broadcast_select_fusion.1 = bf16[528,128]{1,0:T(8,128)(2,1)S(1)} fusion(bf16[528,128]{1,0:T(8,128)(2,1)S(1)} %collective-permute-done.3.refs_6_.refs_11_, pred[]{:T(512)S(6)} %eq.12, bf16[2,128]{1,0:T(2,128)(2,1)S(1)} %fusion.2, bf16[256,128]{1,0:T(8,128)(2,1)} %param.6, bf16[256,128]{1,0:T(8,128)(2,1)} %param.5), kind=kLoop, calls=%fused_computation.9 | loop fusion | flops 608256 | bytes 401921 | tf_op jit(solution)/shard_map/jit(_where)/select_n | solution.py:383
  33.2 3.8 %collective-permute-start.7 = (bf16[1056,128]{1,0:T(8,128)(2,1)S(1)}, bf16[1056,128]{1,0:T(8,128)(2,1)S(1)}, u32[]{:S(2)}, u32[]{:S(2)}) collective-permute-start(bf16[1056,128]{1,0:T(8,128)(2,1)S(1)} %pad_maximum_fusion.1), channel_id=1, source_target_pairs={{0,16},{16,0},{32,48},{48,32},{64,80},{80,64},{96,112},{112,96},{1... | collective-permute-start | bytes 811016 | tf_op jit(solution)/shard_map/ppermute | solution.py:357
  37.0 7.0 %attend_first.1 = (f32[2048,128]{1,0:T(8,128)}, f32[2048,128]{1,0:T(8,128)}, f32[2048,128]{1,0:T(8,128)}) custom-call(s32[4]{0:T(128)S(1)} %pad_add_fusion.refs_0_, bf16[256,1024]{1,0:T(8,128)(2,1)} %refs_2_.1, bf16[528,128]{1,0:T(8,128)(2,1)S(1)} %fusion.1.refs_2_.refs_3_, bf16[528,128]{1,0:T(8,128)(2,1)S(1)} %collective-permute-done.refs_3_.refs_9_, ...), custom_call_target="tpu_custom_call" | custom-call | flops 1 | bytes 1 | tf_op jit(solution)/shard_map/attend_first/pallas_call | solution.py:311
  44.0 1.9 %collective-permute-start.8 = (bf16[528,128]{1,0:T(8,128)(2,1)S(1)}, bf16[528,128]{1,0:T(8,128)(2,1)S(1)}, u32[]{:S(2)}, u32[]{:S(2)}) collective-permute-start(bf16[528,128]{1,0:T(8,128)(2,1)S(1)} %collective-permute-done.4.refs_9_.refs_15_), channel_id=1, source_target_pairs={{0,128},{16,144},{32,160},{48,176},{64,192},{80,208},{96,224},{112... | collective-permute-start | bytes 405512 | tf_op jit(solution)/shard_map/ppermute | solution.py:361
  45.9 1.3 %collective-permute-start.9 = (bf16[528,128]{1,0:T(8,128)(2,1)S(1)}, bf16[528,128]{1,0:T(8,128)(2,1)S(1)}, u32[]{:S(2)}, u32[]{:S(2)}) collective-permute-start(bf16[528,128]{1,0:T(8,128)(2,1)S(1)} %collective-permute-done.4.refs_9_.refs_15_), channel_id=1, source_target_pairs={{0,256},{16,272},{32,288},{48,304},{64,320},{80,336},{96,352},{112... | collective-permute-start | bytes 405512 | tf_op jit(solution)/shard_map/ppermute | solution.py:361
  47.3 1.9 %collective-permute-start.10 = (bf16[2112,128]{1,0:T(8,128)(2,1)S(1)}, bf16[2112,128]{1,0:T(8,128)(2,1)S(1)}, u32[]{:S(2)}, u32[]{:S(2)}) collective-permute-start(bf16[2112,128]{1,0:T(8,128)(2,1)S(1)} %pad_maximum_fusion), channel_id=1, source_target_pairs={{0,16},{16,0},{32,48},{48,32},{64,80},{80,64},{96,112},{112,96},{1... | collective-permute-start | bytes 1622024 | tf_op jit(solution)/shard_map/ppermute | solution.py:357
  49.3 2.8 %collective-permute-done.8.refs_10_.refs_17_ = bf16[528,128]{1,0:T(8,128)(2,1)S(1)} collective-permute-done((bf16[528,128]{1,0:T(8,128)(2,1)S(1)}, bf16[528,128]{1,0:T(8,128)(2,1)S(1)}, u32[]{:S(2)}, u32[]{:S(2)}) %collective-permute-start.8) | collective-permute-done | bytes 135200 | tf_op jit(solution)/shard_map/ppermute | solution.py:361
  52.1 2.2 %collective-permute-done.9.refs_11_.refs_18_ = bf16[528,128]{1,0:T(8,128)(2,1)S(1)} collective-permute-done((bf16[528,128]{1,0:T(8,128)(2,1)S(1)}, bf16[528,128]{1,0:T(8,128)(2,1)S(1)}, u32[]{:S(2)}, u32[]{:S(2)}) %collective-permute-start.9) | collective-permute-done | bytes 135200 | tf_op jit(solution)/shard_map/ppermute | solution.py:361
  54.4 0.7 pad_maximum_fusion.2
  55.1 1.9 %collective-permute-start.11 = (bf16[1056,128]{1,0:T(8,128)(2,1)}, bf16[1056,128]{1,0:T(8,128)(2,1)S(1)}, u32[]{:S(2)}, u32[]{:S(2)}) collective-permute-start(bf16[1056,128]{1,0:T(8,128)(2,1)} %pad_maximum_fusion.2), channel_id=1, source_target_pairs={{0,16},{16,0},{32,48},{48,32},{64,80},{80,64},{96,112},{112,96},{1... | collective-permute-start | bytes 811016 | tf_op jit(solution)/shard_map/ppermute | solution.py:357
  57.2 8.3 %attend_more.2 = (f32[2048,128]{1,0:T(8,128)S(1)}, f32[2048,128]{1,0:T(8,128)S(1)}) custom-call(s32[9]{0:T(128)S(1)} %pad_add_fusion.1.refs_0_, bf16[256,1024]{1,0:T(8,128)(2,1)} %refs_2_.1, bf16[528,128]{1,0:T(8,128)(2,1)S(1)} %fusion.1.refs_2_.refs_3_, f32[2048,128]{1,0:T(8,128)} %get-tuple-element.37.refs_3_.refs_4_, ...), custom_call_target="tpu_custom_call" | custom-call | flops 1 | bytes 1 | tf_op jit(solution)/shard_map/attend_more/pallas_call | solution.py:326
  65.6 5.1 %attend_more.3 = (f32[2048,128]{1,0:T(8,128)S(1)}, f32[2048,128]{1,0:T(8,128)S(1)}) custom-call(s32[4]{0:T(128)S(1)} %broadcast_4_refs_0_.2.refs_0_, bf16[256,1024]{1,0:T(8,128)(2,1)} %refs_2_.1, bf16[528,128]{1,0:T(8,128)(2,1)S(1)} %fusion.1.refs_2_.refs_3_, f32[2048,128]{1,0:T(8,128)} %get-tuple-element.37.refs_3_.refs_4_, ...), custom_call_target="tpu_custom_call" | custom-call | flops 1 | bytes 1 | tf_op jit(solution)/shard_map/attend_more/pallas_call | solution.py:326
  70.7 3.7 %attend_last.1 = bf16[256,1024]{1,0:T(8,128)(2,1)} custom-call(s32[2]{0:T(128)S(1)} %broadcast_5_refs_0_.2.refs_0_, s32[19]{0:T(128)S(1)} %stack.21.refs_1_, bf16[256,1024]{1,0:T(8,128)(2,1)S(1)} %copy-done.1, bf16[528,128]{1,0:T(8,128)(2,1)S(1)} %fusion.1.refs_2_.refs_3_, f32[2048,128]{1,0:T(8,128)S(1)} %copy-done, ...), custom_call_target="tpu_custom_call" | custom-call | flops 1 | bytes 1 | tf_op jit(solution)/shard_map/attend_last/pallas_call | solution.py:340
  (24 shorter events, 0.4 us)
Async XLA Ops:
  1.6 19.3 %collective-permute-start = (bf16[528,128]{1,0:T(8,128)(2,1)S(1)}, bf16[528,128]{1,0:T(8,128)(2,1)S(1)}, u32[]{:S(2)}, u32[]{:S(2)}) collective-permute-start(bf16[528,128]{1,0:T(8,128)(2,1)S(1)} %fusion.1.refs_2_.refs_3_), channel_id=1, source_target_pairs={{0,64},{16,80},{32,96},{48,112},{64,0},{80,16},{96,32},{112,48},{1... | collective-permute-start | bytes 405512 | tf_op jit(solution)/shard_map/ppermute | solution.py:357
  10.7 10.2 %collective-permute-start.1 = (bf16[528,128]{1,0:T(8,128)(2,1)S(1)}, bf16[528,128]{1,0:T(8,128)(2,1)S(1)}, u32[]{:S(2)}, u32[]{:S(2)}) collective-permute-start(bf16[528,128]{1,0:T(8,128)(2,1)S(1)} %fusion.1.refs_2_.refs_3_), channel_id=1, source_target_pairs={{0,32},{16,48},{32,0},{48,16},{64,96},{80,112},{96,64},{112,80},{1... | collective-permute-start | bytes 405512 | tf_op jit(solution)/shard_map/ppermute | solution.py:357
  12.6 8.3 %collective-permute-start.2 = (bf16[528,128]{1,0:T(8,128)(2,1)S(1)}, bf16[528,128]{1,0:T(8,128)(2,1)S(1)}, u32[]{:S(2)}, u32[]{:S(2)}) collective-permute-start(bf16[528,128]{1,0:T(8,128)(2,1)S(1)} %fusion.1.refs_2_.refs_3_), channel_id=1, source_target_pairs={{0,128},{16,144},{32,160},{48,176},{64,192},{80,208},{96,224},{112... | collective-permute-start | bytes 405512 | tf_op jit(solution)/shard_map/ppermute | solution.py:361
  15.7 8.4 %collective-permute-start.3 = (bf16[528,128]{1,0:T(8,128)(2,1)S(1)}, bf16[528,128]{1,0:T(8,128)(2,1)S(1)}, u32[]{:S(2)}, u32[]{:S(2)}) collective-permute-start(bf16[528,128]{1,0:T(8,128)(2,1)S(1)} %fusion.1.refs_2_.refs_3_), channel_id=1, source_target_pairs={{0,256},{16,272},{32,288},{48,304},{64,320},{80,336},{96,352},{112... | collective-permute-start | bytes 405512 | tf_op jit(solution)/shard_map/ppermute | solution.py:361
  24.1 19.9 %collective-permute-start.4 = (bf16[528,128]{1,0:T(8,128)(2,1)S(1)}, bf16[528,128]{1,0:T(8,128)(2,1)S(1)}, u32[]{:S(2)}, u32[]{:S(2)}) collective-permute-start(bf16[528,128]{1,0:T(8,128)(2,1)S(1)} %collective-permute-done.refs_3_.refs_9_), channel_id=1, source_target_pairs={{0,32},{16,48},{32,0},{48,16},{64,96},{80,112},{96,64},{112,80},{1... | collective-permute-start | bytes 405512 | tf_op jit(solution)/shard_map/ppermute | solution.py:357
  29.0 18.2 %collective-permute-start.5 = (bf16[1056,128]{1,0:T(8,128)(2,1)S(1)}, bf16[1056,128]{1,0:T(8,128)(2,1)S(1)}, u32[]{:S(2)}, u32[]{:S(2)}) collective-permute-start(bf16[1056,128]{1,0:T(8,128)(2,1)S(1)} %constant_dynamic-update-slice_fusion), channel_id=1, source_target_pairs={{0,128},{16,144},{32,160},{48,176},{64,192},{80,208},{96,224},{112... | collective-permute-start | bytes 811016 | tf_op jit(solution)/shard_map/ppermute | solution.py:361
  30.9 16.3 %collective-permute-start.6 = (bf16[1056,128]{1,0:T(8,128)(2,1)S(1)}, bf16[1056,128]{1,0:T(8,128)(2,1)S(1)}, u32[]{:S(2)}, u32[]{:S(2)}) collective-permute-start(bf16[1056,128]{1,0:T(8,128)(2,1)S(1)} %constant_dynamic-update-slice_fusion), channel_id=1, source_target_pairs={{0,256},{16,272},{32,288},{48,304},{64,320},{80,336},{96,352},{112... | collective-permute-start | bytes 811016 | tf_op jit(solution)/shard_map/ppermute | solution.py:361
  33.2 24.0 %collective-permute-start.7 = (bf16[1056,128]{1,0:T(8,128)(2,1)S(1)}, bf16[1056,128]{1,0:T(8,128)(2,1)S(1)}, u32[]{:S(2)}, u32[]{:S(2)}) collective-permute-start(bf16[1056,128]{1,0:T(8,128)(2,1)S(1)} %pad_maximum_fusion.1), channel_id=1, source_target_pairs={{0,16},{16,0},{32,48},{48,32},{64,80},{80,64},{96,112},{112,96},{1... | collective-permute-start | bytes 811016 | tf_op jit(solution)/shard_map/ppermute | solution.py:357
  44.0 8.1 %collective-permute-start.8 = (bf16[528,128]{1,0:T(8,128)(2,1)S(1)}, bf16[528,128]{1,0:T(8,128)(2,1)S(1)}, u32[]{:S(2)}, u32[]{:S(2)}) collective-permute-start(bf16[528,128]{1,0:T(8,128)(2,1)S(1)} %collective-permute-done.4.refs_9_.refs_15_), channel_id=1, source_target_pairs={{0,128},{16,144},{32,160},{48,176},{64,192},{80,208},{96,224},{112... | collective-permute-start | bytes 405512 | tf_op jit(solution)/shard_map/ppermute | solution.py:361
  45.9 8.4 %collective-permute-start.9 = (bf16[528,128]{1,0:T(8,128)(2,1)S(1)}, bf16[528,128]{1,0:T(8,128)(2,1)S(1)}, u32[]{:S(2)}, u32[]{:S(2)}) collective-permute-start(bf16[528,128]{1,0:T(8,128)(2,1)S(1)} %collective-permute-done.4.refs_9_.refs_15_), channel_id=1, source_target_pairs={{0,256},{16,272},{32,288},{48,304},{64,320},{80,336},{96,352},{112... | collective-permute-start | bytes 405512 | tf_op jit(solution)/shard_map/ppermute | solution.py:361
  47.3 18.2 %collective-permute-start.10 = (bf16[2112,128]{1,0:T(8,128)(2,1)S(1)}, bf16[2112,128]{1,0:T(8,128)(2,1)S(1)}, u32[]{:S(2)}, u32[]{:S(2)}) collective-permute-start(bf16[2112,128]{1,0:T(8,128)(2,1)S(1)} %pad_maximum_fusion), channel_id=1, source_target_pairs={{0,16},{16,0},{32,48},{48,32},{64,80},{80,64},{96,112},{112,96},{1... | collective-permute-start | bytes 1622024 | tf_op jit(solution)/shard_map/ppermute | solution.py:357
  55.1 15.6 %collective-permute-start.11 = (bf16[1056,128]{1,0:T(8,128)(2,1)}, bf16[1056,128]{1,0:T(8,128)(2,1)S(1)}, u32[]{:S(2)}, u32[]{:S(2)}) collective-permute-start(bf16[1056,128]{1,0:T(8,128)(2,1)} %pad_maximum_fusion.2), channel_id=1, source_target_pairs={{0,16},{16,0},{32,48},{48,32},{64,80},{80,64},{96,112},{112,96},{1... | collective-permute-start | bytes 811016 | tf_op jit(solution)/shard_map/ppermute | solution.py:357
  65.5 5.1 %copy-start = (f32[2048,128]{1,0:T(8,128)S(1)}, f32[2048,128]{1,0:T(8,128)}, u32[]{:S(2)}) copy-start(f32[2048,128]{1,0:T(8,128)} %get-tuple-element.37.refs_3_.refs_4_) | copy-start | bytes 3145732
  65.5 5.1 %copy-start.1 = (bf16[256,1024]{1,0:T(8,128)(2,1)S(1)}, bf16[256,1024]{1,0:T(8,128)(2,1)}, u32[]{:S(2)}) copy-start(bf16[256,1024]{1,0:T(8,128)(2,1)} %refs_2_.1) | copy-start | bytes 1572868

commit v8 on v5

--- a/solution.py
+++ b/solution.py
@@ -180,7 +180,7 @@
     ok_ref, q_hbm, own_ref, shift_in, l_in, acc_in = refs[:6]
     slots = refs[6 : 6 + n]
     l_sum, acc_sum, q, shift, k_buf, v_buf, part, sems = refs[6 + n :]
-    moves = copies([(l_in, l_sum), (acc_in, acc_sum), (q_hbm, q), (shift_in, shift)], sems)
+    moves = copies([(q_hbm, q), (shift_in, shift), (l_in, l_sum), (acc_in, acc_sum)], sems)
     for move in moves:
         move.start()
     full, partial = gather(slots, counts, ok_ref, own_ref, k_buf, v_buf, part)
@@ -362,33 +362,35 @@
     one = jnp.int32(1)
     ids = (doc_ids + 1).astype(jnp.bfloat16).reshape(2, HEAD)
     ids = jnp.pad(ids, ((0, IDS - 2), (0, 0)))
-    own = jnp.concatenate([keys, values, ids], axis=0)
+    (own,) = together(jnp.concatenate([keys, values, ids], axis=0))
     q = queries
 
     b0 = along_x(own, 1)
     c0 = along_x(own, 2)
     p2 = exchange(own, 2)
     p4 = exchange(own, 4)
-    p4, p2 = together(p4, p2)
+    c0, b0, p2, p4 = together(c0, b0, p2, p4)
 
     near1 = exchange(jnp.concatenate([b0, jnp.where(bit[0] == 0, own, c0)]), 1)
     pair = jnp.concatenate([p2, p4])
+    p6 = exchange(p4, 2)
     b24 = along_x(pair, 1)
     c24 = along_x(pair, 2)
-    p6 = exchange(p4, 2)
     state = attend_first(q, own, [p4, p2, b0, c0], [bit[2], bit[1], one, one])
-    state, p6, near1, b24, c24 = together(state, p6, near1, b24, c24)
+    state, p6 = together(state, p6)
+
+    b6 = along_x(p6, 1)
+    c6 = along_x(p6, 2)
+    state, b24, c24 = together(state, b24, c24)
 
     sent = [
         b24,
         jnp.where(bit[1] == 1, p2, c24[:SLOT]),
         jnp.where(bit[2] == 1, p4, c24[SLOT:]),
     ]
-    sent, p6 = together(jnp.concatenate(sent), p6)
+    sent = jnp.concatenate(sent)
     near35 = exchange(sent, 1)
-    b6 = along_x(p6, 1)
-    c6 = along_x(p6, 2)
-    b6, c6 = together(b6, c6)
+    b6, c6, sent = together(b6, c6, sent)
 
     near7 = exchange(jnp.concatenate([b6, jnp.where(bit[2] == 1, p6, c6)]), 1)
     state = attend_more(

time: 74.8 us -> 73.9 us (0.988)
  the two profiles are of different devices: /device:TPU:490 before, /device:TPU:4 now
where the time goes in v8:
time: 73.9 us; the launch traced here: 73.4 us
  starting transfers between devices  36.8 us (50%)
  Pallas kernels  19 us (26%)
  waiting for transfers between devices  14.7 us (20%)
  other arithmetic  2.59 us (4%)
    ppermute x6, starting transfers between devices, exchange(): return lax.ppermute(v, 'ctx', [(i, i ^ mask) for i in range(NX * NZ)])  25.9 us
    ppermute x6, starting transfers between devices, along_x(): lax.ppermute(v, 'ctx', [(i, i + NZ * steps) for i in range((NX - steps) *...  10.8 us
    ppermute x6, waiting for transfers between devices, exchange(): return lax.ppermute(v, 'ctx', [(i, i ^ mask) for i in range(NX * NZ)])  7.96 us
    pallas_call x1, Pallas kernels, attend_more(): pl.pallas_call(functools.partial(more_kernel, counts), out_shape=[SUMS] *...  6.91 us
    ppermute x6, waiting for transfers between devices, along_x(): lax.ppermute(v, 'ctx', [(i, i + NZ * steps) for i in range((NX - steps) *...  6.73 us
    pallas_call x1, Pallas kernels, attend_last(): pl.pallas_call(functools.partial(last_kernel, counts, all_counts), out_sh...  6.5 us
    pallas_call x1, Pallas kernels, attend_first(): pl.pallas_call(functools.partial(first_kernel, counts), out_shape=[pltpu....  5.64 us
  transfers between devices with their start and end apart: 12, of which 6 were waited for; matrix products, arithmetic and copies ran while one was open for 2% of the time, Pallas kernels for 17%

profile of v8, /device:TPU:4, one launch (start us, length us, event | category | flops | bytes accessed | tf_op | source)
XLA Modules:
  0.0 73.4 jit_solution(6305213494826985383)
XLA Ops:
  0.0 0.7 fusion.2
  0.7 0.9 %fusion.1.refs_2_.refs_3_ = bf16[528,128]{1,0:T(8,128)(2,1)S(1)} fusion(bf16[2,128]{1,0:T(2,128)(2,1)S(1)} %fusion.2, bf16[256,128]{1,0:T(8,128)(2,1)} %param.6, bf16[256,128]{1,0:T(8,128)(2,1)} %param.5), kind=kLoop, calls=%fused_computation.5 | loop fusion | flops 540672 | bytes 266752 | tf_op jit(solution)/shard_map/concatenate | solution.py:365
  1.6 9.1 %collective-permute-start.3 = (bf16[528,128]{1,0:T(8,128)(2,1)S(1)}, bf16[528,128]{1,0:T(8,128)(2,1)S(1)}, u32[]{:S(2)}, u32[]{:S(2)}) collective-permute-start(bf16[528,128]{1,0:T(8,128)(2,1)S(1)} %fusion.1.refs_2_.refs_3_), channel_id=1, source_target_pairs={{0,64},{16,80},{32,96},{48,112},{64,0},{80,16},{96,32},{112,48},{1... | collective-permute-start | bytes 405512 | tf_op jit(solution)/shard_map/ppermute | solution.py:348
  10.7 5.2 %collective-permute-start.2 = (bf16[528,128]{1,0:T(8,128)(2,1)S(1)}, bf16[528,128]{1,0:T(8,128)(2,1)S(1)}, u32[]{:S(2)}, u32[]{:S(2)}) collective-permute-start(bf16[528,128]{1,0:T(8,128)(2,1)S(1)} %fusion.1.refs_2_.refs_3_), channel_id=1, source_target_pairs={{0,32},{16,48},{32,0},{48,16},{64,96},{80,112},{96,64},{112,80},{1... | collective-permute-start | bytes 405512 | tf_op jit(solution)/shard_map/ppermute | solution.py:348
  15.9 3.1 %collective-permute-start.1 = (bf16[528,128]{1,0:T(8,128)(2,1)S(1)}, bf16[528,128]{1,0:T(8,128)(2,1)S(1)}, u32[]{:S(2)}, u32[]{:S(2)}) collective-permute-start(bf16[528,128]{1,0:T(8,128)(2,1)S(1)} %fusion.1.refs_2_.refs_3_), channel_id=1, source_target_pairs={{0,128},{16,144},{32,160},{48,176},{64,192},{80,208},{96,224},{112... | collective-permute-start | bytes 405512 | tf_op jit(solution)/shard_map/ppermute | solution.py:352
  19.0 1.3 %collective-permute-start = (bf16[528,128]{1,0:T(8,128)(2,1)S(1)}, bf16[528,128]{1,0:T(8,128)(2,1)S(1)}, u32[]{:S(2)}, u32[]{:S(2)}) collective-permute-start(bf16[528,128]{1,0:T(8,128)(2,1)S(1)} %fusion.1.refs_2_.refs_3_), channel_id=1, source_target_pairs={{0,256},{16,272},{32,288},{48,304},{64,320},{80,336},{96,352},{112... | collective-permute-start | bytes 405512 | tf_op jit(solution)/shard_map/ppermute | solution.py:352
  20.4 1.9 %collective-permute-done.3.refs_3_.refs_10_ = bf16[528,128]{1,0:T(8,128)(2,1)S(1)} collective-permute-done((bf16[528,128]{1,0:T(8,128)(2,1)S(1)}, bf16[528,128]{1,0:T(8,128)(2,1)S(1)}, u32[]{:S(2)}, u32[]{:S(2)}) %collective-permute-start.3) | collective-permute-done | bytes 135200 | tf_op jit(solution)/shard_map/ppermute | solution.py:348
  22.2 1.4 %collective-permute-done.2.refs_4_.refs_9_ = bf16[528,128]{1,0:T(8,128)(2,1)S(1)} collective-permute-done((bf16[528,128]{1,0:T(8,128)(2,1)S(1)}, bf16[528,128]{1,0:T(8,128)(2,1)S(1)}, u32[]{:S(2)}, u32[]{:S(2)}) %collective-permute-start.2) | collective-permute-done | bytes 135200 | tf_op jit(solution)/shard_map/ppermute | solution.py:348
  23.6 3.7 %collective-permute-done.refs_6_.refs_12_ = bf16[528,128]{1,0:T(8,128)(2,1)S(1)} collective-permute-done((bf16[528,128]{1,0:T(8,128)(2,1)S(1)}, bf16[528,128]{1,0:T(8,128)(2,1)S(1)}, u32[]{:S(2)}, u32[]{:S(2)}) %collective-permute-start) | collective-permute-done | bytes 135200 | tf_op jit(solution)/shard_map/ppermute | solution.py:352
  27.4 1.9 %collective-permute-start.4 = (bf16[528,128]{1,0:T(8,128)(2,1)S(1)}, bf16[528,128]{1,0:T(8,128)(2,1)S(1)}, u32[]{:S(2)}, u32[]{:S(2)}) collective-permute-start(bf16[528,128]{1,0:T(8,128)(2,1)S(1)} %collective-permute-done.3.refs_3_.refs_10_), channel_id=1, source_target_pairs={{0,32},{16,48},{32,0},{48,16},{64,96},{80,112},{96,64},{112,80},{1... | collective-permute-start | bytes 405512 | tf_op jit(solution)/shard_map/ppermute | solution.py:348
  29.3 1.3 %collective-permute-start.6 = (bf16[1056,128]{1,0:T(8,128)(2,1)S(1)}, bf16[1056,128]{1,0:T(8,128)(2,1)S(1)}, u32[]{:S(2)}, u32[]{:S(2)}) collective-permute-start(bf16[1056,128]{1,0:T(8,128)(2,1)S(1)} %constant_dynamic-update-slice_fusion), channel_id=1, source_target_pairs={{0,256},{16,272},{32,288},{48,304},{64,320},{80,336},{96,352},{112... | collective-permute-start | bytes 811016 | tf_op jit(solution)/shard_map/ppermute | solution.py:352
  30.6 1.9 %collective-permute-start.5 = (bf16[1056,128]{1,0:T(8,128)(2,1)S(1)}, bf16[1056,128]{1,0:T(8,128)(2,1)S(1)}, u32[]{:S(2)}, u32[]{:S(2)}) collective-permute-start(bf16[1056,128]{1,0:T(8,128)(2,1)S(1)} %constant_dynamic-update-slice_fusion), channel_id=1, source_target_pairs={{0,128},{16,144},{32,160},{48,176},{64,192},{80,208},{96,224},{112... | collective-permute-start | bytes 811016 | tf_op jit(solution)/shard_map/ppermute | solution.py:352
  32.6 3.8 %collective-permute-start.7 = (bf16[1056,128]{1,0:T(8,128)(2,1)S(1)}, bf16[1056,128]{1,0:T(8,128)(2,1)S(1)}, u32[]{:S(2)}, u32[]{:S(2)}) collective-permute-start(bf16[1056,128]{1,0:T(8,128)(2,1)S(1)} %pad_maximum_fusion.1), channel_id=1, source_target_pairs={{0,16},{16,0},{32,48},{48,32},{64,80},{80,64},{96,112},{112,96},{1... | collective-permute-start | bytes 811016 | tf_op jit(solution)/shard_map/ppermute | solution.py:348
  36.5 5.6 %attend_first.1 = (f32[2048,128]{1,0:T(8,128)}, f32[2048,128]{1,0:T(8,128)}, f32[2048,128]{1,0:T(8,128)}) custom-call(s32[4]{0:T(128)S(1)} %pad_add_fusion.refs_0_, bf16[256,1024]{1,0:T(8,128)(2,1)} %refs_2_.1, bf16[528,128]{1,0:T(8,128)(2,1)S(1)} %fusion.1.refs_2_.refs_3_, bf16[528,128]{1,0:T(8,128)(2,1)S(1)} %collective-permute-done.3.refs_3_.refs_10_, ...), custom_call_target="tpu_custom_call" | custom-call | flops 1 | bytes 1 | tf_op jit(solution)/shard_map/attend_first/pallas_call | solution.py:305
  42.1 1.3 %collective-permute-start.9 = (bf16[528,128]{1,0:T(8,128)(2,1)S(1)}, bf16[528,128]{1,0:T(8,128)(2,1)S(1)}, u32[]{:S(2)}, u32[]{:S(2)}) collective-permute-start(bf16[528,128]{1,0:T(8,128)(2,1)S(1)} %collective-permute-done.4.refs_9_.refs_16_), channel_id=1, source_target_pairs={{0,256},{16,272},{32,288},{48,304},{64,320},{80,336},{96,352},{112... | collective-permute-start | bytes 405512 | tf_op jit(solution)/shard_map/ppermute | solution.py:352
  43.4 1.9 %collective-permute-start.8 = (bf16[528,128]{1,0:T(8,128)(2,1)S(1)}, bf16[528,128]{1,0:T(8,128)(2,1)S(1)}, u32[]{:S(2)}, u32[]{:S(2)}) collective-permute-start(bf16[528,128]{1,0:T(8,128)(2,1)S(1)} %collective-permute-done.4.refs_9_.refs_16_), channel_id=1, source_target_pairs={{0,128},{16,144},{32,160},{48,176},{64,192},{80,208},{96,224},{112... | collective-permute-start | bytes 405512 | tf_op jit(solution)/shard_map/ppermute | solution.py:352
  45.5 3.4 %collective-permute-start.10 = (bf16[2112,128]{1,0:T(8,128)(2,1)S(1)}, bf16[2112,128]{1,0:T(8,128)(2,1)S(1)}, u32[]{:S(2)}, u32[]{:S(2)}) collective-permute-start(bf16[2112,128]{1,0:T(8,128)(2,1)S(1)} %pad_maximum_fusion), channel_id=1, source_target_pairs={{0,16},{16,0},{32,48},{48,32},{64,80},{80,64},{96,112},{112,96},{1... | collective-permute-start | bytes 1622024 | tf_op jit(solution)/shard_map/ppermute | solution.py:348
  48.9 1.9 %collective-permute-done.9.refs_11_.refs_19_ = bf16[528,128]{1,0:T(8,128)(2,1)S(1)} collective-permute-done((bf16[528,128]{1,0:T(8,128)(2,1)S(1)}, bf16[528,128]{1,0:T(8,128)(2,1)S(1)}, u32[]{:S(2)}, u32[]{:S(2)}) %collective-permute-start.9) | collective-permute-done | bytes 135200 | tf_op jit(solution)/shard_map/ppermute | solution.py:352
  50.8 1.1 %collective-permute-done.8.refs_10_.refs_18_ = bf16[528,128]{1,0:T(8,128)(2,1)S(1)} collective-permute-done((bf16[528,128]{1,0:T(8,128)(2,1)S(1)}, bf16[528,128]{1,0:T(8,128)(2,1)S(1)}, u32[]{:S(2)}, u32[]{:S(2)}) %collective-permute-start.8) | collective-permute-done | bytes 135200 | tf_op jit(solution)/shard_map/ppermute | solution.py:352
  51.9 0.7 pad_maximum_fusion.2
  52.6 2.5 %collective-permute-start.11 = (bf16[1056,128]{1,0:T(8,128)(2,1)}, bf16[1056,128]{1,0:T(8,128)(2,1)S(1)}, u32[]{:S(2)}, u32[]{:S(2)}) collective-permute-start(bf16[1056,128]{1,0:T(8,128)(2,1)} %pad_maximum_fusion.2), channel_id=1, source_target_pairs={{0,16},{16,0},{32,48},{48,32},{64,80},{80,64},{96,112},{112,96},{1... | collective-permute-start | bytes 811016 | tf_op jit(solution)/shard_map/ppermute | solution.py:348
  55.3 6.9 %attend_more.1 = (f32[2048,128]{1,0:T(8,128)S(1)}, f32[2048,128]{1,0:T(8,128)S(1)}) custom-call(s32[9]{0:T(128)S(1)} %pad_add_fusion.1.refs_0_, bf16[256,1024]{1,0:T(8,128)(2,1)} %refs_2_.1, bf16[528,128]{1,0:T(8,128)(2,1)S(1)} %fusion.1.refs_2_.refs_3_, f32[2048,128]{1,0:T(8,128)} %get-tuple-element.35.refs_3_.refs_4_, ...), custom_call_target="tpu_custom_call" | custom-call | flops 1 | bytes 1 | tf_op jit(solution)/shard_map/attend_more/pallas_call | solution.py:317
  62.2 4.7 %collective-permute-done.11.refs_8_.refs_20_ = bf16[1056,128]{1,0:T(8,128)(2,1)S(1)} collective-permute-done((bf16[1056,128]{1,0:T(8,128)(2,1)}, bf16[1056,128]{1,0:T(8,128)(2,1)S(1)}, u32[]{:S(2)}, u32[]{:S(2)}) %collective-permute-start.11) | collective-permute-done | bytes 270368 | tf_op jit(solution)/shard_map/ppermute | solution.py:348
  66.9 6.5 %attend_last.1 = bf16[256,1024]{1,0:T(8,128)(2,1)} custom-call(s32[6]{0:T(128)S(1)} %broadcast_5_refs_0_.2.refs_0_, s32[19]{0:T(128)S(1)} %stack.21.refs_1_, bf16[256,1024]{1,0:T(8,128)(2,1)S(1)} %copy-done, bf16[528,128]{1,0:T(8,128)(2,1)S(1)} %fusion.1.refs_2_.refs_3_, f32[2048,128]{1,0:T(8,128)S(1)} %copy-done.1, ...), custom_call_target="tpu_custom_call" | custom-call | flops 1 | bytes 1 | tf_op jit(solution)/shard_map/attend_last/pallas_call | solution.py:331
  (24 shorter events, 0.5 us)
Async XLA Ops:
  1.6 20.7 %collective-permute-start.3 = (bf16[528,128]{1,0:T(8,128)(2,1)S(1)}, bf16[528,128]{1,0:T(8,128)(2,1)S(1)}, u32[]{:S(2)}, u32[]{:S(2)}) collective-permute-start(bf16[528,128]{1,0:T(8,128)(2,1)S(1)} %fusion.1.refs_2_.refs_3_), channel_id=1, source_target_pairs={{0,64},{16,80},{32,96},{48,112},{64,0},{80,16},{96,32},{112,48},{1... | collective-permute-start | bytes 405512 | tf_op jit(solution)/shard_map/ppermute | solution.py:348
  10.7 13.0 %collective-permute-start.2 = (bf16[528,128]{1,0:T(8,128)(2,1)S(1)}, bf16[528,128]{1,0:T(8,128)(2,1)S(1)}, u32[]{:S(2)}, u32[]{:S(2)}) collective-permute-start(bf16[528,128]{1,0:T(8,128)(2,1)S(1)} %fusion.1.refs_2_.refs_3_), channel_id=1, source_target_pairs={{0,32},{16,48},{32,0},{48,16},{64,96},{80,112},{96,64},{112,80},{1... | collective-permute-start | bytes 405512 | tf_op jit(solution)/shard_map/ppermute | solution.py:348
  15.9 7.8 %collective-permute-start.1 = (bf16[528,128]{1,0:T(8,128)(2,1)S(1)}, bf16[528,128]{1,0:T(8,128)(2,1)S(1)}, u32[]{:S(2)}, u32[]{:S(2)}) collective-permute-start(bf16[528,128]{1,0:T(8,128)(2,1)S(1)} %fusion.1.refs_2_.refs_3_), channel_id=1, source_target_pairs={{0,128},{16,144},{32,160},{48,176},{64,192},{80,208},{96,224},{112... | collective-permute-start | bytes 405512 | tf_op jit(solution)/shard_map/ppermute | solution.py:352
  19.0 8.4 %collective-permute-start = (bf16[528,128]{1,0:T(8,128)(2,1)S(1)}, bf16[528,128]{1,0:T(8,128)(2,1)S(1)}, u32[]{:S(2)}, u32[]{:S(2)}) collective-permute-start(bf16[528,128]{1,0:T(8,128)(2,1)S(1)} %fusion.1.refs_2_.refs_3_), channel_id=1, source_target_pairs={{0,256},{16,272},{32,288},{48,304},{64,320},{80,336},{96,352},{112... | collective-permute-start | bytes 405512 | tf_op jit(solution)/shard_map/ppermute | solution.py:352
  27.4 14.7 %collective-permute-start.4 = (bf16[528,128]{1,0:T(8,128)(2,1)S(1)}, bf16[528,128]{1,0:T(8,128)(2,1)S(1)}, u32[]{:S(2)}, u32[]{:S(2)}) collective-permute-start(bf16[528,128]{1,0:T(8,128)(2,1)S(1)} %collective-permute-done.3.refs_3_.refs_10_), channel_id=1, source_target_pairs={{0,32},{16,48},{32,0},{48,16},{64,96},{80,112},{96,64},{112,80},{1... | collective-permute-start | bytes 405512 | tf_op jit(solution)/shard_map/ppermute | solution.py:348
  29.3 16.0 %collective-permute-start.6 = (bf16[1056,128]{1,0:T(8,128)(2,1)S(1)}, bf16[1056,128]{1,0:T(8,128)(2,1)S(1)}, u32[]{:S(2)}, u32[]{:S(2)}) collective-permute-start(bf16[1056,128]{1,0:T(8,128)(2,1)S(1)} %constant_dynamic-update-slice_fusion), channel_id=1, source_target_pairs={{0,256},{16,272},{32,288},{48,304},{64,320},{80,336},{96,352},{112... | collective-permute-start | bytes 811016 | tf_op jit(solution)/shard_map/ppermute | solution.py:352
  30.6 14.7 %collective-permute-start.5 = (bf16[1056,128]{1,0:T(8,128)(2,1)S(1)}, bf16[1056,128]{1,0:T(8,128)(2,1)S(1)}, u32[]{:S(2)}, u32[]{:S(2)}) collective-permute-start(bf16[1056,128]{1,0:T(8,128)(2,1)S(1)} %constant_dynamic-update-slice_fusion), channel_id=1, source_target_pairs={{0,128},{16,144},{32,160},{48,176},{64,192},{80,208},{96,224},{112... | collective-permute-start | bytes 811016 | tf_op jit(solution)/shard_map/ppermute | solution.py:352
  32.6 22.7 %collective-permute-start.7 = (bf16[1056,128]{1,0:T(8,128)(2,1)S(1)}, bf16[1056,128]{1,0:T(8,128)(2,1)S(1)}, u32[]{:S(2)}, u32[]{:S(2)}) collective-permute-start(bf16[1056,128]{1,0:T(8,128)(2,1)S(1)} %pad_maximum_fusion.1), channel_id=1, source_target_pairs={{0,16},{16,0},{32,48},{48,32},{64,80},{80,64},{96,112},{112,96},{1... | collective-permute-start | bytes 811016 | tf_op jit(solution)/shard_map/ppermute | solution.py:348
  42.1 8.7 %collective-permute-start.9 = (bf16[528,128]{1,0:T(8,128)(2,1)S(1)}, bf16[528,128]{1,0:T(8,128)(2,1)S(1)}, u32[]{:S(2)}, u32[]{:S(2)}) collective-permute-start(bf16[528,128]{1,0:T(8,128)(2,1)S(1)} %collective-permute-done.4.refs_9_.refs_16_), channel_id=1, source_target_pairs={{0,256},{16,272},{32,288},{48,304},{64,320},{80,336},{96,352},{112... | collective-permute-start | bytes 405512 | tf_op jit(solution)/shard_map/ppermute | solution.py:352
  43.4 8.4 %collective-permute-start.8 = (bf16[528,128]{1,0:T(8,128)(2,1)S(1)}, bf16[528,128]{1,0:T(8,128)(2,1)S(1)}, u32[]{:S(2)}, u32[]{:S(2)}) collective-permute-start(bf16[528,128]{1,0:T(8,128)(2,1)S(1)} %collective-permute-done.4.refs_9_.refs_16_), channel_id=1, source_target_pairs={{0,128},{16,144},{32,160},{48,176},{64,192},{80,208},{96,224},{112... | collective-permute-start | bytes 405512 | tf_op jit(solution)/shard_map/ppermute | solution.py:352
  45.5 21.5 %collective-permute-start.10 = (bf16[2112,128]{1,0:T(8,128)(2,1)S(1)}, bf16[2112,128]{1,0:T(8,128)(2,1)S(1)}, u32[]{:S(2)}, u32[]{:S(2)}) collective-permute-start(bf16[2112,128]{1,0:T(8,128)(2,1)S(1)} %pad_maximum_fusion), channel_id=1, source_target_pairs={{0,16},{16,0},{32,48},{48,32},{64,80},{80,64},{96,112},{112,96},{1... | collective-permute-start | bytes 1622024 | tf_op jit(solution)/shard_map/ppermute | solution.py:348
  52.6 14.3 %collective-permute-start.11 = (bf16[1056,128]{1,0:T(8,128)(2,1)}, bf16[1056,128]{1,0:T(8,128)(2,1)S(1)}, u32[]{:S(2)}, u32[]{:S(2)}) collective-permute-start(bf16[1056,128]{1,0:T(8,128)(2,1)} %pad_maximum_fusion.2), channel_id=1, source_target_pairs={{0,16},{16,0},{32,48},{48,32},{64,80},{80,64},{96,112},{112,96},{1... | collective-permute-start | bytes 811016 | tf_op jit(solution)/shard_map/ppermute | solution.py:348
  55.3 11.6 %copy-start = (bf16[256,1024]{1,0:T(8,128)(2,1)S(1)}, bf16[256,1024]{1,0:T(8,128)(2,1)}, u32[]{:S(2)}) copy-start(bf16[256,1024]{1,0:T(8,128)(2,1)} %refs_2_.1) | copy-start | bytes 1572868
  55.3 11.6 %copy-start.1 = (f32[2048,128]{1,0:T(8,128)S(1)}, f32[2048,128]{1,0:T(8,128)}, u32[]{:S(2)}) copy-start(f32[2048,128]{1,0:T(8,128)} %get-tuple-element.35.refs_3_.refs_4_) | copy-start | bytes 3145732

commit v9 on v8

--- a/solution.py
+++ b/solution.py
@@ -155,24 +155,14 @@
         move.wait()
 
 
-def first_kernel(counts, *refs):
-    n = len(counts)
-    ok_ref, q_hbm, own_ref = refs[:3]
-    slots = refs[3 : 3 + n]
-    shift_out, l_out, acc_out, q, shift, l_sum, acc_sum, k_buf, v_buf, part, sems = refs[3 + n :]
+def own_kernel(q_hbm, own_ref, shift_out, l_out, acc_out, q, shift, l_sum, acc_sum, sems):
     fetch, *keep = copies(
         [(q_hbm, q), (shift, shift_out), (l_sum, l_out), (acc_sum, acc_out)], sems
     )
     fetch.start()
-    full, partial = gather(slots, counts, ok_ref, own_ref, k_buf, v_buf, part)
     fetch.wait()
     add_own(q, own_ref, shift, l_sum, acc_sum)
-    keep[0].start()
-    add_blocks(full, partial, q, shift, l_sum, acc_sum, k_buf, v_buf, part)
-    keep[1].start()
-    keep[2].start()
-    for move in keep:
-        move.wait()
+    run(keep)
 
 
 def more_kernel(counts, *refs):
@@ -300,16 +290,15 @@
     return jnp.stack([jnp.asarray(o, jnp.int32) for o in ok])
 
 
-def attend_first(q, own, arrays, ok):
-    counts = [a.shape[0] // SLOT for a in arrays]
+def attend_own(q, own):
     return pl.pallas_call(
-        functools.partial(first_kernel, counts),
+        own_kernel,
         out_shape=[pltpu.HBM(SUMS.shape, SUMS.dtype)] * 3,
-        in_specs=[SMEM, HBM, VMEM] + [VMEM] * len(arrays),
+        in_specs=[HBM, VMEM],
         out_specs=[HBM] * 3,
-        scratch_shapes=[QUERIES] + [SUM] * 3 + buffers(sum(counts)) + [SEMS],
-        compiler_params=params(VMEM_MIB), cost_estimate=COST, name="attend_first",
-    )(stack_ok(ok), *in_hbm(q), own, *arrays)
+        scratch_shapes=[QUERIES] + [SUM] * 3 + [SEMS],
+        compiler_params=params(VMEM_MIB), cost_estimate=COST, name="attend_own",
+    )(*in_hbm(q), own)
 
 
 def attend_more(state, q, own, arrays, ok):
@@ -369,19 +358,19 @@
     c0 = along_x(own, 2)
     p2 = exchange(own, 2)
     p4 = exchange(own, 4)
-    c0, b0, p2, p4 = together(c0, b0, p2, p4)
+    state = attend_own(q, own)
+    state, p4, p2, b0, c0 = together(state, p4, p2, b0, c0)
 
     near1 = exchange(jnp.concatenate([b0, jnp.where(bit[0] == 0, own, c0)]), 1)
     pair = jnp.concatenate([p2, p4])
     p6 = exchange(p4, 2)
     b24 = along_x(pair, 1)
     c24 = along_x(pair, 2)
-    state = attend_first(q, own, [p4, p2, b0, c0], [bit[2], bit[1], one, one])
-    state, p6 = together(state, p6)
+    (p6,) = together(p6)
 
     b6 = along_x(p6, 1)
     c6 = along_x(p6, 2)
-    state, b24, c24 = together(state, b24, c24)
+    b24, c24 = together(b24, c24)
 
     sent = [
         b24,
@@ -394,7 +383,11 @@
 
     near7 = exchange(jnp.concatenate([b6, jnp.where(bit[2] == 1, p6, c6)]), 1)
     state = attend_more(
-        state, q, own, [near1, b24, c24, p6, b6, c6], [one] * 6 + [bit[2]] + [one] * 2
+        state,
+        q,
+        own,
+        [p4, p2, b0, c0, near1, b24, c24, p6, b6, c6],
+        [bit[2], bit[1]] + [one] * 8 + [bit[2]] + [one] * 2,
     )
     arrays = [p2, p4, b0, c0, near1, b24, c24, p6, near35, b6, c6, near7]
     ok = [bit[1], bit[2]] + [one] * 8 + [bit[2]] + [one] * 8

time: 73.9 us -> 70.3 us (0.951)
  the two profiles are of different devices: /device:TPU:4 before, /device:TPU:28 now
where the time goes in v9:
time: 70.3 us; the launch traced here: 69.8 us
  starting transfers between devices  40.7 us (58%)
  Pallas kernels  18.6 us (26%)
  waiting for transfers between devices  7.64 us (11%)
  other arithmetic  2.43 us (3%)
    ppermute x6, starting transfers between devices, exchange(): return lax.ppermute(v, 'ctx', [(i, i ^ mask) for i in range(NX * NZ)])  29.9 us
    ppermute x6, starting transfers between devices, along_x(): lax.ppermute(v, 'ctx', [(i, i + NZ * steps) for i in range((NX - steps) *...  10.8 us
    pallas_call x1, Pallas kernels, attend_more(): pl.pallas_call(functools.partial(more_kernel, counts), out_shape=[SUMS] *...  8.29 us
    pallas_call x1, Pallas kernels, attend_last(): pl.pallas_call(functools.partial(last_kernel, counts, all_counts), out_sh...  6.48 us
    ppermute x6, waiting for transfers between devices, along_x(): lax.ppermute(v, 'ctx', [(i, i + NZ * steps) for i in range((NX - steps) *...  5.48 us
    pallas_call x1, Pallas kernels, attend_own(): pl.pallas_call(own_kernel, out_shape=[pltpu.HBM(SUMS.shape, SUMS.dtype)]...  3.8 us
    ppermute x6, waiting for transfers between devices, exchange(): return lax.ppermute(v, 'ctx', [(i, i ^ mask) for i in range(NX * NZ)])  2.16 us
  transfers between devices with their start and end apart: 12, of which 4 were waited for; matrix products, arithmetic and copies ran while one was open for 1% of the time, Pallas kernels for 17%

profile of v9, /device:TPU:28, one launch (start us, length us, event | category | flops | bytes accessed | tf_op | source)
XLA Modules:
  0.0 69.8 jit_solution(10208224376165587761)
XLA Ops:
  0.0 0.7 fusion.2
  0.7 0.9 %fusion.1.own_ref.refs_2_.refs_3_ = bf16[528,128]{1,0:T(8,128)(2,1)S(1)} fusion(bf16[2,128]{1,0:T(2,128)(2,1)S(1)} %fusion.2, bf16[256,128]{1,0:T(8,128)(2,1)} %param.6, bf16[256,128]{1,0:T(8,128)(2,1)} %param.5), kind=kLoop, calls=%fused_computation.5 | loop fusion | flops 540672 | bytes 266752 | tf_op jit(solution)/shard_map/concatenate | solution.py:354
  1.6 9.1 %collective-permute-start = (bf16[528,128]{1,0:T(8,128)(2,1)S(1)}, bf16[528,128]{1,0:T(8,128)(2,1)S(1)}, u32[]{:S(2)}, u32[]{:S(2)}) collective-permute-start(bf16[528,128]{1,0:T(8,128)(2,1)S(1)} %fusion.1.own_ref.refs_2_.refs_3_), channel_id=1, source_target_pairs={{0,64},{16,80},{32,96},{48,112},{64,0},{80,16},{96,32},{112,48},{1... | collective-permute-start | bytes 405512 | tf_op jit(solution)/shard_map/ppermute | solution.py:337
  10.7 5.2 %collective-permute-start.1 = (bf16[528,128]{1,0:T(8,128)(2,1)S(1)}, bf16[528,128]{1,0:T(8,128)(2,1)S(1)}, u32[]{:S(2)}, u32[]{:S(2)}) collective-permute-start(bf16[528,128]{1,0:T(8,128)(2,1)S(1)} %fusion.1.own_ref.refs_2_.refs_3_), channel_id=1, source_target_pairs={{0,32},{16,48},{32,0},{48,16},{64,96},{80,112},{96,64},{112,80},{1... | collective-permute-start | bytes 405512 | tf_op jit(solution)/shard_map/ppermute | solution.py:337
  15.9 3.1 %collective-permute-start.2 = (bf16[528,128]{1,0:T(8,128)(2,1)S(1)}, bf16[528,128]{1,0:T(8,128)(2,1)S(1)}, u32[]{:S(2)}, u32[]{:S(2)}) collective-permute-start(bf16[528,128]{1,0:T(8,128)(2,1)S(1)} %fusion.1.own_ref.refs_2_.refs_3_), channel_id=1, source_target_pairs={{0,128},{16,144},{32,160},{48,176},{64,192},{80,208},{96,224},{112... | collective-permute-start | bytes 405512 | tf_op jit(solution)/shard_map/ppermute | solution.py:341
  19.0 1.3 %collective-permute-start.3 = (bf16[528,128]{1,0:T(8,128)(2,1)S(1)}, bf16[528,128]{1,0:T(8,128)(2,1)S(1)}, u32[]{:S(2)}, u32[]{:S(2)}) collective-permute-start(bf16[528,128]{1,0:T(8,128)(2,1)S(1)} %fusion.1.own_ref.refs_2_.refs_3_), channel_id=1, source_target_pairs={{0,256},{16,272},{32,288},{48,304},{64,320},{80,336},{96,352},{112... | collective-permute-start | bytes 405512 | tf_op jit(solution)/shard_map/ppermute | solution.py:341
  20.3 3.8 %attend_own.1 = (f32[2048,128]{1,0:T(8,128)}, f32[2048,128]{1,0:T(8,128)}, f32[2048,128]{1,0:T(8,128)}) custom-call(bf16[256,1024]{1,0:T(8,128)(2,1)} %refs_2_.1, bf16[528,128]{1,0:T(8,128)(2,1)S(1)} %fusion.1.own_ref.refs_2_.refs_3_), custom_call_target="tpu_custom_call" | custom-call | flops 1 | bytes 1 | tf_op jit(solution)/shard_map/attend_own/pallas_call | solution.py:294
  24.1 3.2 %collective-permute-done.3.refs_9_.refs_12_ = bf16[528,128]{1,0:T(8,128)(2,1)S(1)} collective-permute-done((bf16[528,128]{1,0:T(8,128)(2,1)S(1)}, bf16[528,128]{1,0:T(8,128)(2,1)S(1)}, u32[]{:S(2)}, u32[]{:S(2)}) %collective-permute-start.3) | collective-permute-done | bytes 135200 | tf_op jit(solution)/shard_map/ppermute | solution.py:341
  27.4 1.9 %collective-permute-start.5 = (bf16[1056,128]{1,0:T(8,128)(2,1)S(1)}, bf16[1056,128]{1,0:T(8,128)(2,1)S(1)}, u32[]{:S(2)}, u32[]{:S(2)}) collective-permute-start(bf16[1056,128]{1,0:T(8,128)(2,1)S(1)} %constant_dynamic-update-slice_fusion), channel_id=1, source_target_pairs={{0,128},{16,144},{32,160},{48,176},{64,192},{80,208},{96,224},{112... | collective-permute-start | bytes 811016 | tf_op jit(solution)/shard_map/ppermute | solution.py:341
  29.4 1.3 %collective-permute-start.6 = (bf16[1056,128]{1,0:T(8,128)(2,1)S(1)}, bf16[1056,128]{1,0:T(8,128)(2,1)S(1)}, u32[]{:S(2)}, u32[]{:S(2)}) collective-permute-start(bf16[1056,128]{1,0:T(8,128)(2,1)S(1)} %constant_dynamic-update-slice_fusion), channel_id=1, source_target_pairs={{0,256},{16,272},{32,288},{48,304},{64,320},{80,336},{96,352},{112... | collective-permute-start | bytes 811016 | tf_op jit(solution)/shard_map/ppermute | solution.py:341
  30.7 1.9 %collective-permute-start.7 = (bf16[528,128]{1,0:T(8,128)(2,1)S(1)}, bf16[528,128]{1,0:T(8,128)(2,1)S(1)}, u32[]{:S(2)}, u32[]{:S(2)}) collective-permute-start(bf16[528,128]{1,0:T(8,128)(2,1)S(1)} %collective-permute-done.refs_6_.refs_10_), channel_id=1, source_target_pairs={{0,32},{16,48},{32,0},{48,16},{64,96},{80,112},{96,64},{112,80},{1... | collective-permute-start | bytes 405512 | tf_op jit(solution)/shard_map/ppermute | solution.py:337
  32.6 3.8 %collective-permute-start.4 = (bf16[1056,128]{1,0:T(8,128)(2,1)S(1)}, bf16[1056,128]{1,0:T(8,128)(2,1)S(1)}, u32[]{:S(2)}, u32[]{:S(2)}) collective-permute-start(bf16[1056,128]{1,0:T(8,128)(2,1)S(1)} %pad_maximum_fusion.1), channel_id=1, source_target_pairs={{0,16},{16,0},{32,48},{48,32},{64,80},{80,64},{96,112},{112,96},{1... | collective-permute-start | bytes 811016 | tf_op jit(solution)/shard_map/ppermute | solution.py:337
  36.5 2.1 %collective-permute-done.7.refs_13_.refs_16_ = bf16[528,128]{1,0:T(8,128)(2,1)S(1)} collective-permute-done((bf16[528,128]{1,0:T(8,128)(2,1)S(1)}, bf16[528,128]{1,0:T(8,128)(2,1)S(1)}, u32[]{:S(2)}, u32[]{:S(2)}) %collective-permute-start.7) | collective-permute-done | bytes 135200 | tf_op jit(solution)/shard_map/ppermute | solution.py:337
  38.6 1.9 %collective-permute-start.8 = (bf16[528,128]{1,0:T(8,128)(2,1)S(1)}, bf16[528,128]{1,0:T(8,128)(2,1)S(1)}, u32[]{:S(2)}, u32[]{:S(2)}) collective-permute-start(bf16[528,128]{1,0:T(8,128)(2,1)S(1)} %collective-permute-done.7.refs_13_.refs_16_), channel_id=1, source_target_pairs={{0,128},{16,144},{32,160},{48,176},{64,192},{80,208},{96,224},{112... | collective-permute-start | bytes 405512 | tf_op jit(solution)/shard_map/ppermute | solution.py:341
  40.5 1.3 %collective-permute-start.9 = (bf16[528,128]{1,0:T(8,128)(2,1)S(1)}, bf16[528,128]{1,0:T(8,128)(2,1)S(1)}, u32[]{:S(2)}, u32[]{:S(2)}) collective-permute-start(bf16[528,128]{1,0:T(8,128)(2,1)S(1)} %collective-permute-done.7.refs_13_.refs_16_), channel_id=1, source_target_pairs={{0,256},{16,272},{32,288},{48,304},{64,320},{80,336},{96,352},{112... | collective-permute-start | bytes 405512 | tf_op jit(solution)/shard_map/ppermute | solution.py:341
  41.8 0.4 collective-permute-done.5.refs_11_.refs_14_
  42.3 4.8 %collective-permute-start.10 = (bf16[2112,128]{1,0:T(8,128)(2,1)S(1)}, bf16[2112,128]{1,0:T(8,128)(2,1)S(1)}, u32[]{:S(2)}, u32[]{:S(2)}) collective-permute-start(bf16[2112,128]{1,0:T(8,128)(2,1)S(1)} %pad_maximum_fusion), channel_id=1, source_target_pairs={{0,16},{16,0},{32,48},{48,32},{64,80},{80,64},{96,112},{112,96},{1... | collective-permute-start | bytes 1622024 | tf_op jit(solution)/shard_map/ppermute | solution.py:337
  47.1 1.9 %collective-permute-done.9.refs_15_.refs_19_ = bf16[528,128]{1,0:T(8,128)(2,1)S(1)} collective-permute-done((bf16[528,128]{1,0:T(8,128)(2,1)S(1)}, bf16[528,128]{1,0:T(8,128)(2,1)S(1)}, u32[]{:S(2)}, u32[]{:S(2)}) %collective-permute-start.9) | collective-permute-done | bytes 135200 | tf_op jit(solution)/shard_map/ppermute | solution.py:341
  49.0 0.7 %pad_maximum_fusion.2 = bf16[1056,128]{1,0:T(8,128)(2,1)} fusion(bf16[528,128]{1,0:T(8,128)(2,1)S(1)} %broadcast_select_fusion, bf16[528,128]{1,0:T(8,128)(2,1)S(1)} %collective-permute-done.8.refs_14_.refs_18_), kind=kLoop, calls=%fused_computation.3 | loop fusion | flops 540672 | bytes 540672 | tf_op jit(solution)/shard_map/concatenate | solution.py:384
  49.7 5.1 %collective-permute-start.11 = (bf16[1056,128]{1,0:T(8,128)(2,1)}, bf16[1056,128]{1,0:T(8,128)(2,1)S(1)}, u32[]{:S(2)}, u32[]{:S(2)}) collective-permute-start(bf16[1056,128]{1,0:T(8,128)(2,1)} %pad_maximum_fusion.2), channel_id=1, source_target_pairs={{0,16},{16,0},{32,48},{48,32},{64,80},{80,64},{96,112},{112,96},{1... | collective-permute-start | bytes 811016 | tf_op jit(solution)/shard_map/ppermute | solution.py:337
  54.8 0.1 stack.18.refs_1_
  54.9 0.1 stack.19.refs_0_
  55.0 8.3 %attend_more.1 = (f32[2048,128]{1,0:T(8,128)S(1)}, f32[2048,128]{1,0:T(8,128)S(1)}) custom-call(s32[13]{0:T(128)S(1)} %stack.19.refs_0_, bf16[256,1024]{1,0:T(8,128)(2,1)} %refs_2_.1, bf16[528,128]{1,0:T(8,128)(2,1)S(1)} %fusion.1.own_ref.refs_2_.refs_3_, f32[2048,128]{1,0:T(8,128)} %get-tuple-element.24.refs_3_.refs_4_, ...), custom_call_target="tpu_custom_call" | custom-call | flops 1 | bytes 1 | tf_op jit(solution)/shard_map/attend_more/pallas_call | solution.py:306
  63.4 6.5 %attend_last.1 = bf16[256,1024]{1,0:T(8,128)(2,1)} custom-call(s32[6]{0:T(128)S(1)} %broadcast_3_refs_0_.2.refs_0_, s32[19]{0:T(128)S(1)} %stack.18.refs_1_, bf16[256,1024]{1,0:T(8,128)(2,1)S(1)} %copy-done, bf16[528,128]{1,0:T(8,128)(2,1)S(1)} %fusion.1.own_ref.refs_2_.refs_3_, f32[2048,128]{1,0:T(8,128)S(1)} %copy-done.1, ...), custom_call_target="tpu_custom_call" | custom-call | flops 1 | bytes 1 | tf_op jit(solution)/shard_map/attend_last/pallas_call | solution.py:320
  (22 shorter events, 0.2 us)
Async XLA Ops:
  1.6 22.5 %collective-permute-start = (bf16[528,128]{1,0:T(8,128)(2,1)S(1)}, bf16[528,128]{1,0:T(8,128)(2,1)S(1)}, u32[]{:S(2)}, u32[]{:S(2)}) collective-permute-start(bf16[528,128]{1,0:T(8,128)(2,1)S(1)} %fusion.1.own_ref.refs_2_.refs_3_), channel_id=1, source_target_pairs={{0,64},{16,80},{32,96},{48,112},{64,0},{80,16},{96,32},{112,48},{1... | collective-permute-start | bytes 405512 | tf_op jit(solution)/shard_map/ppermute | solution.py:337
  10.7 13.4 %collective-permute-start.1 = (bf16[528,128]{1,0:T(8,128)(2,1)S(1)}, bf16[528,128]{1,0:T(8,128)(2,1)S(1)}, u32[]{:S(2)}, u32[]{:S(2)}) collective-permute-start(bf16[528,128]{1,0:T(8,128)(2,1)S(1)} %fusion.1.own_ref.refs_2_.refs_3_), channel_id=1, source_target_pairs={{0,32},{16,48},{32,0},{48,16},{64,96},{80,112},{96,64},{112,80},{1... | collective-permute-start | bytes 405512 | tf_op jit(solution)/shard_map/ppermute | solution.py:337
  15.9 8.3 %collective-permute-start.2 = (bf16[528,128]{1,0:T(8,128)(2,1)S(1)}, bf16[528,128]{1,0:T(8,128)(2,1)S(1)}, u32[]{:S(2)}, u32[]{:S(2)}) collective-permute-start(bf16[528,128]{1,0:T(8,128)(2,1)S(1)} %fusion.1.own_ref.refs_2_.refs_3_), channel_id=1, source_target_pairs={{0,128},{16,144},{32,160},{48,176},{64,192},{80,208},{96,224},{112... | collective-permute-start | bytes 405512 | tf_op jit(solution)/shard_map/ppermute | solution.py:341
  19.0 8.4 %collective-permute-start.3 = (bf16[528,128]{1,0:T(8,128)(2,1)S(1)}, bf16[528,128]{1,0:T(8,128)(2,1)S(1)}, u32[]{:S(2)}, u32[]{:S(2)}) collective-permute-start(bf16[528,128]{1,0:T(8,128)(2,1)S(1)} %fusion.1.own_ref.refs_2_.refs_3_), channel_id=1, source_target_pairs={{0,256},{16,272},{32,288},{48,304},{64,320},{80,336},{96,352},{112... | collective-permute-start | bytes 405512 | tf_op jit(solution)/shard_map/ppermute | solution.py:341
  27.4 14.8 %collective-permute-start.5 = (bf16[1056,128]{1,0:T(8,128)(2,1)S(1)}, bf16[1056,128]{1,0:T(8,128)(2,1)S(1)}, u32[]{:S(2)}, u32[]{:S(2)}) collective-permute-start(bf16[1056,128]{1,0:T(8,128)(2,1)S(1)} %constant_dynamic-update-slice_fusion), channel_id=1, source_target_pairs={{0,128},{16,144},{32,160},{48,176},{64,192},{80,208},{96,224},{112... | collective-permute-start | bytes 811016 | tf_op jit(solution)/shard_map/ppermute | solution.py:341
  29.4 12.9 %collective-permute-start.6 = (bf16[1056,128]{1,0:T(8,128)(2,1)S(1)}, bf16[1056,128]{1,0:T(8,128)(2,1)S(1)}, u32[]{:S(2)}, u32[]{:S(2)}) collective-permute-start(bf16[1056,128]{1,0:T(8,128)(2,1)S(1)} %constant_dynamic-update-slice_fusion), channel_id=1, source_target_pairs={{0,256},{16,272},{32,288},{48,304},{64,320},{80,336},{96,352},{112... | collective-permute-start | bytes 811016 | tf_op jit(solution)/shard_map/ppermute | solution.py:341
  30.7 8.0 %collective-permute-start.7 = (bf16[528,128]{1,0:T(8,128)(2,1)S(1)}, bf16[528,128]{1,0:T(8,128)(2,1)S(1)}, u32[]{:S(2)}, u32[]{:S(2)}) collective-permute-start(bf16[528,128]{1,0:T(8,128)(2,1)S(1)} %collective-permute-done.refs_6_.refs_10_), channel_id=1, source_target_pairs={{0,32},{16,48},{32,0},{48,16},{64,96},{80,112},{96,64},{112,80},{1... | collective-permute-start | bytes 405512 | tf_op jit(solution)/shard_map/ppermute | solution.py:337
  32.6 22.4 %collective-permute-start.4 = (bf16[1056,128]{1,0:T(8,128)(2,1)S(1)}, bf16[1056,128]{1,0:T(8,128)(2,1)S(1)}, u32[]{:S(2)}, u32[]{:S(2)}) collective-permute-start(bf16[1056,128]{1,0:T(8,128)(2,1)S(1)} %pad_maximum_fusion.1), channel_id=1, source_target_pairs={{0,16},{16,0},{32,48},{48,32},{64,80},{80,64},{96,112},{112,96},{1... | collective-permute-start | bytes 811016 | tf_op jit(solution)/shard_map/ppermute | solution.py:337
  38.6 8.5 %collective-permute-start.8 = (bf16[528,128]{1,0:T(8,128)(2,1)S(1)}, bf16[528,128]{1,0:T(8,128)(2,1)S(1)}, u32[]{:S(2)}, u32[]{:S(2)}) collective-permute-start(bf16[528,128]{1,0:T(8,128)(2,1)S(1)} %collective-permute-done.7.refs_13_.refs_16_), channel_id=1, source_target_pairs={{0,128},{16,144},{32,160},{48,176},{64,192},{80,208},{96,224},{112... | collective-permute-start | bytes 405512 | tf_op jit(solution)/shard_map/ppermute | solution.py:341
  40.5 8.4 %collective-permute-start.9 = (bf16[528,128]{1,0:T(8,128)(2,1)S(1)}, bf16[528,128]{1,0:T(8,128)(2,1)S(1)}, u32[]{:S(2)}, u32[]{:S(2)}) collective-permute-start(bf16[528,128]{1,0:T(8,128)(2,1)S(1)} %collective-permute-done.7.refs_13_.refs_16_), channel_id=1, source_target_pairs={{0,256},{16,272},{32,288},{48,304},{64,320},{80,336},{96,352},{112... | collective-permute-start | bytes 405512 | tf_op jit(solution)/shard_map/ppermute | solution.py:341
  42.3 21.0 %collective-permute-start.10 = (bf16[2112,128]{1,0:T(8,128)(2,1)S(1)}, bf16[2112,128]{1,0:T(8,128)(2,1)S(1)}, u32[]{:S(2)}, u32[]{:S(2)}) collective-permute-start(bf16[2112,128]{1,0:T(8,128)(2,1)S(1)} %pad_maximum_fusion), channel_id=1, source_target_pairs={{0,16},{16,0},{32,48},{48,32},{64,80},{80,64},{96,112},{112,96},{1... | collective-permute-start | bytes 1622024 | tf_op jit(solution)/shard_map/ppermute | solution.py:337
  49.7 13.6 %collective-permute-start.11 = (bf16[1056,128]{1,0:T(8,128)(2,1)}, bf16[1056,128]{1,0:T(8,128)(2,1)S(1)}, u32[]{:S(2)}, u32[]{:S(2)}) collective-permute-start(bf16[1056,128]{1,0:T(8,128)(2,1)} %pad_maximum_fusion.2), channel_id=1, source_target_pairs={{0,16},{16,0},{32,48},{48,32},{64,80},{80,64},{96,112},{112,96},{1... | collective-permute-start | bytes 811016 | tf_op jit(solution)/shard_map/ppermute | solution.py:337
  55.0 8.3 %copy-start = (bf16[256,1024]{1,0:T(8,128)(2,1)S(1)}, bf16[256,1024]{1,0:T(8,128)(2,1)}, u32[]{:S(2)}) copy-start(bf16[256,1024]{1,0:T(8,128)(2,1)} %refs_2_.1) | copy-start | bytes 1572868
  55.0 8.3 %copy-start.1 = (f32[2048,128]{1,0:T(8,128)S(1)}, f32[2048,128]{1,0:T(8,128)}, u32[]{:S(2)}) copy-start(f32[2048,128]{1,0:T(8,128)} %get-tuple-element.24.refs_3_.refs_4_) | copy-start | bytes 3145732

commit v10 on v9

--- a/solution.py
+++ b/solution.py
@@ -366,7 +366,7 @@
     p6 = exchange(p4, 2)
     b24 = along_x(pair, 1)
     c24 = along_x(pair, 2)
-    (p6,) = together(p6)
+    state, p6 = together(state, p6)
 
     b6 = along_x(p6, 1)
     c6 = along_x(p6, 2)

time: 70.3 us -> 70.9 us (level)
  the two profiles are of different devices: /device:TPU:28 before, /device:TPU:20 now
where the time goes in v10:
time: 70.9 us; the launch traced here: 70.4 us
  starting transfers between devices  38.4 us (54%)
  Pallas kernels  17 us (24%)
  waiting for transfers between devices  12.1 us (17%)
  other arithmetic  2.43 us (3%)
    ppermute x6, starting transfers between devices, exchange(): return lax.ppermute(v, 'ctx', [(i, i ^ mask) for i in range(NX * NZ)])  27.6 us
    ppermute x6, starting transfers between devices, along_x(): lax.ppermute(v, 'ctx', [(i, i + NZ * steps) for i in range((NX - steps) *...  10.8 us
    ppermute x6, waiting for transfers between devices, along_x(): lax.ppermute(v, 'ctx', [(i, i + NZ * steps) for i in range((NX - steps) *...  8.94 us
    pallas_call x1, Pallas kernels, attend_more(): pl.pallas_call(functools.partial(more_kernel, counts), out_shape=[SUMS] *...  6.7 us
    pallas_call x1, Pallas kernels, attend_last(): pl.pallas_call(functools.partial(last_kernel, counts, all_counts), out_sh...  6.5 us
    pallas_call x1, Pallas kernels, attend_own(): pl.pallas_call(own_kernel, out_shape=[pltpu.HBM(SUMS.shape, SUMS.dtype)]...  3.8 us
    ppermute x6, waiting for transfers between devices, exchange(): return lax.ppermute(v, 'ctx', [(i, i ^ mask) for i in range(NX * NZ)])  3.12 us
  transfers between devices with their start and end apart: 12, of which 5 were waited for; matrix products, arithmetic and copies ran while one was open for 2% of the time, Pallas kernels for 15%

profile of v10, /device:TPU:20, one launch (start us, length us, event | category | flops | bytes accessed | tf_op | source)
XLA Modules:
  0.0 70.4 jit_solution(17552268688100550228)
XLA Ops:
  0.0 0.7 fusion.2
  0.7 0.9 %fusion.1.own_ref.refs_2_.refs_3_ = bf16[528,128]{1,0:T(8,128)(2,1)S(1)} fusion(bf16[2,128]{1,0:T(2,128)(2,1)S(1)} %fusion.2, bf16[256,128]{1,0:T(8,128)(2,1)} %param.6, bf16[256,128]{1,0:T(8,128)(2,1)} %param.5), kind=kLoop, calls=%fused_computation.5 | loop fusion | flops 540672 | bytes 266752 | tf_op jit(solution)/shard_map/concatenate | solution.py:354
  1.6 9.1 %collective-permute-start = (bf16[528,128]{1,0:T(8,128)(2,1)S(1)}, bf16[528,128]{1,0:T(8,128)(2,1)S(1)}, u32[]{:S(2)}, u32[]{:S(2)}) collective-permute-start(bf16[528,128]{1,0:T(8,128)(2,1)S(1)} %fusion.1.own_ref.refs_2_.refs_3_), channel_id=1, source_target_pairs={{0,64},{16,80},{32,96},{48,112},{64,0},{80,16},{96,32},{112,48},{1... | collective-permute-start | bytes 405512 | tf_op jit(solution)/shard_map/ppermute | solution.py:337
  10.7 5.2 %collective-permute-start.1 = (bf16[528,128]{1,0:T(8,128)(2,1)S(1)}, bf16[528,128]{1,0:T(8,128)(2,1)S(1)}, u32[]{:S(2)}, u32[]{:S(2)}) collective-permute-start(bf16[528,128]{1,0:T(8,128)(2,1)S(1)} %fusion.1.own_ref.refs_2_.refs_3_), channel_id=1, source_target_pairs={{0,32},{16,48},{32,0},{48,16},{64,96},{80,112},{96,64},{112,80},{1... | collective-permute-start | bytes 405512 | tf_op jit(solution)/shard_map/ppermute | solution.py:337
  15.9 3.1 %collective-permute-start.2 = (bf16[528,128]{1,0:T(8,128)(2,1)S(1)}, bf16[528,128]{1,0:T(8,128)(2,1)S(1)}, u32[]{:S(2)}, u32[]{:S(2)}) collective-permute-start(bf16[528,128]{1,0:T(8,128)(2,1)S(1)} %fusion.1.own_ref.refs_2_.refs_3_), channel_id=1, source_target_pairs={{0,128},{16,144},{32,160},{48,176},{64,192},{80,208},{96,224},{112... | collective-permute-start | bytes 405512 | tf_op jit(solution)/shard_map/ppermute | solution.py:341
  19.0 1.3 %collective-permute-start.3 = (bf16[528,128]{1,0:T(8,128)(2,1)S(1)}, bf16[528,128]{1,0:T(8,128)(2,1)S(1)}, u32[]{:S(2)}, u32[]{:S(2)}) collective-permute-start(bf16[528,128]{1,0:T(8,128)(2,1)S(1)} %fusion.1.own_ref.refs_2_.refs_3_), channel_id=1, source_target_pairs={{0,256},{16,272},{32,288},{48,304},{64,320},{80,336},{96,352},{112... | collective-permute-start | bytes 405512 | tf_op jit(solution)/shard_map/ppermute | solution.py:341
  20.3 3.8 %attend_own.1 = (f32[2048,128]{1,0:T(8,128)}, f32[2048,128]{1,0:T(8,128)}, f32[2048,128]{1,0:T(8,128)}) custom-call(bf16[256,1024]{1,0:T(8,128)(2,1)} %refs_2_.1, bf16[528,128]{1,0:T(8,128)(2,1)S(1)} %fusion.1.own_ref.refs_2_.refs_3_), custom_call_target="tpu_custom_call" | custom-call | flops 1 | bytes 1 | tf_op jit(solution)/shard_map/attend_own/pallas_call | solution.py:294
  24.1 3.2 %collective-permute-done.3.refs_9_.refs_12_ = bf16[528,128]{1,0:T(8,128)(2,1)S(1)} collective-permute-done((bf16[528,128]{1,0:T(8,128)(2,1)S(1)}, bf16[528,128]{1,0:T(8,128)(2,1)S(1)}, u32[]{:S(2)}, u32[]{:S(2)}) %collective-permute-start.3) | collective-permute-done | bytes 135200 | tf_op jit(solution)/shard_map/ppermute | solution.py:341
  27.4 1.9 %collective-permute-start.4 = (bf16[528,128]{1,0:T(8,128)(2,1)S(1)}, bf16[528,128]{1,0:T(8,128)(2,1)S(1)}, u32[]{:S(2)}, u32[]{:S(2)}) collective-permute-start(bf16[528,128]{1,0:T(8,128)(2,1)S(1)} %collective-permute-done.refs_6_.refs_10_), channel_id=1, source_target_pairs={{0,32},{16,48},{32,0},{48,16},{64,96},{80,112},{96,64},{112,80},{1... | collective-permute-start | bytes 405512 | tf_op jit(solution)/shard_map/ppermute | solution.py:337
  29.3 1.9 %collective-permute-start.6 = (bf16[1056,128]{1,0:T(8,128)(2,1)S(1)}, bf16[1056,128]{1,0:T(8,128)(2,1)S(1)}, u32[]{:S(2)}, u32[]{:S(2)}) collective-permute-start(bf16[1056,128]{1,0:T(8,128)(2,1)S(1)} %constant_dynamic-update-slice_fusion), channel_id=1, source_target_pairs={{0,128},{16,144},{32,160},{48,176},{64,192},{80,208},{96,224},{112... | collective-permute-start | bytes 811016 | tf_op jit(solution)/shard_map/ppermute | solution.py:341
  31.3 1.3 %collective-permute-start.7 = (bf16[1056,128]{1,0:T(8,128)(2,1)S(1)}, bf16[1056,128]{1,0:T(8,128)(2,1)S(1)}, u32[]{:S(2)}, u32[]{:S(2)}) collective-permute-start(bf16[1056,128]{1,0:T(8,128)(2,1)S(1)} %constant_dynamic-update-slice_fusion), channel_id=1, source_target_pairs={{0,256},{16,272},{32,288},{48,304},{64,320},{80,336},{96,352},{112... | collective-permute-start | bytes 811016 | tf_op jit(solution)/shard_map/ppermute | solution.py:341
  32.6 3.8 %collective-permute-start.5 = (bf16[1056,128]{1,0:T(8,128)(2,1)S(1)}, bf16[1056,128]{1,0:T(8,128)(2,1)S(1)}, u32[]{:S(2)}, u32[]{:S(2)}) collective-permute-start(bf16[1056,128]{1,0:T(8,128)(2,1)S(1)} %pad_maximum_fusion.1), channel_id=1, source_target_pairs={{0,16},{16,0},{32,48},{48,32},{64,80},{80,64},{96,112},{112,96},{1... | collective-permute-start | bytes 811016 | tf_op jit(solution)/shard_map/ppermute | solution.py:337
  36.5 1.9 %collective-permute-start.8 = (bf16[528,128]{1,0:T(8,128)(2,1)S(1)}, bf16[528,128]{1,0:T(8,128)(2,1)S(1)}, u32[]{:S(2)}, u32[]{:S(2)}) collective-permute-start(bf16[528,128]{1,0:T(8,128)(2,1)S(1)} %collective-permute-done.4.refs_13_.refs_16_), channel_id=1, source_target_pairs={{0,128},{16,144},{32,160},{48,176},{64,192},{80,208},{96,224},{112... | collective-permute-start | bytes 405512 | tf_op jit(solution)/shard_map/ppermute | solution.py:341
  38.4 1.3 %collective-permute-start.9 = (bf16[528,128]{1,0:T(8,128)(2,1)S(1)}, bf16[528,128]{1,0:T(8,128)(2,1)S(1)}, u32[]{:S(2)}, u32[]{:S(2)}) collective-permute-start(bf16[528,128]{1,0:T(8,128)(2,1)S(1)} %collective-permute-done.4.refs_13_.refs_16_), channel_id=1, source_target_pairs={{0,256},{16,272},{32,288},{48,304},{64,320},{80,336},{96,352},{112... | collective-permute-start | bytes 405512 | tf_op jit(solution)/shard_map/ppermute | solution.py:341
  39.7 4.1 %collective-permute-done.6.refs_11_.refs_14_ = bf16[1056,128]{1,0:T(8,128)(2,1)S(1)} collective-permute-done((bf16[1056,128]{1,0:T(8,128)(2,1)S(1)}, bf16[1056,128]{1,0:T(8,128)(2,1)S(1)}, u32[]{:S(2)}, u32[]{:S(2)}) %collective-permute-start.6) | collective-permute-done | bytes 270368 | tf_op jit(solution)/shard_map/ppermute | solution.py:341
  43.8 0.7 %collective-permute-done.7.refs_12_.refs_15_ = bf16[1056,128]{1,0:T(8,128)(2,1)S(1)} collective-permute-done((bf16[1056,128]{1,0:T(8,128)(2,1)S(1)}, bf16[1056,128]{1,0:T(8,128)(2,1)S(1)}, u32[]{:S(2)}, u32[]{:S(2)}) %collective-permute-start.7) | collective-permute-done | bytes 270368 | tf_op jit(solution)/shard_map/ppermute | solution.py:341
  44.6 3.8 %collective-permute-start.10 = (bf16[2112,128]{1,0:T(8,128)(2,1)S(1)}, bf16[2112,128]{1,0:T(8,128)(2,1)S(1)}, u32[]{:S(2)}, u32[]{:S(2)}) collective-permute-start(bf16[2112,128]{1,0:T(8,128)(2,1)S(1)} %pad_maximum_fusion), channel_id=1, source_target_pairs={{0,16},{16,0},{32,48},{48,32},{64,80},{80,64},{96,112},{112,96},{1... | collective-permute-start | bytes 1622024 | tf_op jit(solution)/shard_map/ppermute | solution.py:337
  48.4 0.9 %collective-permute-done.8.refs_14_.refs_18_ = bf16[528,128]{1,0:T(8,128)(2,1)S(1)} collective-permute-done((bf16[528,128]{1,0:T(8,128)(2,1)S(1)}, bf16[528,128]{1,0:T(8,128)(2,1)S(1)}, u32[]{:S(2)}, u32[]{:S(2)}) %collective-permute-start.8) | collective-permute-done | bytes 135200 | tf_op jit(solution)/shard_map/ppermute | solution.py:341
  49.3 0.7 %pad_maximum_fusion.2 = bf16[1056,128]{1,0:T(8,128)(2,1)} fusion(bf16[528,128]{1,0:T(8,128)(2,1)S(1)} %broadcast_select_fusion, bf16[528,128]{1,0:T(8,128)(2,1)S(1)} %collective-permute-done.8.refs_14_.refs_18_), kind=kLoop, calls=%fused_computation.3 | loop fusion | flops 540672 | bytes 540672 | tf_op jit(solution)/shard_map/concatenate | solution.py:384
  50.0 3.8 %collective-permute-start.11 = (bf16[1056,128]{1,0:T(8,128)(2,1)}, bf16[1056,128]{1,0:T(8,128)(2,1)S(1)}, u32[]{:S(2)}, u32[]{:S(2)}) collective-permute-start(bf16[1056,128]{1,0:T(8,128)(2,1)} %pad_maximum_fusion.2), channel_id=1, source_target_pairs={{0,16},{16,0},{32,48},{48,32},{64,80},{80,64},{96,112},{112,96},{1... | collective-permute-start | bytes 811016 | tf_op jit(solution)/shard_map/ppermute | solution.py:337
  53.9 0.1 stack.18.refs_1_
  54.1 6.7 %attend_more.1 = (f32[2048,128]{1,0:T(8,128)S(1)}, f32[2048,128]{1,0:T(8,128)S(1)}) custom-call(s32[13]{0:T(128)S(1)} %stack.19.refs_0_, bf16[256,1024]{1,0:T(8,128)(2,1)} %refs_2_.1, bf16[528,128]{1,0:T(8,128)(2,1)S(1)} %fusion.1.own_ref.refs_2_.refs_3_, f32[2048,128]{1,0:T(8,128)} %get-tuple-element.32.refs_3_.refs_4_, ...), custom_call_target="tpu_custom_call" | custom-call | flops 1 | bytes 1 | tf_op jit(solution)/shard_map/attend_more/pallas_call | solution.py:306
  60.8 3.1 %collective-permute-done.11.refs_8_.refs_20_ = bf16[1056,128]{1,0:T(8,128)(2,1)S(1)} collective-permute-done((bf16[1056,128]{1,0:T(8,128)(2,1)}, bf16[1056,128]{1,0:T(8,128)(2,1)S(1)}, u32[]{:S(2)}, u32[]{:S(2)}) %collective-permute-start.11) | collective-permute-done | bytes 270368 | tf_op jit(solution)/shard_map/ppermute | solution.py:337
  63.9 6.5 %attend_last.1 = bf16[256,1024]{1,0:T(8,128)(2,1)} custom-call(s32[6]{0:T(128)S(1)} %broadcast_3_refs_0_.2.refs_0_, s32[19]{0:T(128)S(1)} %stack.18.refs_1_, bf16[256,1024]{1,0:T(8,128)(2,1)S(1)} %copy-done, bf16[528,128]{1,0:T(8,128)(2,1)S(1)} %fusion.1.own_ref.refs_2_.refs_3_, f32[2048,128]{1,0:T(8,128)S(1)} %copy-done.1, ...), custom_call_target="tpu_custom_call" | custom-call | flops 1 | bytes 1 | tf_op jit(solution)/shard_map/attend_last/pallas_call | solution.py:320
  (22 shorter events, 0.3 us)
Async XLA Ops:
  1.6 22.5 %collective-permute-start = (bf16[528,128]{1,0:T(8,128)(2,1)S(1)}, bf16[528,128]{1,0:T(8,128)(2,1)S(1)}, u32[]{:S(2)}, u32[]{:S(2)}) collective-permute-start(bf16[528,128]{1,0:T(8,128)(2,1)S(1)} %fusion.1.own_ref.refs_2_.refs_3_), channel_id=1, source_target_pairs={{0,64},{16,80},{32,96},{48,112},{64,0},{80,16},{96,32},{112,48},{1... | collective-permute-start | bytes 405512 | tf_op jit(solution)/shard_map/ppermute | solution.py:337
  10.7 13.4 %collective-permute-start.1 = (bf16[528,128]{1,0:T(8,128)(2,1)S(1)}, bf16[528,128]{1,0:T(8,128)(2,1)S(1)}, u32[]{:S(2)}, u32[]{:S(2)}) collective-permute-start(bf16[528,128]{1,0:T(8,128)(2,1)S(1)} %fusion.1.own_ref.refs_2_.refs_3_), channel_id=1, source_target_pairs={{0,32},{16,48},{32,0},{48,16},{64,96},{80,112},{96,64},{112,80},{1... | collective-permute-start | bytes 405512 | tf_op jit(solution)/shard_map/ppermute | solution.py:337
  15.9 8.3 %collective-permute-start.2 = (bf16[528,128]{1,0:T(8,128)(2,1)S(1)}, bf16[528,128]{1,0:T(8,128)(2,1)S(1)}, u32[]{:S(2)}, u32[]{:S(2)}) collective-permute-start(bf16[528,128]{1,0:T(8,128)(2,1)S(1)} %fusion.1.own_ref.refs_2_.refs_3_), channel_id=1, source_target_pairs={{0,128},{16,144},{32,160},{48,176},{64,192},{80,208},{96,224},{112... | collective-permute-start | bytes 405512 | tf_op jit(solution)/shard_map/ppermute | solution.py:341
  19.0 8.4 %collective-permute-start.3 = (bf16[528,128]{1,0:T(8,128)(2,1)S(1)}, bf16[528,128]{1,0:T(8,128)(2,1)S(1)}, u32[]{:S(2)}, u32[]{:S(2)}) collective-permute-start(bf16[528,128]{1,0:T(8,128)(2,1)S(1)} %fusion.1.own_ref.refs_2_.refs_3_), channel_id=1, source_target_pairs={{0,256},{16,272},{32,288},{48,304},{64,320},{80,336},{96,352},{112... | collective-permute-start | bytes 405512 | tf_op jit(solution)/shard_map/ppermute | solution.py:341
  27.4 9.1 %collective-permute-start.4 = (bf16[528,128]{1,0:T(8,128)(2,1)S(1)}, bf16[528,128]{1,0:T(8,128)(2,1)S(1)}, u32[]{:S(2)}, u32[]{:S(2)}) collective-permute-start(bf16[528,128]{1,0:T(8,128)(2,1)S(1)} %collective-permute-done.refs_6_.refs_10_), channel_id=1, source_target_pairs={{0,32},{16,48},{32,0},{48,16},{64,96},{80,112},{96,64},{112,80},{1... | collective-permute-start | bytes 405512 | tf_op jit(solution)/shard_map/ppermute | solution.py:337
  29.3 14.4 %collective-permute-start.6 = (bf16[1056,128]{1,0:T(8,128)(2,1)S(1)}, bf16[1056,128]{1,0:T(8,128)(2,1)S(1)}, u32[]{:S(2)}, u32[]{:S(2)}) collective-permute-start(bf16[1056,128]{1,0:T(8,128)(2,1)S(1)} %constant_dynamic-update-slice_fusion), channel_id=1, source_target_pairs={{0,128},{16,144},{32,160},{48,176},{64,192},{80,208},{96,224},{112... | collective-permute-start | bytes 811016 | tf_op jit(solution)/shard_map/ppermute | solution.py:341
  31.3 13.2 %collective-permute-start.7 = (bf16[1056,128]{1,0:T(8,128)(2,1)S(1)}, bf16[1056,128]{1,0:T(8,128)(2,1)S(1)}, u32[]{:S(2)}, u32[]{:S(2)}) collective-permute-start(bf16[1056,128]{1,0:T(8,128)(2,1)S(1)} %constant_dynamic-update-slice_fusion), channel_id=1, source_target_pairs={{0,256},{16,272},{32,288},{48,304},{64,320},{80,336},{96,352},{112... | collective-permute-start | bytes 811016 | tf_op jit(solution)/shard_map/ppermute | solution.py:341
  32.6 21.4 %collective-permute-start.5 = (bf16[1056,128]{1,0:T(8,128)(2,1)S(1)}, bf16[1056,128]{1,0:T(8,128)(2,1)S(1)}, u32[]{:S(2)}, u32[]{:S(2)}) collective-permute-start(bf16[1056,128]{1,0:T(8,128)(2,1)S(1)} %pad_maximum_fusion.1), channel_id=1, source_target_pairs={{0,16},{16,0},{32,48},{48,32},{64,80},{80,64},{96,112},{112,96},{1... | collective-permute-start | bytes 811016 | tf_op jit(solution)/shard_map/ppermute | solution.py:337
  36.5 12.8 %collective-permute-start.8 = (bf16[528,128]{1,0:T(8,128)(2,1)S(1)}, bf16[528,128]{1,0:T(8,128)(2,1)S(1)}, u32[]{:S(2)}, u32[]{:S(2)}) collective-permute-start(bf16[528,128]{1,0:T(8,128)(2,1)S(1)} %collective-permute-done.4.refs_13_.refs_16_), channel_id=1, source_target_pairs={{0,128},{16,144},{32,160},{48,176},{64,192},{80,208},{96,224},{112... | collective-permute-start | bytes 405512 | tf_op jit(solution)/shard_map/ppermute | solution.py:341
  38.4 10.9 %collective-permute-start.9 = (bf16[528,128]{1,0:T(8,128)(2,1)S(1)}, bf16[528,128]{1,0:T(8,128)(2,1)S(1)}, u32[]{:S(2)}, u32[]{:S(2)}) collective-permute-start(bf16[528,128]{1,0:T(8,128)(2,1)S(1)} %collective-permute-done.4.refs_13_.refs_16_), channel_id=1, source_target_pairs={{0,256},{16,272},{32,288},{48,304},{64,320},{80,336},{96,352},{112... | collective-permute-start | bytes 405512 | tf_op jit(solution)/shard_map/ppermute | solution.py:341
  44.6 19.3 %collective-permute-start.10 = (bf16[2112,128]{1,0:T(8,128)(2,1)S(1)}, bf16[2112,128]{1,0:T(8,128)(2,1)S(1)}, u32[]{:S(2)}, u32[]{:S(2)}) collective-permute-start(bf16[2112,128]{1,0:T(8,128)(2,1)S(1)} %pad_maximum_fusion), channel_id=1, source_target_pairs={{0,16},{16,0},{32,48},{48,32},{64,80},{80,64},{96,112},{112,96},{1... | collective-permute-start | bytes 1622024 | tf_op jit(solution)/shard_map/ppermute | solution.py:337
  50.0 13.8 %collective-permute-start.11 = (bf16[1056,128]{1,0:T(8,128)(2,1)}, bf16[1056,128]{1,0:T(8,128)(2,1)S(1)}, u32[]{:S(2)}, u32[]{:S(2)}) collective-permute-start(bf16[1056,128]{1,0:T(8,128)(2,1)} %pad_maximum_fusion.2), channel_id=1, source_target_pairs={{0,16},{16,0},{32,48},{48,32},{64,80},{80,64},{96,112},{112,96},{1... | collective-permute-start | bytes 811016 | tf_op jit(solution)/shard_map/ppermute | solution.py:337
  54.0 9.8 %copy-start = (bf16[256,1024]{1,0:T(8,128)(2,1)S(1)}, bf16[256,1024]{1,0:T(8,128)(2,1)}, u32[]{:S(2)}) copy-start(bf16[256,1024]{1,0:T(8,128)(2,1)} %refs_2_.1) | copy-start | bytes 1572868
  54.0 9.8 %copy-start.1 = (f32[2048,128]{1,0:T(8,128)S(1)}, f32[2048,128]{1,0:T(8,128)}, u32[]{:S(2)}) copy-start(f32[2048,128]{1,0:T(8,128)} %get-tuple-element.32.refs_3_.refs_4_) | copy-start | bytes 3145732

commit v11 on v10

--- a/solution.py
+++ b/solution.py
@@ -45,7 +45,7 @@
     return visible, in_first
 
 
-def add_own(q_ref, own_ref, shift_ref, l_ref, acc_ref):
+def add_own(q_ref, own_ref, shift_ref, l_ref, acc_ref, send):
     visible, in_first = own_masks(own_ref)
     keys = own_ref[:BLOCK, :]
     values = own_ref[BLOCK : 2 * BLOCK, :]
@@ -62,6 +62,7 @@
         shift_ref[rows, :] = jnp.where(
             in_first, jnp.broadcast_to(top, (BLOCK, HEAD)), -NEGATIVE
         )
+        send(h)
 
 
 def seen_rows(first_id, ids):
@@ -156,13 +157,21 @@
 
 
 def own_kernel(q_hbm, own_ref, shift_out, l_out, acc_out, q, shift, l_sum, acc_sum, sems):
-    fetch, *keep = copies(
-        [(q_hbm, q), (shift, shift_out), (l_sum, l_out), (acc_sum, acc_out)], sems
-    )
-    fetch.start()
-    fetch.wait()
-    add_own(q, own_ref, shift, l_sum, acc_sum)
-    run(keep)
+    fetch = copies([(q_hbm, q)], sems)
+    run(fetch)
+    pairs = [(shift, shift_out), (l_sum, l_out), (acc_sum, acc_out)]
+    keep = []
+
+    def send(h):
+        rows = pl.ds(h * BLOCK, BLOCK)
+        for i, (a, b) in enumerate(pairs):
+            sem = sems.at[1 + 3 * h + i]
+            keep.append(pltpu.make_async_copy(a.at[rows, :], b.at[rows, :], sem))
+            keep[-1].start()
+
+    add_own(q, own_ref, shift, l_sum, acc_sum, send)
+    for move in keep:
+        move.wait()
 
 
 def more_kernel(counts, *refs):
@@ -296,7 +305,7 @@
         out_shape=[pltpu.HBM(SUMS.shape, SUMS.dtype)] * 3,
         in_specs=[HBM, VMEM],
         out_specs=[HBM] * 3,
-        scratch_shapes=[QUERIES] + [SUM] * 3 + [SEMS],
+        scratch_shapes=[QUERIES] + [SUM] * 3 + [pltpu.SemaphoreType.DMA((1 + 3 * HEADS,))],
         compiler_params=params(VMEM_MIB), cost_estimate=COST, name="attend_own",
     )(*in_hbm(q), own)
 

time: 70.9 us -> 70.8 us (level)
  Pallas kernels: 17 us -> 18.3 us
    pallas_call x1, Pallas kernels: 6.7 us -> 8.28 us  [attend_more(): pl.pallas_call(functools.partial(more_kernel, counts), out_shape=[SUMS] *...]
    ppermute x6, waiting for transfers between devices: 3.12 us -> 1.54 us  [exchange(): return lax.ppermute(v, 'ctx', [(i, i ^ mask) for i in range(NX * NZ)])]
    ppermute x6, waiting for transfers between devices: 8.94 us -> 10 us  [along_x(): lax.ppermute(v, 'ctx', [(i, i + NZ * steps) for i in range((NX - steps) *...]
    ppermute x6, starting transfers between devices: 27.6 us -> 26.9 us  [exchange(): return lax.ppermute(v, 'ctx', [(i, i ^ mask) for i in range(NX * NZ)])]
  transfers between devices with their start and end apart: 12 -> 12, of which waited for: 5 -> 4; matrix products, arithmetic and copies ran while one was open for 2% -> 2% of each run, Pallas kernels for 15% -> 17%
where the time goes in v11:
time: 70.8 us; the launch traced here: 70.4 us
  starting transfers between devices  37.7 us (53%)
  Pallas kernels  18.3 us (26%)
  waiting for transfers between devices  11.6 us (16%)
  other arithmetic  2.43 us (3%)
    ppermute x6, starting transfers between devices, exchange(): return lax.ppermute(v, 'ctx', [(i, i ^ mask) for i in range(NX * NZ)])  26.9 us
    ppermute x6, starting transfers between devices, along_x(): lax.ppermute(v, 'ctx', [(i, i + NZ * steps) for i in range((NX - steps) *...  10.8 us
    ppermute x6, waiting for transfers between devices, along_x(): lax.ppermute(v, 'ctx', [(i, i + NZ * steps) for i in range((NX - steps) *...  10 us
    pallas_call x1, Pallas kernels, attend_more(): pl.pallas_call(functools.partial(more_kernel, counts), out_shape=[SUMS] *...  8.28 us
    pallas_call x1, Pallas kernels, attend_last(): pl.pallas_call(functools.partial(last_kernel, counts, all_counts), out_sh...  6.51 us
    pallas_call x1, Pallas kernels, attend_own(): pl.pallas_call(own_kernel, out_shape=[pltpu.HBM(SUMS.shape, SUMS.dtype)]...  3.48 us
    ppermute x6, waiting for transfers between devices, exchange(): return lax.ppermute(v, 'ctx', [(i, i ^ mask) for i in range(NX * NZ)])  1.54 us
  transfers between devices with their start and end apart: 12, of which 4 were waited for; matrix products, arithmetic and copies ran while one was open for 2% of the time, Pallas kernels for 17%

profile of v11, /device:TPU:20, one launch (start us, length us, event | category | flops | bytes accessed | tf_op | source)
XLA Modules:
  0.0 70.4 jit_solution(18034309723289069011)
XLA Ops:
  0.0 0.7 fusion.2
  0.7 0.9 %fusion.1.own_ref.refs_2_.refs_3_ = bf16[528,128]{1,0:T(8,128)(2,1)S(1)} fusion(bf16[2,128]{1,0:T(2,128)(2,1)S(1)} %fusion.2, bf16[256,128]{1,0:T(8,128)(2,1)} %param.6, bf16[256,128]{1,0:T(8,128)(2,1)} %param.5), kind=kLoop, calls=%fused_computation.5 | loop fusion | flops 540672 | bytes 266752 | tf_op jit(solution)/shard_map/concatenate | solution.py:363
  1.6 9.1 %collective-permute-start = (bf16[528,128]{1,0:T(8,128)(2,1)S(1)}, bf16[528,128]{1,0:T(8,128)(2,1)S(1)}, u32[]{:S(2)}, u32[]{:S(2)}) collective-permute-start(bf16[528,128]{1,0:T(8,128)(2,1)S(1)} %fusion.1.own_ref.refs_2_.refs_3_), channel_id=1, source_target_pairs={{0,64},{16,80},{32,96},{48,112},{64,0},{80,16},{96,32},{112,48},{1... | collective-permute-start | bytes 405512 | tf_op jit(solution)/shard_map/ppermute | solution.py:346
  10.7 5.2 %collective-permute-start.1 = (bf16[528,128]{1,0:T(8,128)(2,1)S(1)}, bf16[528,128]{1,0:T(8,128)(2,1)S(1)}, u32[]{:S(2)}, u32[]{:S(2)}) collective-permute-start(bf16[528,128]{1,0:T(8,128)(2,1)S(1)} %fusion.1.own_ref.refs_2_.refs_3_), channel_id=1, source_target_pairs={{0,32},{16,48},{32,0},{48,16},{64,96},{80,112},{96,64},{112,80},{1... | collective-permute-start | bytes 405512 | tf_op jit(solution)/shard_map/ppermute | solution.py:346
  15.9 3.1 %collective-permute-start.2 = (bf16[528,128]{1,0:T(8,128)(2,1)S(1)}, bf16[528,128]{1,0:T(8,128)(2,1)S(1)}, u32[]{:S(2)}, u32[]{:S(2)}) collective-permute-start(bf16[528,128]{1,0:T(8,128)(2,1)S(1)} %fusion.1.own_ref.refs_2_.refs_3_), channel_id=1, source_target_pairs={{0,128},{16,144},{32,160},{48,176},{64,192},{80,208},{96,224},{112... | collective-permute-start | bytes 405512 | tf_op jit(solution)/shard_map/ppermute | solution.py:350
  19.0 1.3 %collective-permute-start.3 = (bf16[528,128]{1,0:T(8,128)(2,1)S(1)}, bf16[528,128]{1,0:T(8,128)(2,1)S(1)}, u32[]{:S(2)}, u32[]{:S(2)}) collective-permute-start(bf16[528,128]{1,0:T(8,128)(2,1)S(1)} %fusion.1.own_ref.refs_2_.refs_3_), channel_id=1, source_target_pairs={{0,256},{16,272},{32,288},{48,304},{64,320},{80,336},{96,352},{112... | collective-permute-start | bytes 405512 | tf_op jit(solution)/shard_map/ppermute | solution.py:350
  20.3 3.5 %attend_own.1 = (f32[2048,128]{1,0:T(8,128)}, f32[2048,128]{1,0:T(8,128)}, f32[2048,128]{1,0:T(8,128)}) custom-call(bf16[256,1024]{1,0:T(8,128)(2,1)} %refs_2_.1, bf16[528,128]{1,0:T(8,128)(2,1)S(1)} %fusion.1.own_ref.refs_2_.refs_3_), custom_call_target="tpu_custom_call" | custom-call | flops 1 | bytes 1 | tf_op jit(solution)/shard_map/attend_own/pallas_call | solution.py:303
  23.8 3.6 %collective-permute-done.3.refs_9_.refs_12_ = bf16[528,128]{1,0:T(8,128)(2,1)S(1)} collective-permute-done((bf16[528,128]{1,0:T(8,128)(2,1)S(1)}, bf16[528,128]{1,0:T(8,128)(2,1)S(1)}, u32[]{:S(2)}, u32[]{:S(2)}) %collective-permute-start.3) | collective-permute-done | bytes 135200 | tf_op jit(solution)/shard_map/ppermute | solution.py:350
  27.4 1.9 %collective-permute-start.4 = (bf16[528,128]{1,0:T(8,128)(2,1)S(1)}, bf16[528,128]{1,0:T(8,128)(2,1)S(1)}, u32[]{:S(2)}, u32[]{:S(2)}) collective-permute-start(bf16[528,128]{1,0:T(8,128)(2,1)S(1)} %collective-permute-done.refs_6_.refs_10_), channel_id=1, source_target_pairs={{0,32},{16,48},{32,0},{48,16},{64,96},{80,112},{96,64},{112,80},{1... | collective-permute-start | bytes 405512 | tf_op jit(solution)/shard_map/ppermute | solution.py:346
  29.3 1.9 %collective-permute-start.6 = (bf16[1056,128]{1,0:T(8,128)(2,1)S(1)}, bf16[1056,128]{1,0:T(8,128)(2,1)S(1)}, u32[]{:S(2)}, u32[]{:S(2)}) collective-permute-start(bf16[1056,128]{1,0:T(8,128)(2,1)S(1)} %constant_dynamic-update-slice_fusion), channel_id=1, source_target_pairs={{0,128},{16,144},{32,160},{48,176},{64,192},{80,208},{96,224},{112... | collective-permute-start | bytes 811016 | tf_op jit(solution)/shard_map/ppermute | solution.py:350
  31.3 1.3 %collective-permute-start.7 = (bf16[1056,128]{1,0:T(8,128)(2,1)S(1)}, bf16[1056,128]{1,0:T(8,128)(2,1)S(1)}, u32[]{:S(2)}, u32[]{:S(2)}) collective-permute-start(bf16[1056,128]{1,0:T(8,128)(2,1)S(1)} %constant_dynamic-update-slice_fusion), channel_id=1, source_target_pairs={{0,256},{16,272},{32,288},{48,304},{64,320},{80,336},{96,352},{112... | collective-permute-start | bytes 811016 | tf_op jit(solution)/shard_map/ppermute | solution.py:350
  32.6 3.8 %collective-permute-start.5 = (bf16[1056,128]{1,0:T(8,128)(2,1)S(1)}, bf16[1056,128]{1,0:T(8,128)(2,1)S(1)}, u32[]{:S(2)}, u32[]{:S(2)}) collective-permute-start(bf16[1056,128]{1,0:T(8,128)(2,1)S(1)} %pad_maximum_fusion.1), channel_id=1, source_target_pairs={{0,16},{16,0},{32,48},{48,32},{64,80},{80,64},{96,112},{112,96},{1... | collective-permute-start | bytes 811016 | tf_op jit(solution)/shard_map/ppermute | solution.py:346
  36.5 1.9 %collective-permute-start.8 = (bf16[528,128]{1,0:T(8,128)(2,1)S(1)}, bf16[528,128]{1,0:T(8,128)(2,1)S(1)}, u32[]{:S(2)}, u32[]{:S(2)}) collective-permute-start(bf16[528,128]{1,0:T(8,128)(2,1)S(1)} %collective-permute-done.4.refs_13_.refs_16_), channel_id=1, source_target_pairs={{0,128},{16,144},{32,160},{48,176},{64,192},{80,208},{96,224},{112... | collective-permute-start | bytes 405512 | tf_op jit(solution)/shard_map/ppermute | solution.py:350
  38.4 1.3 %collective-permute-start.9 = (bf16[528,128]{1,0:T(8,128)(2,1)S(1)}, bf16[528,128]{1,0:T(8,128)(2,1)S(1)}, u32[]{:S(2)}, u32[]{:S(2)}) collective-permute-start(bf16[528,128]{1,0:T(8,128)(2,1)S(1)} %collective-permute-done.4.refs_13_.refs_16_), channel_id=1, source_target_pairs={{0,256},{16,272},{32,288},{48,304},{64,320},{80,336},{96,352},{112... | collective-permute-start | bytes 405512 | tf_op jit(solution)/shard_map/ppermute | solution.py:350
  39.7 5.6 %collective-permute-done.6.refs_11_.refs_14_ = bf16[1056,128]{1,0:T(8,128)(2,1)S(1)} collective-permute-done((bf16[1056,128]{1,0:T(8,128)(2,1)S(1)}, bf16[1056,128]{1,0:T(8,128)(2,1)S(1)}, u32[]{:S(2)}, u32[]{:S(2)}) %collective-permute-start.6) | collective-permute-done | bytes 270368 | tf_op jit(solution)/shard_map/ppermute | solution.py:350
  45.4 3.0 %collective-permute-start.10 = (bf16[2112,128]{1,0:T(8,128)(2,1)S(1)}, bf16[2112,128]{1,0:T(8,128)(2,1)S(1)}, u32[]{:S(2)}, u32[]{:S(2)}) collective-permute-start(bf16[2112,128]{1,0:T(8,128)(2,1)S(1)} %pad_maximum_fusion), channel_id=1, source_target_pairs={{0,16},{16,0},{32,48},{48,32},{64,80},{80,64},{96,112},{112,96},{1... | collective-permute-start | bytes 1622024 | tf_op jit(solution)/shard_map/ppermute | solution.py:346
  48.4 0.9 %collective-permute-done.8.refs_14_.refs_18_ = bf16[528,128]{1,0:T(8,128)(2,1)S(1)} collective-permute-done((bf16[528,128]{1,0:T(8,128)(2,1)S(1)}, bf16[528,128]{1,0:T(8,128)(2,1)S(1)}, u32[]{:S(2)}, u32[]{:S(2)}) %collective-permute-start.8) | collective-permute-done | bytes 135200 | tf_op jit(solution)/shard_map/ppermute | solution.py:350
  49.3 0.7 %pad_maximum_fusion.2 = bf16[1056,128]{1,0:T(8,128)(2,1)} fusion(bf16[528,128]{1,0:T(8,128)(2,1)S(1)} %broadcast_select_fusion, bf16[528,128]{1,0:T(8,128)(2,1)S(1)} %collective-permute-done.8.refs_14_.refs_18_), kind=kLoop, calls=%fused_computation.3 | loop fusion | flops 540672 | bytes 540672 | tf_op jit(solution)/shard_map/concatenate | solution.py:393
  50.0 3.8 %collective-permute-start.11 = (bf16[1056,128]{1,0:T(8,128)(2,1)}, bf16[1056,128]{1,0:T(8,128)(2,1)S(1)}, u32[]{:S(2)}, u32[]{:S(2)}) collective-permute-start(bf16[1056,128]{1,0:T(8,128)(2,1)} %pad_maximum_fusion.2), channel_id=1, source_target_pairs={{0,16},{16,0},{32,48},{48,32},{64,80},{80,64},{96,112},{112,96},{1... | collective-permute-start | bytes 811016 | tf_op jit(solution)/shard_map/ppermute | solution.py:346
  53.9 0.1 stack.18.refs_1_
  54.0 0.1 stack.19.refs_0_
  54.1 8.3 %attend_more.1 = (f32[2048,128]{1,0:T(8,128)S(1)}, f32[2048,128]{1,0:T(8,128)S(1)}) custom-call(s32[13]{0:T(128)S(1)} %stack.19.refs_0_, bf16[256,1024]{1,0:T(8,128)(2,1)} %refs_2_.1, bf16[528,128]{1,0:T(8,128)(2,1)S(1)} %fusion.1.own_ref.refs_2_.refs_3_, f32[2048,128]{1,0:T(8,128)} %get-tuple-element.32.refs_3_.refs_4_, ...), custom_call_target="tpu_custom_call" | custom-call | flops 1 | bytes 1 | tf_op jit(solution)/shard_map/attend_more/pallas_call | solution.py:315
  62.3 1.5 %collective-permute-done.11.refs_8_.refs_20_ = bf16[1056,128]{1,0:T(8,128)(2,1)S(1)} collective-permute-done((bf16[1056,128]{1,0:T(8,128)(2,1)}, bf16[1056,128]{1,0:T(8,128)(2,1)S(1)}, u32[]{:S(2)}, u32[]{:S(2)}) %collective-permute-start.11) | collective-permute-done | bytes 270368 | tf_op jit(solution)/shard_map/ppermute | solution.py:346
  63.9 6.5 %attend_last.1 = bf16[256,1024]{1,0:T(8,128)(2,1)} custom-call(s32[6]{0:T(128)S(1)} %broadcast_3_refs_0_.2.refs_0_, s32[19]{0:T(128)S(1)} %stack.18.refs_1_, bf16[256,1024]{1,0:T(8,128)(2,1)S(1)} %copy-done, bf16[528,128]{1,0:T(8,128)(2,1)S(1)} %fusion.1.own_ref.refs_2_.refs_3_, f32[2048,128]{1,0:T(8,128)S(1)} %copy-done.1, ...), custom_call_target="tpu_custom_call" | custom-call | flops 1 | bytes 1 | tf_op jit(solution)/shard_map/attend_last/pallas_call | solution.py:329
  (22 shorter events, 0.2 us)
Async XLA Ops:
  1.6 22.2 %collective-permute-start = (bf16[528,128]{1,0:T(8,128)(2,1)S(1)}, bf16[528,128]{1,0:T(8,128)(2,1)S(1)}, u32[]{:S(2)}, u32[]{:S(2)}) collective-permute-start(bf16[528,128]{1,0:T(8,128)(2,1)S(1)} %fusion.1.own_ref.refs_2_.refs_3_), channel_id=1, source_target_pairs={{0,64},{16,80},{32,96},{48,112},{64,0},{80,16},{96,32},{112,48},{1... | collective-permute-start | bytes 405512 | tf_op jit(solution)/shard_map/ppermute | solution.py:346
  10.7 13.1 %collective-permute-start.1 = (bf16[528,128]{1,0:T(8,128)(2,1)S(1)}, bf16[528,128]{1,0:T(8,128)(2,1)S(1)}, u32[]{:S(2)}, u32[]{:S(2)}) collective-permute-start(bf16[528,128]{1,0:T(8,128)(2,1)S(1)} %fusion.1.own_ref.refs_2_.refs_3_), channel_id=1, source_target_pairs={{0,32},{16,48},{32,0},{48,16},{64,96},{80,112},{96,64},{112,80},{1... | collective-permute-start | bytes 405512 | tf_op jit(solution)/shard_map/ppermute | solution.py:346
  15.9 7.9 %collective-permute-start.2 = (bf16[528,128]{1,0:T(8,128)(2,1)S(1)}, bf16[528,128]{1,0:T(8,128)(2,1)S(1)}, u32[]{:S(2)}, u32[]{:S(2)}) collective-permute-start(bf16[528,128]{1,0:T(8,128)(2,1)S(1)} %fusion.1.own_ref.refs_2_.refs_3_), channel_id=1, source_target_pairs={{0,128},{16,144},{32,160},{48,176},{64,192},{80,208},{96,224},{112... | collective-permute-start | bytes 405512 | tf_op jit(solution)/shard_map/ppermute | solution.py:350
  19.0 8.4 %collective-permute-start.3 = (bf16[528,128]{1,0:T(8,128)(2,1)S(1)}, bf16[528,128]{1,0:T(8,128)(2,1)S(1)}, u32[]{:S(2)}, u32[]{:S(2)}) collective-permute-start(bf16[528,128]{1,0:T(8,128)(2,1)S(1)} %fusion.1.own_ref.refs_2_.refs_3_), channel_id=1, source_target_pairs={{0,256},{16,272},{32,288},{48,304},{64,320},{80,336},{96,352},{112... | collective-permute-start | bytes 405512 | tf_op jit(solution)/shard_map/ppermute | solution.py:350
  27.4 9.1 %collective-permute-start.4 = (bf16[528,128]{1,0:T(8,128)(2,1)S(1)}, bf16[528,128]{1,0:T(8,128)(2,1)S(1)}, u32[]{:S(2)}, u32[]{:S(2)}) collective-permute-start(bf16[528,128]{1,0:T(8,128)(2,1)S(1)} %collective-permute-done.refs_6_.refs_10_), channel_id=1, source_target_pairs={{0,32},{16,48},{32,0},{48,16},{64,96},{80,112},{96,64},{112,80},{1... | collective-permute-start | bytes 405512 | tf_op jit(solution)/shard_map/ppermute | solution.py:346
  29.3 15.9 %collective-permute-start.6 = (bf16[1056,128]{1,0:T(8,128)(2,1)S(1)}, bf16[1056,128]{1,0:T(8,128)(2,1)S(1)}, u32[]{:S(2)}, u32[]{:S(2)}) collective-permute-start(bf16[1056,128]{1,0:T(8,128)(2,1)S(1)} %constant_dynamic-update-slice_fusion), channel_id=1, source_target_pairs={{0,128},{16,144},{32,160},{48,176},{64,192},{80,208},{96,224},{112... | collective-permute-start | bytes 811016 | tf_op jit(solution)/shard_map/ppermute | solution.py:350
  31.3 14.0 %collective-permute-start.7 = (bf16[1056,128]{1,0:T(8,128)(2,1)S(1)}, bf16[1056,128]{1,0:T(8,128)(2,1)S(1)}, u32[]{:S(2)}, u32[]{:S(2)}) collective-permute-start(bf16[1056,128]{1,0:T(8,128)(2,1)S(1)} %constant_dynamic-update-slice_fusion), channel_id=1, source_target_pairs={{0,256},{16,272},{32,288},{48,304},{64,320},{80,336},{96,352},{112... | collective-permute-start | bytes 811016 | tf_op jit(solution)/shard_map/ppermute | solution.py:350
  32.6 21.4 %collective-permute-start.5 = (bf16[1056,128]{1,0:T(8,128)(2,1)S(1)}, bf16[1056,128]{1,0:T(8,128)(2,1)S(1)}, u32[]{:S(2)}, u32[]{:S(2)}) collective-permute-start(bf16[1056,128]{1,0:T(8,128)(2,1)S(1)} %pad_maximum_fusion.1), channel_id=1, source_target_pairs={{0,16},{16,0},{32,48},{48,32},{64,80},{80,64},{96,112},{112,96},{1... | collective-permute-start | bytes 811016 | tf_op jit(solution)/shard_map/ppermute | solution.py:346
  36.5 12.8 %collective-permute-start.8 = (bf16[528,128]{1,0:T(8,128)(2,1)S(1)}, bf16[528,128]{1,0:T(8,128)(2,1)S(1)}, u32[]{:S(2)}, u32[]{:S(2)}) collective-permute-start(bf16[528,128]{1,0:T(8,128)(2,1)S(1)} %collective-permute-done.4.refs_13_.refs_16_), channel_id=1, source_target_pairs={{0,128},{16,144},{32,160},{48,176},{64,192},{80,208},{96,224},{112... | collective-permute-start | bytes 405512 | tf_op jit(solution)/shard_map/ppermute | solution.py:350
  38.4 10.9 %collective-permute-start.9 = (bf16[528,128]{1,0:T(8,128)(2,1)S(1)}, bf16[528,128]{1,0:T(8,128)(2,1)S(1)}, u32[]{:S(2)}, u32[]{:S(2)}) collective-permute-start(bf16[528,128]{1,0:T(8,128)(2,1)S(1)} %collective-permute-done.4.refs_13_.refs_16_), channel_id=1, source_target_pairs={{0,256},{16,272},{32,288},{48,304},{64,320},{80,336},{96,352},{112... | collective-permute-start | bytes 405512 | tf_op jit(solution)/shard_map/ppermute | solution.py:350
  45.4 18.5 %collective-permute-start.10 = (bf16[2112,128]{1,0:T(8,128)(2,1)S(1)}, bf16[2112,128]{1,0:T(8,128)(2,1)S(1)}, u32[]{:S(2)}, u32[]{:S(2)}) collective-permute-start(bf16[2112,128]{1,0:T(8,128)(2,1)S(1)} %pad_maximum_fusion), channel_id=1, source_target_pairs={{0,16},{16,0},{32,48},{48,32},{64,80},{80,64},{96,112},{112,96},{1... | collective-permute-start | bytes 1622024 | tf_op jit(solution)/shard_map/ppermute | solution.py:346
  50.0 13.8 %collective-permute-start.11 = (bf16[1056,128]{1,0:T(8,128)(2,1)}, bf16[1056,128]{1,0:T(8,128)(2,1)S(1)}, u32[]{:S(2)}, u32[]{:S(2)}) collective-permute-start(bf16[1056,128]{1,0:T(8,128)(2,1)} %pad_maximum_fusion.2), channel_id=1, source_target_pairs={{0,16},{16,0},{32,48},{48,32},{64,80},{80,64},{96,112},{112,96},{1... | collective-permute-start | bytes 811016 | tf_op jit(solution)/shard_map/ppermute | solution.py:346
  54.0 9.8 %copy-start = (bf16[256,1024]{1,0:T(8,128)(2,1)S(1)}, bf16[256,1024]{1,0:T(8,128)(2,1)}, u32[]{:S(2)}) copy-start(bf16[256,1024]{1,0:T(8,128)(2,1)} %refs_2_.1) | copy-start | bytes 1572868
  54.0 9.8 %copy-start.1 = (f32[2048,128]{1,0:T(8,128)S(1)}, f32[2048,128]{1,0:T(8,128)}, u32[]{:S(2)}) copy-start(f32[2048,128]{1,0:T(8,128)} %get-tuple-element.32.refs_3_.refs_4_) | copy-start | bytes 3145732
